TPU v7x, 256 devices: a whole 4x4x8 slice. The times are simulated.
256 devices in a mesh: blk: 16 (over x, z_hi), uly: 16 (over z_lo, y, core).
Axes of the slice: x: 4, y: 4, z: 8 (z_hi: 4, z_lo: 2; z = z_hi * 2 + z_lo), core: 2. Of those that a mesh axis runs over, the one named last changes fastest.
Arguments:
- query_rows: bfloat16 [16384, 2048], P(('blk', 'uly')), may hold values from -30 to 30
- key_rows: bfloat16 [16384, 128], P(('blk', 'uly')), may hold values from -20 to 20
- value_rows: bfloat16 [16384, 128], P(('blk', 'uly')), may hold values from -6 to 6
- saved_out: bfloat16 [16384, 2048], P(('blk', 'uly')), may hold values from -6 to 6
- out_grad: bfloat16 [16384, 2048], P(('blk', 'uly')), may hold values from -6 to 6
- doc_lengths: int32 [64], replicated, may hold values from 1 to 512, 16384 in all
Outputs:
- query_grad: bfloat16 [16384, 2048], P(('blk', 'uly'))
- key_grad: bfloat16 [16384, 128], P(('blk', 'uly'))
- value_grad: bfloat16 [16384, 128], P(('blk', 'uly'))
Inputs may be any that keep to these rules, and one draw needn't show every extreme that they name: `doc_lengths`: lengths of the documents in order of position; they sum to 16384 and the longest is exactly 512.
All inputs are finite; a program needn't handle non-finite values.
Results may differ from a plain program's by a relative error of at most 0.011.
Values may be sent and summed in bfloat16 or wider, within the bound.
No kernel may reach another device: no remote copies, remote signals or barrier semaphores. Data moves between devices by JAX's collectives and lax.ppermute only.
A program may use at most 64 MiB of HBM per device.

v0:
```python
import math

import jax
import jax.numpy as jnp
from jax import lax
from jax.sharding import PartitionSpec as P

DH = 128
HQ = 16
KVH = 1
REACH = 1


MASKED_SCORE = -1e30
score_rows = 512


def passed_along(x, axis, by):
    length = lax.axis_size(axis)
    pairs = [(i, i + by) for i in range(length) if 0 <= i + by < length]
    return lax.ppermute(x, axis, pairs)


def row_places(owner_index, block_rows, blocks):
    half_rows = block_rows // 2
    offsets = jnp.arange(block_rows, dtype=jnp.int32)
    return jnp.where(
        offsets < half_rows,
        owner_index * half_rows + offsets,
        (2 * blocks - 1 - owner_index) * half_rows + offsets - half_rows,
    )


def doc_of_rows(places, doc_ends):
    return jnp.sum((places[:, None] >= doc_ends[None, :]).astype(jnp.int32), axis=1)


def row_spans(row_start, total_rows):
    stride = min(score_rows, total_rows - row_start)
    return [
        (row_lo, min(row_lo + stride, total_rows))
        for row_lo in range(row_start, total_rows, stride)
    ]


def pair_visible(query_where, key_where, row_lo, row_hi, key_count):
    query_places, query_docs = query_where
    key_places, key_docs = key_where
    same_doc = query_docs[row_lo:row_hi, None] == key_docs[None, :key_count]
    return same_doc & (query_places[row_lo:row_hi, None] >= key_places[None, :key_count])


def score_tile(query_block, key_block, row_lo, row_hi, key_count, scaling):
    return (
        jnp.einsum(
            "qhd,kd->hqk",
            query_block[row_lo:row_hi],
            key_block[:key_count],
            preferred_element_type=jnp.float32,
        )
        * scaling
    )


def visit_case(build_case, key_lower, half_rows, block_rows, tile_state):
    if key_lower:
        return build_case(0, half_rows)(tile_state)
    return build_case(half_rows, block_rows)(tile_state)


def stats_case(query_block, key_block, query_where, key_where, row_start, key_count, scaling):

    def stats_tile_case(tile_state):
        row_max, row_sum = tile_state
        for row_lo, row_hi in row_spans(row_start, query_block.shape[0]):
            scores = score_tile(query_block, key_block, row_lo, row_hi, key_count, scaling)
            visible = pair_visible(query_where, key_where, row_lo, row_hi, key_count)[None]
            old_max = row_max[:, row_lo:row_hi]
            new_max = jnp.maximum(
                old_max, jnp.max(jnp.where(visible, scores, MASKED_SCORE), axis=-1)
            )
            weights = jnp.where(visible, jnp.exp(scores - new_max[..., None]), 0.0)
            summed = row_sum[:, row_lo:row_hi] * jnp.exp(old_max - new_max) + jnp.sum(
                weights, axis=-1
            )
            row_max = row_max.at[:, row_lo:row_hi].set(new_max)
            row_sum = row_sum.at[:, row_lo:row_hi].set(summed)
        return (row_max, row_sum)

    return stats_tile_case


def grad_case(query_side, key_side, row_start, key_count, scaling):
    query_block, grad_block, log_norm, row_dot, query_where = query_side
    key_block, value_block, key_where = key_side

    def grad_tile_case(accums):
        query_acc, key_acc, value_acc = accums
        for row_lo, row_hi in row_spans(row_start, query_block.shape[0]):
            scores = score_tile(query_block, key_block, row_lo, row_hi, key_count, scaling)
            visible = pair_visible(query_where, key_where, row_lo, row_hi, key_count)[None]
            weights = jnp.where(visible, jnp.exp(scores - log_norm[:, row_lo:row_hi, None]), 0.0)
            grad_scores = jnp.einsum(
                "qhd,kd->hqk",
                grad_block[row_lo:row_hi],
                value_block[:key_count],
                preferred_element_type=jnp.float32,
            )
            score_grads = (weights * (grad_scores - row_dot[:, row_lo:row_hi, None])).astype(
                jnp.bfloat16
            )
            weights = weights.astype(jnp.bfloat16)
            value_acc = value_acc.at[:key_count].add(
                jnp.einsum(
                    "hqk,qhd->kd",
                    weights,
                    grad_block[row_lo:row_hi],
                    preferred_element_type=jnp.float32,
                )
            )
            key_acc = key_acc.at[:key_count].add(
                jnp.einsum(
                    "hqk,qhd->kd",
                    score_grads,
                    query_block[row_lo:row_hi],
                    preferred_element_type=jnp.float32,
                )
                * scaling
            )
            query_acc = query_acc.at[row_lo:row_hi].add(
                jnp.einsum(
                    "hqk,kd->qhd",
                    score_grads,
                    key_block[:key_count],
                    preferred_element_type=jnp.float32,
                )
                * scaling
            )
        return (query_acc, key_acc, value_acc)

    return grad_tile_case


def on_device(query_rows, key_rows, value_rows, saved_out, out_grad, doc_lengths):
    blocks = lax.axis_size("blk")
    groups = lax.axis_size("uly")
    my_block = lax.axis_index("blk")
    tok_rows = query_rows.shape[0]
    local_heads = HQ // groups
    block_rows = tok_rows * groups
    half_rows = block_rows // 2
    scaling = 1.0 / math.sqrt(DH)
    kv_copies = groups // KVH
    query_three = query_rows.reshape(tok_rows, HQ, DH)
    saved_three = saved_out.reshape(tok_rows, HQ, DH)
    grad_three = out_grad.reshape(tok_rows, HQ, DH)
    key_three = jnp.repeat(key_rows.reshape(tok_rows, KVH, DH), kv_copies, axis=1)
    value_three = jnp.repeat(value_rows.reshape(tok_rows, KVH, DH), kv_copies, axis=1)
    query_block, saved_block, grad_block, key_block, value_block = (
        lax.all_to_all(query_three, "uly", split_axis=1, concat_axis=0, tiled=True),
        lax.all_to_all(saved_three, "uly", split_axis=1, concat_axis=0, tiled=True),
        lax.all_to_all(grad_three, "uly", split_axis=1, concat_axis=0, tiled=True),
        lax.all_to_all(key_three, "uly", split_axis=1, concat_axis=0, tiled=True),
        lax.all_to_all(value_three, "uly", split_axis=1, concat_axis=0, tiled=True),
    )
    key_block = key_block.reshape(block_rows, DH)
    value_block = value_block.reshape(block_rows, DH)
    row_dot = jnp.sum(grad_block.astype(jnp.float32) * saved_block.astype(jnp.float32), axis=-1).T
    doc_ends = jnp.cumsum(doc_lengths)

    def where_of(owner_index):
        places = row_places(owner_index, block_rows, blocks)
        inside = (owner_index >= 0) & (owner_index < blocks)
        return (places, jnp.where(inside, doc_of_rows(places, doc_ends), -1))

    home_where = where_of(my_block)
    visits = [(facing, stride) for facing in (1, -1) for stride in range(1, REACH + 1)]
    start_max = jnp.full((local_heads, block_rows), MASKED_SCORE, jnp.float32)
    start_sum = jnp.zeros((local_heads, block_rows), jnp.float32)
    stats_start = stats_case(
        query_block, key_block, home_where, home_where, 0, block_rows, scaling
    )((start_max, start_sum))
    zero_keys = jnp.zeros((block_rows, DH), jnp.float32)
    zero_queries = jnp.zeros((block_rows, local_heads, DH), jnp.float32)
    stored = []
    stats_now = stats_start
    for stats_facing, stats_stride in visits:
        visitor = passed_along(key_block, "blk", stats_facing * stats_stride)
        visitor_keys = visitor
        stats_remote = where_of(my_block - stats_facing * stats_stride)

        def stats_build_case(row_start, key_count):
            return stats_case(
                query_block, visitor_keys, home_where, stats_remote, row_start, key_count, scaling
            )

        stats_now = visit_case(stats_build_case, stats_facing > 0, half_rows, block_rows, stats_now)
    for facing, stride in visits:
        stored.append(passed_along((key_block, value_block), "blk", facing * stride))
    log_norm = stats_now[0] + jnp.log(stats_now[1])
    query_side = (query_block, grad_block, log_norm, row_dot, home_where)
    query_acc, key_acc, value_acc = grad_case(
        query_side, (key_block, value_block, home_where), 0, block_rows, scaling
    )((zero_queries, zero_keys, zero_keys))
    for number, (facing, stride) in enumerate(visits):
        keys_vis, values_vis = stored[number]
        remote = where_of(my_block - facing * stride)

        def build_case(row_start, key_count):
            return grad_case(
                query_side, (keys_vis, values_vis, remote), row_start, key_count, scaling
            )

        query_acc, part_key, part_value = visit_case(
            build_case, facing > 0, half_rows, block_rows, (query_acc, zero_keys, zero_keys)
        )
        back_key, back_value = passed_along((part_key, part_value), "blk", -facing * stride)
        key_acc = key_acc + back_key
        value_acc = value_acc + back_value
    query_home = lax.all_to_all(
        query_acc.astype(jnp.bfloat16), "uly", split_axis=0, concat_axis=1, tiled=True
    )
    key_home, value_home = (
        lax.all_to_all(
            key_acc.reshape(block_rows, 1, DH), "uly", split_axis=0, concat_axis=1, tiled=True
        ),
        lax.all_to_all(
            value_acc.reshape(block_rows, 1, DH), "uly", split_axis=0, concat_axis=1, tiled=True
        ),
    )
    query_grad = query_home.reshape(tok_rows, HQ * DH)
    key_grad = jnp.sum(key_home.reshape(tok_rows, KVH, kv_copies, DH), axis=2).reshape(
        tok_rows, KVH * DH
    )
    value_grad = jnp.sum(value_home.reshape(tok_rows, KVH, kv_copies, DH), axis=2).reshape(
        tok_rows, KVH * DH
    )
    return (query_grad, key_grad.astype(jnp.bfloat16), value_grad.astype(jnp.bfloat16))


def solution(mesh):
    placed = (
        P(("blk", "uly"), None),
        P(("blk", "uly"), None),
        P(("blk", "uly"), None),
        P(("blk", "uly"), None),
        P(("blk", "uly"), None),
        P(),
    )
    return jax.shard_map(
        on_device,
        mesh=mesh,
        in_specs=placed,
        out_specs=(P(("blk", "uly"), None), P(("blk", "uly"), None), P(("blk", "uly"), None)),
        check_vma=False,
    )
```

profile of v0, /device:TPU:39, one launch (start us, length us, event | category | flops | bytes accessed | tf_op | source)
XLA Modules:
  0.0 201.3 jit_solution(14948434106449134186)
XLA Ops:
  1.7 12.6 %all_to_all.108 = bf16[64,16,128]{2,0,1:T(8,128)(2,1)S(1)} all-to-all(bf16[64,16,128]{2,0,1:T(8,128)(2,1)S(1)} %copy_bitcast_fusion.3), channel_id=1, replica_groups=mesh['blk'=16,'uly'=16] {'uly'}, dimensions={1} | all-to-all | bytes 524288 | tf_op jit(solution)/shard_map/all_to_all | solution.py:160
  15.8 4.9 %all-to-all-start = ((bf16[64,16,128]{2,0,1:T(8,128)(2,1)}), bf16[64,16,128]{2,0,1:T(8,128)(2,1)S(1)}, u32[]{:S(2)}, u32[]{:S(2)}) async-start(bf16[64,16,128]{2,0,1:T(8,128)(2,1)} %reshape.1476), calls=%async_computation | async-start | bytes 524288 | tf_op jit(solution)/shard_map/all_to_all | solution.py:163
  21.7 5.6 %all-to-all-done = bf16[64,16,128]{2,0,1:T(8,128)(2,1)S(1)} async-done(((bf16[64,16,128]{2,0,1:T(8,128)(2,1)}), bf16[64,16,128]{2,0,1:T(8,128)(2,1)S(1)}, u32[]{:S(2)}, u32[]{:S(2)}) %all-to-all-start) | async-done | bytes 262176 | tf_op jit(solution)/shard_map/all_to_all | solution.py:163
  28.7 5.6 %all-to-all-start.2 = ((bf16[64,16,128]{2,0,1:T(8,128)(2,1)}), bf16[64,16,128]{2,0,1:T(8,128)(2,1)}, u32[]{:S(2)}, u32[]{:S(2)}) async-start(bf16[64,16,128]{2,0,1:T(8,128)(2,1)} %reshape.1481), calls=%async_computation.2 | async-start | bytes 524288 | tf_op jit(solution)/shard_map/all_to_all | solution.py:164
  35.3 5.7 %all-to-all-done.2 = bf16[64,16,128]{2,0,1:T(8,128)(2,1)} async-done(((bf16[64,16,128]{2,0,1:T(8,128)(2,1)}), bf16[64,16,128]{2,0,1:T(8,128)(2,1)}, u32[]{:S(2)}, u32[]{:S(2)}) %all-to-all-start.2) | async-done | bytes 262176 | tf_op jit(solution)/shard_map/all_to_all | solution.py:164
  41.0 5.0 %all-to-all-start.4 = ((bf16[64,16,128]{2,0,1:T(8,128)(2,1)}), bf16[64,16,128]{2,0,1:T(8,128)(2,1)S(1)}, u32[]{:S(2)}, u32[]{:S(2)}) async-start(bf16[64,16,128]{2,0,1:T(8,128)(2,1)} %copy_bitcast_fusion.1), calls=%async_computation.4 | async-start | bytes 524288 | tf_op jit(solution)/shard_map/all_to_all | solution.py:161
  46.8 5.7 %all-to-all-done.4 = bf16[64,16,128]{2,0,1:T(8,128)(2,1)S(1)} async-done(((bf16[64,16,128]{2,0,1:T(8,128)(2,1)}), bf16[64,16,128]{2,0,1:T(8,128)(2,1)S(1)}, u32[]{:S(2)}, u32[]{:S(2)}) %all-to-all-start.4) | async-done | bytes 262176 | tf_op jit(solution)/shard_map/all_to_all | solution.py:161
  52.5 5.0 %all-to-all-start.3 = ((bf16[64,16,128]{2,0,1:T(8,128)(2,1)}), bf16[64,16,128]{2,0,1:T(8,128)(2,1)S(1)}, u32[]{:S(2)}, u32[]{:S(2)}) async-start(bf16[64,16,128]{2,0,1:T(8,128)(2,1)} %copy_bitcast_fusion.2), calls=%async_computation.3 | async-start | bytes 524288 | tf_op jit(solution)/shard_map/all_to_all | solution.py:162
  58.2 7.3 %collective-permute-start.3 = (bf16[1024,128]{1,0:T(8,128)(2,1)}, bf16[1024,128]{1,0:T(8,128)(2,1)}, u32[]{:S(2)}, u32[]{:S(2)}) collective-permute-start(bf16[1024,128]{1,0:T(8,128)(2,1)} %bitcast.41), channel_id=1, source_target_pairs={{16,0},{32,16},{48,32},{64,48},{80,64},{96,80},{112,96},{128,112},... | collective-permute-start | bytes 786440 | tf_op jit(solution)/shard_map/ppermute | solution.py:21
  67.4 6.4 %collective-permute-start.1 = (bf16[1024,128]{1,0:T(8,128)(2,1)S(1)}, bf16[1024,128]{1,0:T(8,128)(2,1)S(1)}, u32[]{:S(2)}, u32[]{:S(2)}) collective-permute-start(bf16[1024,128]{1,0:T(8,128)(2,1)S(1)} %bitcast.352), channel_id=1, source_target_pairs={{16,0},{32,16},{48,32},{64,48},{80,64},{96,80},{112,96},{128,112},... | collective-permute-start | bytes 786440 | tf_op jit(solution)/shard_map/ppermute | solution.py:21
  76.6 10.5 %collective-permute-done.1 = bf16[1024,128]{1,0:T(8,128)(2,1)S(1)} collective-permute-done((bf16[1024,128]{1,0:T(8,128)(2,1)S(1)}, bf16[1024,128]{1,0:T(8,128)(2,1)S(1)}, u32[]{:S(2)}, u32[]{:S(2)}) %collective-permute-start.1) | collective-permute-done | bytes 262176 | tf_op jit(solution)/shard_map/ppermute | solution.py:21
  92.9 2.4 %fusion.18 = (f32[512]{0:T(512)S(1)}, f32[512]{0:T(512)S(1)}, f32[512]{0:T(512)S(1)}) fusion(f32[1024,512]{1,0:T(8,128)S(1)} %get-tuple-element.385, f32[512]{0:T(512)S(1)} %get-tuple-element.384, s32[1024]{0:T(1024)S(1)} %add_select_fusion.2, s32[512]{0:T(512)S(1)} %get-tuple-element.383, s32[1024]{0:T(1024)S(1)} %broadcast_select_fusion.4, ...), kind=kLoop, calls=%fused_computation.33 | loop fusion | flops 11008512 | bytes 6328320 | tf_op jit(solution)/shard_map/reduce_sum | solution.py:83
  107.7 4.4 %collective-permute-start.7 = (f32[1024,128]{1,0:T(8,128)}, f32[1024,128]{1,0:T(8,128)}, u32[]{:S(2)}, u32[]{:S(2)}) collective-permute-start(f32[1024,128]{1,0:T(8,128)} %fusion.57), channel_id=1, source_target_pairs={{0,16},{16,32},{32,48},{48,64},{64,80},{80,96},{96,112},{112,128},... | collective-permute-start | bytes 1572872 | tf_op jit(solution)/shard_map/ppermute | solution.py:21
  112.2 4.0 %collective-permute-start.6 = (f32[1024,128]{1,0:T(8,128)}, f32[1024,128]{1,0:T(8,128)}, u32[]{:S(2)}, u32[]{:S(2)}) collective-permute-start(f32[1024,128]{1,0:T(8,128)} %fusion.44), channel_id=1, source_target_pairs={{16,0},{32,16},{48,32},{64,48},{80,64},{96,80},{112,96},{128,112},... | collective-permute-start | bytes 1572872 | tf_op jit(solution)/shard_map/ppermute | solution.py:21
  125.1 2.4 %reduce.83 = bf16[1024,128]{1,0:T(8,128)(2,1)} reduce(bf16[1024,1,128]{2,0,1:T(8,128)(2,1)} %convert_element_type.80, bf16[]{:T(256)} %broadcast.1137), dimensions={1}, to_apply=%copy.53.reduce_sub_computation | reduce | bytes 524290 | tf_op jit(solution)/shard_map/convert_element_type | solution.py:221
  129.2 10.3 %all-to-all-start.5 = ((bf16[16,2,4096]{2,1,0:T(2,128)(2,1)}), bf16[16,2,4096]{2,1,0:T(2,128)(2,1)}, u32[]{:S(2)}, u32[]{:S(2)}) async-start(bf16[16,2,4096]{2,1,0:T(2,128)(2,1)} %reshape.1506), calls=%async_computation.5 | async-start | bytes 524288 | tf_op jit(solution)/shard_map/all_to_all | solution.py:220
  139.6 2.3 %fusion.62 = f32[1024,128]{1,0:T(8,128)S(1)} fusion(bf16[512,128]{1,0:T(8,128)(2,1)} %bitcast.379, f32[1024,512]{1,0:T(8,128)} %copy-done.9, f32[512]{0:T(512)} %bitcast.409, s32[512]{0:T(512)S(1)} %copy-done.20, s32[512]{0:T(512)} %copy-done.24, s32[1024]{0:T(1024)S(1)} %add_select_fusion.2, s32[1024]{0:T(1024)S(1)} %broadcast_select_fusion.4), kind=kOutput, calls=%fused_computation.93 | convolution fusion | flops 137887744 | bytes 2766848 | tf_op jit(solution)/shard_map/hqk,qhd->kd/dot_general | solution.py:114
  143.2 2.8 %fusion.40 = f32[1024,128]{1,0:T(8,128)} fusion(f32[1024,128]{1,0:T(8,128)} %collective-permute-done.7, f32[1024,128]{1,0:T(8,128)} %collective-permute-done.6, f32[1024,128]{1,0:T(8,128)S(1)} %fusion.62, bf16[512,128]{1,0:T(8,128)(2,1)S(1)} %bitcast.375, f32[1024,512]{1,0:T(8,128)S(1)} %fusion.111, f32[512]{0:T(512)S(1)} %bitcast.405, ...), kind=kOutput, calls=%fused_computation.65 | convolution fusion | flops 138280960 | bytes 4339712 | tf_op jit(solution)/shard_map/hqk,qhd->kd/dot_general | solution.py:114
  146.2 5.6 %all-to-all-start.7 = ((f32[1024,1,128]{2,1,0:T(1,128)}), f32[1024,1,128]{2,1,0:T(1,128)S(1)}, u32[]{:S(2)}, u32[]{:S(2)}) async-start(f32[1024,1,128]{2,1,0:T(1,128)} %bitcast.368), calls=%async_computation.7 | async-start | bytes 1048576 | tf_op jit(solution)/shard_map/all_to_all | solution.py:227
  155.9 6.4 %collective-permute-start.4 = (f32[1024,128]{1,0:T(8,128)}, f32[1024,128]{1,0:T(8,128)S(1)}, u32[]{:S(2)}, u32[]{:S(2)}) collective-permute-start(f32[1024,128]{1,0:T(8,128)} %fusion.48), channel_id=1, source_target_pairs={{16,0},{32,16},{48,32},{64,48},{80,64},{96,80},{112,96},{128,112},... | collective-permute-start | bytes 1572872 | tf_op jit(solution)/shard_map/ppermute | solution.py:21
  163.6 19.7 %collective-permute-done.5 = f32[1024,128]{1,0:T(8,128)S(1)} collective-permute-done((f32[1024,128]{1,0:T(8,128)}, f32[1024,128]{1,0:T(8,128)S(1)}, u32[]{:S(2)}, u32[]{:S(2)}) %collective-permute-start.5) | collective-permute-done | bytes 524320 | tf_op jit(solution)/shard_map/ppermute | solution.py:21
  185.1 6.5 %all-to-all-start.6 = ((f32[1024,1,128]{2,1,0:T(1,128)}), f32[1024,1,128]{2,1,0:T(1,128)S(1)}, u32[]{:S(2)}, u32[]{:S(2)}) async-start(f32[1024,1,128]{2,1,0:T(1,128)} %bitcast.88), calls=%async_computation.6 | async-start | bytes 1048576 | tf_op jit(solution)/shard_map/all_to_all | solution.py:224
  191.5 2.2 %reshape.1507 = bf16[1024,1,128]{2,1,0:T(2,128)(2,1)S(1)} reshape(bf16[16,2,4096]{2,1,0:T(2,128)(2,1)} %all-to-all-done.5) | data formatting | bytes 524288
  195.3 5.4 %all-to-all-done.6 = f32[1024,1,128]{2,1,0:T(1,128)S(1)} async-done(((f32[1024,1,128]{2,1,0:T(1,128)}), f32[1024,1,128]{2,1,0:T(1,128)S(1)}, u32[]{:S(2)}, u32[]{:S(2)}) %all-to-all-start.6) | async-done | bytes 524320 | tf_op jit(solution)/shard_map/all_to_all | solution.py:224
  (154 shorter events, 51.2 us)
Async XLA Ops:
  1.6 44.4 %copy-start.15 = (bf16[64,2048]{1,0:T(8,128)(2,1)S(1)}, bf16[64,2048]{1,0:T(8,128)(2,1)}, u32[]{:S(2)}) copy-start(bf16[64,2048]{1,0:T(8,128)(2,1)} %param.72) | copy-start | bytes 786436
  15.8 11.5 %all-to-all-start = ((bf16[64,16,128]{2,0,1:T(8,128)(2,1)}), bf16[64,16,128]{2,0,1:T(8,128)(2,1)S(1)}, u32[]{:S(2)}, u32[]{:S(2)}) async-start(bf16[64,16,128]{2,0,1:T(8,128)(2,1)} %reshape.1476), calls=%async_computation | async-start | bytes 524288 | tf_op jit(solution)/shard_map/all_to_all | solution.py:163
  27.3 80.0 %copy-start.5 = (bf16[64,16,128]{2,0,1:T(8,128)(2,1)}, bf16[64,16,128]{2,0,1:T(8,128)(2,1)S(1)}, u32[]{:S(2)}) copy-start(bf16[64,16,128]{2,0,1:T(8,128)(2,1)S(1)} %all-to-all-done) | copy-start | bytes 786436
  28.7 12.3 %all-to-all-start.2 = ((bf16[64,16,128]{2,0,1:T(8,128)(2,1)}), bf16[64,16,128]{2,0,1:T(8,128)(2,1)}, u32[]{:S(2)}, u32[]{:S(2)}) async-start(bf16[64,16,128]{2,0,1:T(8,128)(2,1)} %reshape.1481), calls=%async_computation.2 | async-start | bytes 524288 | tf_op jit(solution)/shard_map/all_to_all | solution.py:164
  34.5 64.8 %copy-start.19 = (s32[512]{0:T(512)}, s32[512]{0:T(512)S(1)}, u32[]{:S(2)}) copy-start(s32[512]{0:T(512)S(1)} %get-tuple-element.383) | copy-start | bytes 6148
  41.0 11.6 %all-to-all-start.4 = ((bf16[64,16,128]{2,0,1:T(8,128)(2,1)}), bf16[64,16,128]{2,0,1:T(8,128)(2,1)S(1)}, u32[]{:S(2)}, u32[]{:S(2)}) async-start(bf16[64,16,128]{2,0,1:T(8,128)(2,1)} %copy_bitcast_fusion.1), calls=%async_computation.4 | async-start | bytes 524288 | tf_op jit(solution)/shard_map/all_to_all | solution.py:161
  46.0 53.3 %copy-start.24 = (s32[512]{0:T(512)}, s32[512]{0:T(512)S(1)}, u32[]{:S(2)}) copy-start(s32[512]{0:T(512)S(1)} %get-tuple-element.381) | copy-start | bytes 6148
  46.0 60.1 %copy-start.21 = (s32[512]{0:T(512)}, s32[512]{0:T(512)S(1)}, u32[]{:S(2)}) copy-start(s32[512]{0:T(512)S(1)} %get-tuple-element.380) | copy-start | bytes 6148
  52.5 23.2 %all-to-all-start.3 = ((bf16[64,16,128]{2,0,1:T(8,128)(2,1)}), bf16[64,16,128]{2,0,1:T(8,128)(2,1)S(1)}, u32[]{:S(2)}, u32[]{:S(2)}) async-start(bf16[64,16,128]{2,0,1:T(8,128)(2,1)} %copy_bitcast_fusion.2), calls=%async_computation.3 | async-start | bytes 524288 | tf_op jit(solution)/shard_map/all_to_all | solution.py:162
  57.6 48.5 %copy-start.27 = (s32[512]{0:T(512)}, s32[512]{0:T(512)S(1)}, u32[]{:S(2)}) copy-start(s32[512]{0:T(512)S(1)} %slice.574) | copy-start | bytes 6148
  57.6 48.5 %copy-start.29 = (s32[512]{0:T(512)}, s32[512]{0:T(512)S(1)}, u32[]{:S(2)}) copy-start(s32[512]{0:T(512)S(1)} %slice.573) | copy-start | bytes 6148
  58.2 46.1 %copy-start.25 = (s32[1024]{0:T(1024)}, s32[1024]{0:T(1024)S(1)}, u32[]{:S(2)}) copy-start(s32[1024]{0:T(1024)S(1)} %broadcast_select_fusion.2) | copy-start | bytes 12292
  58.2 61.9 %collective-permute-start.3 = (bf16[1024,128]{1,0:T(8,128)(2,1)}, bf16[1024,128]{1,0:T(8,128)(2,1)}, u32[]{:S(2)}, u32[]{:S(2)}) collective-permute-start(bf16[1024,128]{1,0:T(8,128)(2,1)} %bitcast.41), channel_id=1, source_target_pairs={{16,0},{32,16},{48,32},{64,48},{80,64},{96,80},{112,96},{128,112},... | collective-permute-start | bytes 786440 | tf_op jit(solution)/shard_map/ppermute | solution.py:21
  65.5 33.8 %collective-permute-start.2 = (bf16[1024,128]{1,0:T(8,128)(2,1)}, bf16[1024,128]{1,0:T(8,128)(2,1)}, u32[]{:S(2)}, u32[]{:S(2)}) collective-permute-start(bf16[1024,128]{1,0:T(8,128)(2,1)} %bitcast.41), channel_id=1, source_target_pairs={{0,16},{16,32},{32,48},{48,64},{64,80},{80,96},{96,112},{112,128},... | collective-permute-start | bytes 786440 | tf_op jit(solution)/shard_map/ppermute | solution.py:21
  67.4 19.7 %collective-permute-start.1 = (bf16[1024,128]{1,0:T(8,128)(2,1)S(1)}, bf16[1024,128]{1,0:T(8,128)(2,1)S(1)}, u32[]{:S(2)}, u32[]{:S(2)}) collective-permute-start(bf16[1024,128]{1,0:T(8,128)(2,1)S(1)} %bitcast.352), channel_id=1, source_target_pairs={{16,0},{32,16},{48,32},{64,48},{80,64},{96,80},{112,96},{128,112},... | collective-permute-start | bytes 786440 | tf_op jit(solution)/shard_map/ppermute | solution.py:21
  73.8 17.1 %collective-permute-start = (bf16[1024,128]{1,0:T(8,128)(2,1)S(1)}, bf16[1024,128]{1,0:T(8,128)(2,1)S(1)}, u32[]{:S(2)}, u32[]{:S(2)}) collective-permute-start(bf16[1024,128]{1,0:T(8,128)(2,1)S(1)} %bitcast.353), channel_id=1, source_target_pairs={{0,16},{16,32},{32,48},{48,64},{64,80},{80,96},{96,112},{112,128},... | collective-permute-start | bytes 786440 | tf_op jit(solution)/shard_map/ppermute | solution.py:21
  76.1 44.0 %copy-start.16 = (bf16[8,64,1,128]{3,1,0,2:T(8,128)(2,1)}, bf16[8,64,1,128]{3,1,0,2:T(8,128)(2,1)S(1)}, u32[]{:S(2)}) copy-start(bf16[8,64,1,128]{3,1,0,2:T(8,128)(2,1)S(1)} %get-tuple-element.373) | copy-start | bytes 393220
  107.7 35.4 %collective-permute-start.7 = (f32[1024,128]{1,0:T(8,128)}, f32[1024,128]{1,0:T(8,128)}, u32[]{:S(2)}, u32[]{:S(2)}) collective-permute-start(f32[1024,128]{1,0:T(8,128)} %fusion.57), channel_id=1, source_target_pairs={{0,16},{16,32},{32,48},{48,64},{64,80},{80,96},{96,112},{112,128},... | collective-permute-start | bytes 1572872 | tf_op jit(solution)/shard_map/ppermute | solution.py:21
  112.2 31.0 %collective-permute-start.6 = (f32[1024,128]{1,0:T(8,128)}, f32[1024,128]{1,0:T(8,128)}, u32[]{:S(2)}, u32[]{:S(2)}) collective-permute-start(f32[1024,128]{1,0:T(8,128)} %fusion.44), channel_id=1, source_target_pairs={{16,0},{32,16},{48,32},{64,48},{80,64},{96,80},{112,96},{128,112},... | collective-permute-start | bytes 1572872 | tf_op jit(solution)/shard_map/ppermute | solution.py:21
  129.2 17.0 %all-to-all-start.5 = ((bf16[16,2,4096]{2,1,0:T(2,128)(2,1)}), bf16[16,2,4096]{2,1,0:T(2,128)(2,1)}, u32[]{:S(2)}, u32[]{:S(2)}) async-start(bf16[16,2,4096]{2,1,0:T(2,128)(2,1)} %reshape.1506), calls=%async_computation.5 | async-start | bytes 524288 | tf_op jit(solution)/shard_map/all_to_all | solution.py:220
  146.2 38.8 %all-to-all-start.7 = ((f32[1024,1,128]{2,1,0:T(1,128)}), f32[1024,1,128]{2,1,0:T(1,128)S(1)}, u32[]{:S(2)}, u32[]{:S(2)}) async-start(f32[1024,1,128]{2,1,0:T(1,128)} %bitcast.368), calls=%async_computation.7 | async-start | bytes 1048576 | tf_op jit(solution)/shard_map/all_to_all | solution.py:227
  154.0 29.3 %collective-permute-start.5 = (f32[1024,128]{1,0:T(8,128)}, f32[1024,128]{1,0:T(8,128)S(1)}, u32[]{:S(2)}, u32[]{:S(2)}) collective-permute-start(f32[1024,128]{1,0:T(8,128)} %convolution_multiply_fusion.2), channel_id=1, source_target_pairs={{0,16},{16,32},{32,48},{48,64},{64,80},{80,96},{96,112},{112,128},... | collective-permute-start | bytes 1572872 | tf_op jit(solution)/shard_map/ppermute | solution.py:21
  155.9 27.9 %collective-permute-start.4 = (f32[1024,128]{1,0:T(8,128)}, f32[1024,128]{1,0:T(8,128)S(1)}, u32[]{:S(2)}, u32[]{:S(2)}) collective-permute-start(f32[1024,128]{1,0:T(8,128)} %fusion.48), channel_id=1, source_target_pairs={{16,0},{32,16},{48,32},{64,48},{80,64},{96,80},{112,96},{128,112},... | collective-permute-start | bytes 1572872 | tf_op jit(solution)/shard_map/ppermute | solution.py:21
  185.1 15.6 %all-to-all-start.6 = ((f32[1024,1,128]{2,1,0:T(1,128)}), f32[1024,1,128]{2,1,0:T(1,128)S(1)}, u32[]{:S(2)}, u32[]{:S(2)}) async-start(f32[1024,1,128]{2,1,0:T(1,128)} %bitcast.88), calls=%async_computation.6 | async-start | bytes 1048576 | tf_op jit(solution)/shard_map/all_to_all | solution.py:224
  (25 other events, 187.1 us)
where the time goes:
time: 205 us; the launch traced here: 201 us
  starting transfers between devices  77.1 us (38%)
  waiting for transfers between devices  55.2 us (27%)
  matrix products  28.9 us (14%)
  local copies, waits for them, and re-layouts  15 us (7%)
  blocking collectives  12.6 us (6%)
  other arithmetic  10.9 us (5%)
    ppermute x8, starting transfers between devices, passed_along(): return lax.ppermute(x, axis, pairs)  34.2 us
    ppermute x8, waiting for transfers between devices, passed_along(): return lax.ppermute(x, axis, pairs)  32.6 us
    all_to_all x1, blocking collectives, on_device(): lax.all_to_all(query_three, 'uly', split_axis=1, concat_axis=0, tiled=True)  12.6 us
    all_to_all x1, starting transfers between devices, on_device(): lax.all_to_all(query_acc.astype(jnp.bfloat16), 'uly', split_axis=0, conca...  10.3 us
    dot_general x5, matrix products, grad_tile_case(): jnp.einsum('hqk,qhd->kd', weights, grad_block[row_lo:row_hi], preferred_e...  8.36 us
    dot_general x5, matrix products, grad_tile_case(): jnp.einsum('qhd,kd->hqk', grad_block[row_lo:row_hi], value_block[:key_cou...  8.34 us
    dot_general x5, matrix products, grad_tile_case(): jnp.einsum('hqk,qhd->kd', score_grads, query_block[row_lo:row_hi], prefer...  6.92 us
    all_to_all x1, starting transfers between devices, on_device(): lax.all_to_all(key_acc.reshape(block_rows, 1, DH), 'uly', split_axis=0, c...  6.46 us
  transfers between devices with their start and end apart: 15, of which 9 were waited for; matrix products, arithmetic and copies ran while one was open for 25% of the time, Pallas kernels for 0%

commit v1 on v0

v1 whole, which is shorter than its diff:
```python
import math

import jax
import jax.numpy as jnp
from jax import lax
from jax.experimental import pallas as pl
from jax.experimental.pallas import tpu as pltpu
from jax.sharding import PartitionSpec as P

DH = 128
HQ = 16
ROWS = 64
CHUNKS = 256
CHIPS = CHUNKS // 2
HALF_CHUNKS = 8
HALVES = CHUNKS // HALF_CHUNKS
COLS = HQ * ROWS
CHIP_ROWS = 2 * ROWS
WINDOW = 5 * CHIP_ROWS
PAST = 4 * CHIP_ROWS
TILE = 256
NEG = -1e30
SCALING = 1.0 / math.sqrt(DH)
EXP2_SCALING = SCALING * math.log2(math.e)
AXES = ("blk", "uly")
STEPS = ((1, 4), (2, 3))


def device_of(chunk):
    half, place = divmod(chunk, HALF_CHUNKS)
    if half < HALVES // 2:
        return half * 16 + place
    return (HALVES - 1 - half) * 16 + 8 + place


def swap_cores(x):
    return lax.ppermute(x, "uly", [(i, i ^ 1) for i in range(16)])


def move_chips(x, steps, sign):
    pairs = []
    for chunk in range(CHUNKS):
        chip, core = divmod(chunk, 2)
        target = chip + sign * steps[core]
        if 0 <= target < CHIPS:
            pairs.append((device_of(chunk), device_of(2 * target + core)))
    return lax.ppermute(x, AXES, pairs)


def dot_nt(a, b):
    return lax.dot_general(a, b, (((1,), (1,)), ((), ())), preferred_element_type=jnp.float32)


def dot_nn(a, b):
    return lax.dot_general(a, b, (((1,), (0,)), ((), ())), preferred_element_type=jnp.float32)


def dot_tn(a, b):
    return lax.dot_general(a, b, (((0,), (0,)), ((), ())), preferred_element_type=jnp.float32)


def prepare_kernel(q_ref, o_ref, g_ref, len_ref, q2_ref, g2_ref, dot_ref, bias_ref):
    blk = lax.axis_index("blk")
    uly = lax.axis_index("uly")
    core = lax.rem(uly, 2)
    place = lax.rem(uly, HALF_CHUNKS)
    half = jnp.where(uly < HALF_CHUNKS, blk, HALVES - 1 - blk)
    chunk = half * HALF_CHUNKS + place
    chip = chunk // 2

    ones = jnp.ones((8, DH), jnp.bfloat16)
    for h in range(HQ):
        cols = slice(h * DH, (h + 1) * DH)
        rows = slice(h * ROWS, (h + 1) * ROWS)
        grad = g_ref[:, cols]
        q2_ref[rows, :] = q_ref[:, cols]
        g2_ref[rows, :] = grad
        prod = grad.astype(jnp.float32) * o_ref[:, cols].astype(jnp.float32)
        high = prod.astype(jnp.bfloat16)
        low = (prod - high.astype(jnp.float32)).astype(jnp.bfloat16)
        dot_ref[:, rows] = dot_nt(ones, high) + dot_nt(ones, low)

    lens = jnp.broadcast_to(len_ref[...].astype(jnp.float32), (64, 64))
    doc = lax.broadcasted_iota(jnp.int32, (64, 64), 0)
    other = lax.broadcasted_iota(jnp.int32, (64, 64), 1)
    starts = jnp.sum(jnp.where(other < doc, lens, 0.0), axis=1, keepdims=True).astype(jnp.int32)
    lane = lax.broadcasted_iota(jnp.int32, (1, DH), 1)
    here = chunk * ROWS + lax.rem(lane, ROWS)
    first = jnp.max(jnp.where(starts <= here, starts, 0), axis=0, keepdims=True)
    index = lax.broadcasted_iota(jnp.int32, (ROWS, DH), 0)
    for part in range(WINDOW // ROWS):
        group, side = divmod(part, 2)
        if group == 4:
            back, owner = 0, core
        elif group < 2:
            back, owner = jnp.where(core == 0, STEPS[group][0], STEPS[group][1]), core
        else:
            back, owner = jnp.where(core == 0, STEPS[group - 2][1], STEPS[group - 2][0]), 1 - core
        held = owner if side == 0 else 1 - owner
        where = (2 * (chip - back) + held) * ROWS + index
        seen = (where >= first) & (where <= here)
        bias_ref[part * ROWS : (part + 1) * ROWS, :] = jnp.where(seen, 0.0, NEG)


def main_kernel(q2_ref, g2_ref, dot_ref, bias_ref, z_ref, y_ref, w_ref,
                keep_ref, give_ref, p_ref, ds_ref, s_ref):
    def keys(part, cols):
        ref, at = ((z_ref, 0), (z_ref, 1), (y_ref, 0), (y_ref, 1), (w_ref, 0))[part]
        return ref[at * CHIP_ROWS : (at + 1) * CHIP_ROWS, cols]

    parts = range(WINDOW // CHIP_ROWS)
    key_cols, value_cols = slice(0, DH), slice(DH, 2 * DH)

    def folded(x, op):
        return op(x.reshape(CHIP_ROWS // 8, 8, TILE), axis=0)

    for tile in range(COLS // TILE):
        cols = slice(tile * TILE, (tile + 1) * TILE)
        query = q2_ref[cols, :]
        grad = g2_ref[cols, :]
        top = None
        for part in parts:
            bias = bias_ref[part * CHIP_ROWS : (part + 1) * CHIP_ROWS, :]
            scores = dot_nt(keys(part, key_cols), query) + jnp.concatenate([bias, bias], axis=1)
            s_ref[tile, part] = scores
            part_top = folded(scores, jnp.max)
            top = part_top if top is None else jnp.maximum(top, part_top)
        top = jnp.max(top, axis=0, keepdims=True)
        total = None
        for part in parts:
            weights = jnp.exp2((s_ref[tile, part] - top) * EXP2_SCALING)
            s_ref[tile, part] = weights
            part_total = folded(weights, jnp.sum)
            total = part_total if total is None else total + part_total
        inverse = 1.0 / jnp.sum(total, axis=0, keepdims=True)
        row_dot = dot_ref[0:1, cols]
        for part in parts:
            rows = slice(part * CHIP_ROWS, (part + 1) * CHIP_ROWS)
            weights = s_ref[tile, part] * inverse
            grads = weights * (dot_nt(keys(part, value_cols), grad) - row_dot)
            p_ref[rows, cols] = weights.astype(jnp.bfloat16)
            ds_ref[rows, cols] = grads.astype(jnp.bfloat16)
    for ref, at in ((keep_ref, 0), (give_ref, PAST // 2)):
        rows = slice(at, at + PAST // 2)
        ref[:, key_cols] = (dot_nn(ds_ref[rows, :], q2_ref[...]) * SCALING).astype(ref.dtype)
        ref[:, value_cols] = dot_nn(p_ref[rows, :], g2_ref[...]).astype(ref.dtype)


def finish_kernel(q2_ref, g2_ref, p_ref, ds_ref, z_ref, y_ref, w_ref, dq_ref, own_ref):
    key_cols, value_cols = slice(0, DH), slice(DH, 2 * DH)
    own = slice(PAST, WINDOW)
    own_ref[:, key_cols] = dot_nn(ds_ref[own, :], q2_ref[...]) * SCALING
    own_ref[:, value_cols] = dot_nn(p_ref[own, :], g2_ref[...])
    keys = jnp.concatenate([z_ref[:, key_cols], y_ref[:, key_cols], w_ref[:, key_cols]], axis=0)
    for tile in range(COLS // TILE):
        cols = slice(tile * TILE, (tile + 1) * TILE)
        grads = dot_tn(keys, ds_ref[:, cols]) * SCALING
        for j in range(TILE // DH):
            pair = grads[:, j * DH : (j + 1) * DH].T.astype(jnp.bfloat16)
            head = tile * (TILE // ROWS) + 2 * j
            dq_ref[:, head * DH : (head + 1) * DH] = pair[:ROWS]
            dq_ref[:, (head + 1) * DH : (head + 2) * DH] = pair[ROWS:]


def call(kernel, outs, scratch=(), flops=0, moved=0):
    vmem = pl.BlockSpec(memory_space=pltpu.VMEM)
    return lambda *args: pl.pallas_call(
        kernel,
        out_shape=outs,
        in_specs=[vmem] * len(args),
        out_specs=[vmem] * len(outs),
        scratch_shapes=list(scratch),
        compiler_params=pltpu.CompilerParams(vmem_limit_bytes=24 * 1024 * 1024),
        cost_estimate=pl.CostEstimate(flops=flops, bytes_accessed=moved, transcendentals=0),
    )(*args)


def on_device(query_rows, key_rows, value_rows, saved_out, out_grad, doc_lengths):
    shape = jax.ShapeDtypeStruct
    bf16, f32 = jnp.bfloat16, jnp.float32
    mine = jnp.concatenate([key_rows, value_rows], axis=1)
    own = jnp.concatenate([mine, swap_cores(mine)], axis=0)
    fetched = [move_chips(own, steps, 1) for steps in STEPS]
    q2, g2, row_dot, bias = call(
        prepare_kernel,
        [shape((COLS, DH), bf16), shape((COLS, DH), bf16), shape((8, COLS), f32), shape((WINDOW, DH), f32)],
        flops=10**9, moved=2 * 10**6,
    )(query_rows, saved_out, out_grad, doc_lengths.reshape(1, 64))
    near = jnp.concatenate(fetched, axis=0)
    far = swap_cores(near)
    keep, give, weights, grads = call(
        main_kernel,
        [shape((PAST // 2, 2 * DH), f32), shape((PAST // 2, 2 * DH), bf16),
         shape((WINDOW, COLS), bf16), shape((WINDOW, COLS), bf16)],
        [pltpu.VMEM((COLS // TILE, WINDOW // CHIP_ROWS, CHIP_ROWS, TILE), f32)],
        flops=10**9, moved=2 * 10**6,
    )(q2, g2, row_dot, bias, near, far, own)
    sums = (keep + swap_cores(give).astype(f32)).astype(bf16)
    back = [
        move_chips(sums[i * CHIP_ROWS : (i + 1) * CHIP_ROWS], steps, -1)
        for i, steps in enumerate(STEPS)
    ]
    query_grad, own_sums = call(
        finish_kernel,
        [shape((ROWS, HQ * DH), bf16), shape((CHIP_ROWS, 2 * DH), f32)],
        flops=10**9, moved=2 * 10**6,
    )(q2, g2, weights, grads, near, far, own)
    totals = own_sums + back[0].astype(f32) + back[1].astype(f32)
    result = totals[:ROWS] + swap_cores(totals[ROWS:].astype(bf16)).astype(f32)
    result = result.astype(bf16)
    return (query_grad, result[:, :DH], result[:, DH:])


def solution(mesh):
    placed = P(AXES, None)
    return jax.shard_map(
        on_device,
        mesh=mesh,
        in_specs=(placed,) * 5 + (P(),),
        out_specs=(placed,) * 3,
        check_vma=False,
    )
```

time: 205 us -> 42.6 us (0.21)
  the two profiles are of different devices: /device:TPU:39 before, /device:TPU:55 now
where the time goes in v1:
time: 42.6 us; the launch traced here: 42.2 us
  starting transfers between devices  21.4 us (50%)
  waiting for transfers between devices  10.4 us (24%)
  local copies, waits for them, and re-layouts  5.59 us (13%)
  Pallas kernels  3.98 us (9%)
  between operations  0.73 us (2%)
    ppermute x4, starting transfers between devices, move_chips(): return lax.ppermute(x, AXES, pairs)  17 us
    ppermute x4, waiting for transfers between devices, move_chips(): return lax.ppermute(x, AXES, pairs)  7.72 us
    ppermute x4, starting transfers between devices, swap_cores(): return lax.ppermute(x, 'uly', [(i, i ^ 1) for i in range(16)])  4.41 us
    unnamed x10, local copies, waits for them, and re-layouts  4.23 us
    pallas_call x3, Pallas kernels, call(): pl.pallas_call(kernel, out_shape=outs, in_specs=[vmem] * len(args), out_s...  3.98 us
    ppermute x4, waiting for transfers between devices, swap_cores(): return lax.ppermute(x, 'uly', [(i, i ^ 1) for i in range(16)])  2.71 us
  transfers between devices with their start and end apart: 8, of which 5 were waited for; matrix products, arithmetic and copies ran while one was open for 0% of the time, Pallas kernels for 4%

profile of v1, /device:TPU:55, one launch (start us, length us, event | category | flops | bytes accessed | tf_op | source)
XLA Modules:
  0.0 42.2 jit_solution(4385823506994106406)
XLA Ops:
  0.6 0.7 %constant_dynamic-update-slice_fusion.1 = bf16[64,256]{1,0:T(8,128)(2,1)S(1)} fusion(bf16[64,128]{1,0:T(8,128)(2,1)} %param.7), kind=kLoop, calls=%fused_computation.7 | loop fusion | bytes 32768
  1.4 0.7 %constant_dynamic-update-slice_fusion = bf16[64,256]{1,0:T(8,128)(2,1)S(1)} fusion(bf16[64,256]{1,0:T(8,128)(2,1)S(1)} %constant_dynamic-update-slice_fusion.1, bf16[64,128]{1,0:T(8,128)(2,1)} %param.8), kind=kLoop, calls=%fused_computation.6 | loop fusion | bytes 32768 | tf_op jit(solution)/shard_map/concatenate | solution.py:181
  2.1 0.7 %collective-permute-start = (bf16[64,256]{1,0:T(8,128)(2,1)S(1)}, bf16[64,256]{1,0:T(8,128)(2,1)S(1)}, u32[]{:S(2)}, u32[]{:S(2)}) collective-permute-start(bf16[64,256]{1,0:T(8,128)(2,1)S(1)} %constant_dynamic-update-slice_fusion), channel_id=1, source_target_pairs={{0,1},{1,0},{2,3},{3,2},{4,5},{5,4},{6,7},{7,6},{8,9},{9,8},{10,11... | collective-permute-start | bytes 98312 | tf_op jit(solution)/shard_map/ppermute | solution.py:37
  2.8 0.9 %collective-permute-done = bf16[64,256]{1,0:T(8,128)(2,1)S(1)} collective-permute-done((bf16[64,256]{1,0:T(8,128)(2,1)S(1)}, bf16[64,256]{1,0:T(8,128)(2,1)S(1)}, u32[]{:S(2)}, u32[]{:S(2)}) %collective-permute-start) | collective-permute-done | bytes 32800 | tf_op jit(solution)/shard_map/ppermute | solution.py:37
  3.6 7.3 %collective-permute-start.1 = (bf16[128,256]{1,0:T(8,128)(2,1)S(1)}, bf16[128,256]{1,0:T(8,128)(2,1)S(1)}, u32[]{:S(2)}, u32[]{:S(2)}) collective-permute-start(bf16[128,256]{1,0:T(8,128)(2,1)S(1)} %pad_maximum_fusion.w_ref), channel_id=1, source_target_pairs={{0,2},{1,17},{2,4},{3,19},{4,6},{5,21},{6,16},{7,23},{16,18},{17,3... | collective-permute-start | bytes 196616 | tf_op jit(solution)/shard_map/ppermute | solution.py:47
  10.9 3.0 %collective-permute-start.2 = (bf16[128,256]{1,0:T(8,128)(2,1)S(1)}, bf16[128,256]{1,0:T(8,128)(2,1)S(1)}, u32[]{:S(2)}, u32[]{:S(2)}) collective-permute-start(bf16[128,256]{1,0:T(8,128)(2,1)S(1)} %pad_maximum_fusion.w_ref), channel_id=1, source_target_pairs={{0,4},{1,7},{2,6},{3,17},{4,16},{5,19},{6,18},{7,21},{16,20},{17,2... | collective-permute-start | bytes 196616 | tf_op jit(solution)/shard_map/ppermute | solution.py:47
  13.9 3.8 %collective-permute-done.2 = bf16[128,256]{1,0:T(8,128)(2,1)S(1)} collective-permute-done((bf16[128,256]{1,0:T(8,128)(2,1)S(1)}, bf16[128,256]{1,0:T(8,128)(2,1)S(1)}, u32[]{:S(2)}, u32[]{:S(2)}) %collective-permute-start.2) | collective-permute-done | bytes 65568 | tf_op jit(solution)/shard_map/ppermute | solution.py:47
  17.7 0.0 copy-start
  17.7 0.9 %copy-done = bf16[64,2048]{1,0:T(8,128)(2,1)S(1)} copy-done((bf16[64,2048]{1,0:T(8,128)(2,1)S(1)}, bf16[64,2048]{1,0:T(8,128)(2,1)}, u32[]{:S(2)}) %copy-start) | copy-done | bytes 262168
  18.7 0.9 %copy-done.1 = bf16[64,2048]{1,0:T(8,128)(2,1)S(1)} copy-done((bf16[64,2048]{1,0:T(8,128)(2,1)S(1)}, bf16[64,2048]{1,0:T(8,128)(2,1)}, u32[]{:S(2)}) %copy-start.1) | copy-done | bytes 262168
  19.6 0.9 %copy-done.2 = bf16[64,2048]{1,0:T(8,128)(2,1)S(1)} copy-done((bf16[64,2048]{1,0:T(8,128)(2,1)S(1)}, bf16[64,2048]{1,0:T(8,128)(2,1)}, u32[]{:S(2)}) %copy-start.2) | copy-done | bytes 262168
  20.6 0.7 %copy-done.3 = s32[64]{0:T(128)S(1)} copy-done((s32[64]{0:T(128)S(1)}, s32[64]{0:T(128)}, u32[]{:S(2)}) %copy-start.3) | copy-done | bytes 280
  21.2 0.5 %shard_map.85 = (bf16[1024,128]{1,0:T(8,128)(2,1)S(1)}, bf16[1024,128]{1,0:T(8,128)(2,1)S(1)}, f32[8,1024]{1,0:T(8,128)S(1)}, f32[640,128]{1,0:T(8,128)S(1)}) custom-call(bf16[64,2048]{1,0:T(8,128)(2,1)S(1)} %copy-done, bf16[64,2048]{1,0:T(8,128)(2,1)S(1)} %copy-done.1, bf16[64,2048]{1,0:T(8,128)(2,1)S(1)} %copy-done.2, s32[1,64]{1,0:T(1,128)S(1)} %bitcast.1), custom_call_target="tpu_custom_call" | custom-call | flops 1000000000 | bytes 2000000 | tf_op jit(solution)/shard_map/pallas_call | solution.py:167
  21.7 2.2 %shard_map.86 = (f32[256,256]{1,0:T(8,128)S(1)}, bf16[256,256]{1,0:T(8,128)(2,1)S(1)}, bf16[640,1024]{1,0:T(8,128)(2,1)S(1)}, bf16[640,1024]{1,0:T(8,128)(2,1)S(1)}) custom-call(bf16[1024,128]{1,0:T(8,128)(2,1)S(1)} %get-tuple-element.13.q2_ref, bf16[1024,128]{1,0:T(8,128)(2,1)S(1)} %get-tuple-element.14.g2_ref, f32[8,1024]{1,0:T(8,128)S(1)} %get-tuple-element.15.dot_ref, ...), custom_call_target="tpu_custom_call" | custom-call | flops 1000000000 | bytes 2000000 | tf_op jit(solution)/shard_map/pallas_call | solution.py:167
  24.0 0.6 %collective-permute-start.4 = (bf16[256,256]{1,0:T(8,128)(2,1)S(1)}, bf16[256,256]{1,0:T(8,128)(2,1)S(1)}, u32[]{:S(2)}, u32[]{:S(2)}) collective-permute-start(bf16[256,256]{1,0:T(8,128)(2,1)S(1)} %get-tuple-element.22), channel_id=1, source_target_pairs={{0,1},{1,0},{2,3},{3,2},{4,5},{5,4},{6,7},{7,6},{8,9},{9,8},{10,11... | collective-permute-start | bytes 393224 | tf_op jit(solution)/shard_map/ppermute | solution.py:37
  24.6 1.0 %collective-permute-done.4 = bf16[256,256]{1,0:T(8,128)(2,1)S(1)} collective-permute-done((bf16[256,256]{1,0:T(8,128)(2,1)S(1)}, bf16[256,256]{1,0:T(8,128)(2,1)S(1)}, u32[]{:S(2)}, u32[]{:S(2)}) %collective-permute-start.4) | collective-permute-done | bytes 131104 | tf_op jit(solution)/shard_map/ppermute | solution.py:37
  25.6 1.9 %collective-permute-start.5 = (bf16[128,256]{1,0:T(8,128)(2,1)S(1)}, bf16[128,256]{1,0:T(8,128)(2,1)S(1)}, u32[]{:S(2)}, u32[]{:S(2)}) collective-permute-start(bf16[128,256]{1,0:T(8,128)(2,1)S(1)} %get-tuple-element.23), channel_id=1, source_target_pairs={{2,0},{4,2},{6,4},{16,6},{17,1},{18,16},{19,3},{20,18},{21,5},{22,... | collective-permute-start | bytes 196616 | tf_op jit(solution)/shard_map/ppermute | solution.py:47
  27.5 4.8 %collective-permute-start.6 = (bf16[128,256]{1,0:T(8,128)(2,1)S(1)}, bf16[128,256]{1,0:T(8,128)(2,1)S(1)}, u32[]{:S(2)}, u32[]{:S(2)}) collective-permute-start(bf16[128,256]{1,0:T(8,128)(2,1)S(1)} %get-tuple-element.24), channel_id=1, source_target_pairs={{4,0},{6,2},{7,1},{16,4},{17,3},{18,6},{19,5},{20,16},{21,7},{22,1... | collective-permute-start | bytes 196616 | tf_op jit(solution)/shard_map/ppermute | solution.py:47
  32.3 1.3 %shard_map.87 = (bf16[64,2048]{1,0:T(8,128)(2,1)}, f32[128,256]{1,0:T(8,128)S(1)}) custom-call(bf16[1024,128]{1,0:T(8,128)(2,1)S(1)} %get-tuple-element.13.q2_ref, bf16[1024,128]{1,0:T(8,128)(2,1)S(1)} %get-tuple-element.14.g2_ref, bf16[640,1024]{1,0:T(8,128)(2,1)S(1)} %get-tuple-element.17.p_ref, bf16[640,1024]{1,0:T(8,128)(2,1)S(1)} %get-tuple-element.18.ds_ref, ...), custom_call_target="tpu_custom_call" | custom-call | flops 1000000000 | bytes 2000000 | tf_op jit(solution)/shard_map/pallas_call | solution.py:167
  33.6 0.0 collective-permute-done.5
  33.6 3.9 %collective-permute-done.6 = bf16[128,256]{1,0:T(8,128)(2,1)S(1)} collective-permute-done((bf16[128,256]{1,0:T(8,128)(2,1)S(1)}, bf16[128,256]{1,0:T(8,128)(2,1)S(1)}, u32[]{:S(2)}, u32[]{:S(2)}) %collective-permute-start.6) | collective-permute-done | bytes 65568 | tf_op jit(solution)/shard_map/ppermute | solution.py:47
  37.5 3.1 %collective-permute-start.7 = (bf16[64,256]{1,0:T(8,128)(2,1)S(1)}, bf16[64,256]{1,0:T(8,128)(2,1)S(1)}, u32[]{:S(2)}, u32[]{:S(2)}) collective-permute-start(bf16[64,256]{1,0:T(8,128)(2,1)S(1)} %slice.35), channel_id=1, source_target_pairs={{0,1},{1,0},{2,3},{3,2},{4,5},{5,4},{6,7},{7,6},{8,9},{9,8},{10,11... | collective-permute-start | bytes 98312 | tf_op jit(solution)/shard_map/ppermute | solution.py:37
  40.7 0.9 %collective-permute-done.7 = bf16[64,256]{1,0:T(8,128)(2,1)S(1)} collective-permute-done((bf16[64,256]{1,0:T(8,128)(2,1)S(1)}, bf16[64,256]{1,0:T(8,128)(2,1)S(1)}, u32[]{:S(2)}, u32[]{:S(2)}) %collective-permute-start.7) | collective-permute-done | bytes 32800 | tf_op jit(solution)/shard_map/ppermute | solution.py:37
  41.5 0.6 %fusion.2 = (bf16[64,128]{1,0:T(8,128)(2,1)}, bf16[64,128]{1,0:T(8,128)(2,1)}) fusion(bf16[64,256]{1,0:T(8,128)(2,1)S(1)} %fusion), kind=kLoop, calls=%fused_computation.11 | loop fusion | bytes 65536 | tf_op jit(solution)/shard_map/slice | solution.py:211
  (14 shorter events, 0.1 us)
Async XLA Ops:
  2.1 1.5 %collective-permute-start = (bf16[64,256]{1,0:T(8,128)(2,1)S(1)}, bf16[64,256]{1,0:T(8,128)(2,1)S(1)}, u32[]{:S(2)}, u32[]{:S(2)}) collective-permute-start(bf16[64,256]{1,0:T(8,128)(2,1)S(1)} %constant_dynamic-update-slice_fusion), channel_id=1, source_target_pairs={{0,1},{1,0},{2,3},{3,2},{4,5},{5,4},{6,7},{7,6},{8,9},{9,8},{10,11... | collective-permute-start | bytes 98312 | tf_op jit(solution)/shard_map/ppermute | solution.py:37
  3.6 10.3 %collective-permute-start.1 = (bf16[128,256]{1,0:T(8,128)(2,1)S(1)}, bf16[128,256]{1,0:T(8,128)(2,1)S(1)}, u32[]{:S(2)}, u32[]{:S(2)}) collective-permute-start(bf16[128,256]{1,0:T(8,128)(2,1)S(1)} %pad_maximum_fusion.w_ref), channel_id=1, source_target_pairs={{0,2},{1,17},{2,4},{3,19},{4,6},{5,21},{6,16},{7,23},{16,18},{17,3... | collective-permute-start | bytes 196616 | tf_op jit(solution)/shard_map/ppermute | solution.py:47
  10.9 6.8 %collective-permute-start.2 = (bf16[128,256]{1,0:T(8,128)(2,1)S(1)}, bf16[128,256]{1,0:T(8,128)(2,1)S(1)}, u32[]{:S(2)}, u32[]{:S(2)}) collective-permute-start(bf16[128,256]{1,0:T(8,128)(2,1)S(1)} %pad_maximum_fusion.w_ref), channel_id=1, source_target_pairs={{0,4},{1,7},{2,6},{3,17},{4,16},{5,19},{6,18},{7,21},{16,20},{17,2... | collective-permute-start | bytes 196616 | tf_op jit(solution)/shard_map/ppermute | solution.py:47
  17.7 4.0 %collective-permute-start.3 = (bf16[256,256]{1,0:T(8,128)(2,1)S(1)}, bf16[256,256]{1,0:T(8,128)(2,1)S(1)}, u32[]{:S(2)}, u32[]{:S(2)}) collective-permute-start(bf16[256,256]{1,0:T(8,128)(2,1)S(1)} %constant_dynamic-update-slice_fusion.2.z_ref), channel_id=1, source_target_pairs={{0,1},{1,0},{2,3},{3,2},{4,5},{5,4},{6,7},{7,6},{8,9},{9,8},{10,11... | collective-permute-start | bytes 393224 | tf_op jit(solution)/shard_map/ppermute | solution.py:37
  17.7 1.0 %copy-start = (bf16[64,2048]{1,0:T(8,128)(2,1)S(1)}, bf16[64,2048]{1,0:T(8,128)(2,1)}, u32[]{:S(2)}) copy-start(bf16[64,2048]{1,0:T(8,128)(2,1)} %q_ref.1) | copy-start | bytes 786436
  18.7 0.9 %copy-start.1 = (bf16[64,2048]{1,0:T(8,128)(2,1)S(1)}, bf16[64,2048]{1,0:T(8,128)(2,1)}, u32[]{:S(2)}) copy-start(bf16[64,2048]{1,0:T(8,128)(2,1)} %o_ref.1) | copy-start | bytes 786436
  19.6 0.9 %copy-start.2 = (bf16[64,2048]{1,0:T(8,128)(2,1)S(1)}, bf16[64,2048]{1,0:T(8,128)(2,1)}, u32[]{:S(2)}) copy-start(bf16[64,2048]{1,0:T(8,128)(2,1)} %g_ref.1) | copy-start | bytes 786436
  20.6 0.7 %copy-start.3 = (s32[64]{0:T(128)S(1)}, s32[64]{0:T(128)}, u32[]{:S(2)}) copy-start(s32[64]{0:T(128)} %param.11) | copy-start | bytes 772
  24.0 1.6 %collective-permute-start.4 = (bf16[256,256]{1,0:T(8,128)(2,1)S(1)}, bf16[256,256]{1,0:T(8,128)(2,1)S(1)}, u32[]{:S(2)}, u32[]{:S(2)}) collective-permute-start(bf16[256,256]{1,0:T(8,128)(2,1)S(1)} %get-tuple-element.22), channel_id=1, source_target_pairs={{0,1},{1,0},{2,3},{3,2},{4,5},{5,4},{6,7},{7,6},{8,9},{9,8},{10,11... | collective-permute-start | bytes 393224 | tf_op jit(solution)/shard_map/ppermute | solution.py:37
  25.6 8.0 %collective-permute-start.5 = (bf16[128,256]{1,0:T(8,128)(2,1)S(1)}, bf16[128,256]{1,0:T(8,128)(2,1)S(1)}, u32[]{:S(2)}, u32[]{:S(2)}) collective-permute-start(bf16[128,256]{1,0:T(8,128)(2,1)S(1)} %get-tuple-element.23), channel_id=1, source_target_pairs={{2,0},{4,2},{6,4},{16,6},{17,1},{18,16},{19,3},{20,18},{21,5},{22,... | collective-permute-start | bytes 196616 | tf_op jit(solution)/shard_map/ppermute | solution.py:47
  27.5 10.0 %collective-permute-start.6 = (bf16[128,256]{1,0:T(8,128)(2,1)S(1)}, bf16[128,256]{1,0:T(8,128)(2,1)S(1)}, u32[]{:S(2)}, u32[]{:S(2)}) collective-permute-start(bf16[128,256]{1,0:T(8,128)(2,1)S(1)} %get-tuple-element.24), channel_id=1, source_target_pairs={{4,0},{6,2},{7,1},{16,4},{17,3},{18,6},{19,5},{20,16},{21,7},{22,1... | collective-permute-start | bytes 196616 | tf_op jit(solution)/shard_map/ppermute | solution.py:47
  37.5 4.0 %collective-permute-start.7 = (bf16[64,256]{1,0:T(8,128)(2,1)S(1)}, bf16[64,256]{1,0:T(8,128)(2,1)S(1)}, u32[]{:S(2)}, u32[]{:S(2)}) collective-permute-start(bf16[64,256]{1,0:T(8,128)(2,1)S(1)} %slice.35), channel_id=1, source_target_pairs={{0,1},{1,0},{2,3},{3,2},{4,5},{5,4},{6,7},{7,6},{8,9},{9,8},{10,11... | collective-permute-start | bytes 98312 | tf_op jit(solution)/shard_map/ppermute | solution.py:37

commit v2 on v1

--- a/solution.py
+++ b/solution.py
@@ -23,7 +23,7 @@
 SCALING = 1.0 / math.sqrt(DH)
 EXP2_SCALING = SCALING * math.log2(math.e)
 AXES = ("blk", "uly")
-STEPS = ((1, 4), (2, 3))
+STEPS = ((2, 3), (1, 4))
 
 
 def device_of(chunk):
@@ -41,9 +41,8 @@
     pairs = []
     for chunk in range(CHUNKS):
         chip, core = divmod(chunk, 2)
-        target = chip + sign * steps[core]
-        if 0 <= target < CHIPS:
-            pairs.append((device_of(chunk), device_of(2 * target + core)))
+        target = (chip + sign * steps[core]) % CHIPS
+        pairs.append((device_of(chunk), device_of(2 * target + core)))
     return lax.ppermute(x, AXES, pairs)
 
 
@@ -59,7 +58,18 @@
     return lax.dot_general(a, b, (((0,), (0,)), ((), ())), preferred_element_type=jnp.float32)
 
 
-def prepare_kernel(q_ref, o_ref, g_ref, len_ref, q2_ref, g2_ref, dot_ref, bias_ref):
+def pack_kernel(mine_ref, other_k_ref, other_v_ref, w_ref):
+    w_ref[:ROWS, :] = mine_ref[...]
+    w_ref[ROWS:, :DH] = other_k_ref[...]
+    w_ref[ROWS:, DH:] = other_v_ref[...]
+
+
+def prepare_kernel(q_hbm, o_hbm, g_hbm, len_hbm, q2_ref, g2_ref, dot_ref, bias_ref,
+                   q_ref, o_ref, g_ref, len_ref, sems):
+    pairs = ((len_hbm, len_ref), (g_hbm, g_ref), (o_hbm, o_ref), (q_hbm, q_ref))
+    copies = [pltpu.make_async_copy(src, dst, sems.at[i]) for i, (src, dst) in enumerate(pairs)]
+    for copy in copies:
+        copy.start()
     blk = lax.axis_index("blk")
     uly = lax.axis_index("uly")
     core = lax.rem(uly, 2)
@@ -68,18 +78,7 @@
     chunk = half * HALF_CHUNKS + place
     chip = chunk // 2
 
-    ones = jnp.ones((8, DH), jnp.bfloat16)
-    for h in range(HQ):
-        cols = slice(h * DH, (h + 1) * DH)
-        rows = slice(h * ROWS, (h + 1) * ROWS)
-        grad = g_ref[:, cols]
-        q2_ref[rows, :] = q_ref[:, cols]
-        g2_ref[rows, :] = grad
-        prod = grad.astype(jnp.float32) * o_ref[:, cols].astype(jnp.float32)
-        high = prod.astype(jnp.bfloat16)
-        low = (prod - high.astype(jnp.float32)).astype(jnp.bfloat16)
-        dot_ref[:, rows] = dot_nt(ones, high) + dot_nt(ones, low)
-
+    copies[0].wait()
     lens = jnp.broadcast_to(len_ref[...].astype(jnp.float32), (64, 64))
     doc = lax.broadcasted_iota(jnp.int32, (64, 64), 0)
     other = lax.broadcasted_iota(jnp.int32, (64, 64), 1)
@@ -100,6 +99,20 @@
         where = (2 * (chip - back) + held) * ROWS + index
         seen = (where >= first) & (where <= here)
         bias_ref[part * ROWS : (part + 1) * ROWS, :] = jnp.where(seen, 0.0, NEG)
+
+    for copy in copies[1:]:
+        copy.wait()
+    ones = jnp.ones((8, DH), jnp.bfloat16)
+    for h in range(HQ):
+        cols = slice(h * DH, (h + 1) * DH)
+        rows = slice(h * ROWS, (h + 1) * ROWS)
+        grad = g_ref[:, cols]
+        q2_ref[rows, :] = q_ref[:, cols]
+        g2_ref[rows, :] = grad
+        prod = grad.astype(jnp.float32) * o_ref[:, cols].astype(jnp.float32)
+        high = prod.astype(jnp.bfloat16)
+        low = (prod - high.astype(jnp.float32)).astype(jnp.bfloat16)
+        dot_ref[:, rows] = dot_nt(ones, high) + dot_nt(ones, low)
 
 
 def main_kernel(q2_ref, g2_ref, dot_ref, bias_ref, z_ref, y_ref, w_ref,
@@ -162,30 +175,35 @@
             dq_ref[:, (head + 1) * DH : (head + 2) * DH] = pair[ROWS:]
 
 
-def call(kernel, outs, scratch=(), flops=0, moved=0):
+def call(kernel, outs, scratch=(), space=pltpu.VMEM):
     vmem = pl.BlockSpec(memory_space=pltpu.VMEM)
     return lambda *args: pl.pallas_call(
         kernel,
         out_shape=outs,
-        in_specs=[vmem] * len(args),
+        in_specs=[pl.BlockSpec(memory_space=space)] * len(args),
         out_specs=[vmem] * len(outs),
         scratch_shapes=list(scratch),
         compiler_params=pltpu.CompilerParams(vmem_limit_bytes=24 * 1024 * 1024),
-        cost_estimate=pl.CostEstimate(flops=flops, bytes_accessed=moved, transcendentals=0),
+        cost_estimate=pl.CostEstimate(flops=10**9, bytes_accessed=2 * 10**6, transcendentals=0),
     )(*args)
 
 
 def on_device(query_rows, key_rows, value_rows, saved_out, out_grad, doc_lengths):
     shape = jax.ShapeDtypeStruct
     bf16, f32 = jnp.bfloat16, jnp.float32
+    other = (swap_cores(key_rows), swap_cores(value_rows))
     mine = jnp.concatenate([key_rows, value_rows], axis=1)
-    own = jnp.concatenate([mine, swap_cores(mine)], axis=0)
+    other, mine = lax.optimization_barrier((other, mine))
+    own = call(pack_kernel, [shape((CHIP_ROWS, 2 * DH), bf16)])(mine, *other)[0]
     fetched = [move_chips(own, steps, 1) for steps in STEPS]
-    q2, g2, row_dot, bias = call(
+    prepared = call(
         prepare_kernel,
         [shape((COLS, DH), bf16), shape((COLS, DH), bf16), shape((8, COLS), f32), shape((WINDOW, DH), f32)],
-        flops=10**9, moved=2 * 10**6,
+        [pltpu.VMEM((ROWS, HQ * DH), bf16)] * 3
+        + [pltpu.VMEM((1, 64), jnp.int32), pltpu.SemaphoreType.DMA((4,))],
+        pl.ANY,
     )(query_rows, saved_out, out_grad, doc_lengths.reshape(1, 64))
+    fetched, (q2, g2, row_dot, bias) = lax.optimization_barrier((fetched, prepared))
     near = jnp.concatenate(fetched, axis=0)
     far = swap_cores(near)
     keep, give, weights, grads = call(
@@ -193,7 +211,6 @@
         [shape((PAST // 2, 2 * DH), f32), shape((PAST // 2, 2 * DH), bf16),
          shape((WINDOW, COLS), bf16), shape((WINDOW, COLS), bf16)],
         [pltpu.VMEM((COLS // TILE, WINDOW // CHIP_ROWS, CHIP_ROWS, TILE), f32)],
-        flops=10**9, moved=2 * 10**6,
     )(q2, g2, row_dot, bias, near, far, own)
     sums = (keep + swap_cores(give).astype(f32)).astype(bf16)
     back = [
@@ -203,7 +220,6 @@
     query_grad, own_sums = call(
         finish_kernel,
         [shape((ROWS, HQ * DH), bf16), shape((CHIP_ROWS, 2 * DH), f32)],
-        flops=10**9, moved=2 * 10**6,
     )(q2, g2, weights, grads, near, far, own)
     totals = own_sums + back[0].astype(f32) + back[1].astype(f32)
     result = totals[:ROWS] + swap_cores(totals[ROWS:].astype(bf16)).astype(f32)

time: 42.6 us -> 31.8 us (0.75)
  the two profiles are of different devices: /device:TPU:55 before, /device:TPU:63 now
where the time goes in v2:
time: 31.8 us; the launch traced here: 31.6 us
  starting transfers between devices  15.8 us (50%)
  waiting for transfers between devices  9.36 us (29%)
  Pallas kernels  4.23 us (13%)
  other arithmetic  0.79 us (2%)
  between operations  0.73 us (2%)
  local copies, waits for them, and re-layouts  0.66 us (2%)
    ppermute x4, starting transfers between devices, move_chips(): return lax.ppermute(x, AXES, pairs)  10.9 us
    ppermute x4, waiting for transfers between devices, move_chips(): return lax.ppermute(x, AXES, pairs)  6.01 us
    ppermute x5, starting transfers between devices, swap_cores(): return lax.ppermute(x, 'uly', [(i, i ^ 1) for i in range(16)])  4.89 us
    pallas_call x4, Pallas kernels, call(): pl.pallas_call(kernel, out_shape=outs, in_specs=[pl.BlockSpec(memory_spac...  4.23 us
    ppermute x5, waiting for transfers between devices, swap_cores(): return lax.ppermute(x, 'uly', [(i, i ^ 1) for i in range(16)])  3.36 us
    concatenate x1, other arithmetic, on_device(): mine = jnp.concatenate([key_rows, value_rows], axis=1)  0.74 us
  transfers between devices with their start and end apart: 9, of which 8 were waited for; matrix products, arithmetic and copies ran while one was open for 2% of the time, Pallas kernels for 6%

profile of v2, /device:TPU:63, one launch (start us, length us, event | category | flops | bytes accessed | tf_op | source)
XLA Modules:
  0.0 31.6 jit_solution(6451562878163448732)
XLA Ops:
  0.6 0.8 %collective-permute-start = (bf16[64,128]{1,0:T(8,128)(2,1)}, bf16[64,128]{1,0:T(8,128)(2,1)S(1)}, u32[]{:S(2)}, u32[]{:S(2)}) collective-permute-start(bf16[64,128]{1,0:T(8,128)(2,1)} %param.7), channel_id=1, source_target_pairs={{0,1},{1,0},{2,3},{3,2},{4,5},{5,4},{6,7},{7,6},{8,9},{9,8},{10,11... | collective-permute-start | bytes 49160 | tf_op jit(solution)/shard_map/ppermute | solution.py:37
  1.4 0.1 collective-permute-start.1
  1.5 0.7 %pad_maximum_fusion.mine_ref = bf16[64,256]{1,0:T(8,128)(2,1)S(1)} fusion(bf16[64,128]{1,0:T(8,128)(2,1)} %param.8, bf16[64,128]{1,0:T(8,128)(2,1)} %param.7), kind=kLoop, calls=%fused_computation.5 | loop fusion | flops 65536 | bytes 65536 | tf_op jit(solution)/shard_map/concatenate | solution.py:195
  2.2 0.0 copy-start.2
  2.3 0.0 copy-start.3
  2.3 0.2 collective-permute-done.other_k_ref
  2.4 0.3 %collective-permute-done.1.other_v_ref = bf16[64,128]{1,0:T(8,128)(2,1)S(1)} collective-permute-done((bf16[64,128]{1,0:T(8,128)(2,1)}, bf16[64,128]{1,0:T(8,128)(2,1)S(1)}, u32[]{:S(2)}, u32[]{:S(2)}) %collective-permute-start.1) | collective-permute-done | bytes 16416 | tf_op jit(solution)/shard_map/ppermute | solution.py:37
  2.8 5.6 %collective-permute-start.2 = (bf16[128,256]{1,0:T(8,128)(2,1)S(1)}, bf16[128,256]{1,0:T(8,128)(2,1)S(1)}, u32[]{:S(2)}, u32[]{:S(2)}) collective-permute-start(bf16[128,256]{1,0:T(8,128)(2,1)S(1)} %shard_map.85.w_ref), channel_id=1, source_target_pairs={{0,4},{1,7},{2,6},{3,17},{4,16},{5,19},{6,18},{7,21},{16,20},{17,2... | collective-permute-start | bytes 196616 | tf_op jit(solution)/shard_map/ppermute | solution.py:46
  8.4 1.2 %collective-permute-start.3 = (bf16[128,256]{1,0:T(8,128)(2,1)S(1)}, bf16[128,256]{1,0:T(8,128)(2,1)S(1)}, u32[]{:S(2)}, u32[]{:S(2)}) collective-permute-start(bf16[128,256]{1,0:T(8,128)(2,1)S(1)} %shard_map.85.w_ref), channel_id=1, source_target_pairs={{0,2},{1,17},{2,4},{3,19},{4,6},{5,21},{6,16},{7,23},{16,18},{17,3... | collective-permute-start | bytes 196616 | tf_op jit(solution)/shard_map/ppermute | solution.py:46
  9.6 0.8 %shard_map.86 = (bf16[1024,128]{1,0:T(8,128)(2,1)S(1)}, bf16[1024,128]{1,0:T(8,128)(2,1)S(1)}, f32[8,1024]{1,0:T(8,128)S(1)}, f32[640,128]{1,0:T(8,128)S(1)}) custom-call(bf16[64,2048]{1,0:T(8,128)(2,1)S(1)} %copy-done, bf16[64,2048]{1,0:T(8,128)(2,1)S(1)} %copy-done.1, bf16[64,2048]{1,0:T(8,128)(2,1)S(1)} %copy-done.2, s32[1,64]{1,0:T(1,128)S(1)} %bitcast.1), custom_call_target="tpu_custom_call" | custom-call | flops 1000000000 | bytes 2000000 | tf_op jit(solution)/shard_map/pallas_call | solution.py:180
  10.4 2.0 %collective-permute-done.3 = bf16[128,256]{1,0:T(8,128)(2,1)S(1)} collective-permute-done((bf16[128,256]{1,0:T(8,128)(2,1)S(1)}, bf16[128,256]{1,0:T(8,128)(2,1)S(1)}, u32[]{:S(2)}, u32[]{:S(2)}) %collective-permute-start.3) | collective-permute-done | bytes 65568 | tf_op jit(solution)/shard_map/ppermute | solution.py:46
  12.5 1.3 %collective-permute-start.4 = (bf16[256,256]{1,0:T(8,128)(2,1)S(1)}, bf16[256,256]{1,0:T(8,128)(2,1)S(1)}, u32[]{:S(2)}, u32[]{:S(2)}) collective-permute-start(bf16[256,256]{1,0:T(8,128)(2,1)S(1)} %constant_dynamic-update-slice_fusion.z_ref), channel_id=1, source_target_pairs={{0,1},{1,0},{2,3},{3,2},{4,5},{5,4},{6,7},{7,6},{8,9},{9,8},{10,11... | collective-permute-start | bytes 393224 | tf_op jit(solution)/shard_map/ppermute | solution.py:37
  13.7 1.0 %collective-permute-done.4.y_ref = bf16[256,256]{1,0:T(8,128)(2,1)S(1)} collective-permute-done((bf16[256,256]{1,0:T(8,128)(2,1)S(1)}, bf16[256,256]{1,0:T(8,128)(2,1)S(1)}, u32[]{:S(2)}, u32[]{:S(2)}) %collective-permute-start.4) | collective-permute-done | bytes 131104 | tf_op jit(solution)/shard_map/ppermute | solution.py:37
  14.7 2.2 %shard_map.87 = (f32[256,256]{1,0:T(8,128)S(1)}, bf16[256,256]{1,0:T(8,128)(2,1)S(1)}, bf16[640,1024]{1,0:T(8,128)(2,1)S(1)}, bf16[640,1024]{1,0:T(8,128)(2,1)S(1)}) custom-call(bf16[1024,128]{1,0:T(8,128)(2,1)S(1)} %get-tuple-element.29.q2_ref, bf16[1024,128]{1,0:T(8,128)(2,1)S(1)} %get-tuple-element.30.g2_ref, f32[8,1024]{1,0:T(8,128)S(1)} %get-tuple-element.31.dot_ref, ...), custom_call_target="tpu_custom_call" | custom-call | flops 1000000000 | bytes 2000000 | tf_op jit(solution)/shard_map/pallas_call | solution.py:180
  16.9 0.4 %collective-permute-start.5 = (bf16[256,256]{1,0:T(8,128)(2,1)S(1)}, bf16[256,256]{1,0:T(8,128)(2,1)S(1)}, u32[]{:S(2)}, u32[]{:S(2)}) collective-permute-start(bf16[256,256]{1,0:T(8,128)(2,1)S(1)} %get-tuple-element.40), channel_id=1, source_target_pairs={{0,1},{1,0},{2,3},{3,2},{4,5},{5,4},{6,7},{7,6},{8,9},{9,8},{10,11... | collective-permute-start | bytes 393224 | tf_op jit(solution)/shard_map/ppermute | solution.py:37
  17.4 1.0 %collective-permute-done.5 = bf16[256,256]{1,0:T(8,128)(2,1)S(1)} collective-permute-done((bf16[256,256]{1,0:T(8,128)(2,1)S(1)}, bf16[256,256]{1,0:T(8,128)(2,1)S(1)}, u32[]{:S(2)}, u32[]{:S(2)}) %collective-permute-start.5) | collective-permute-done | bytes 131104 | tf_op jit(solution)/shard_map/ppermute | solution.py:37
  18.4 0.1 collective-permute-start.6
  18.5 4.0 %collective-permute-start.7 = (bf16[128,256]{1,0:T(8,128)(2,1)S(1)}, bf16[128,256]{1,0:T(8,128)(2,1)S(1)}, u32[]{:S(2)}, u32[]{:S(2)}) collective-permute-start(bf16[128,256]{1,0:T(8,128)(2,1)S(1)} %get-tuple-element.42), channel_id=1, source_target_pairs={{0,14},{1,9},{2,0},{3,11},{4,2},{5,13},{6,4},{7,15},{16,6},{17,1},... | collective-permute-start | bytes 196616 | tf_op jit(solution)/shard_map/ppermute | solution.py:46
  22.5 1.3 %shard_map.88 = (bf16[64,2048]{1,0:T(8,128)(2,1)}, f32[128,256]{1,0:T(8,128)S(1)}) custom-call(bf16[1024,128]{1,0:T(8,128)(2,1)S(1)} %get-tuple-element.29.q2_ref, bf16[1024,128]{1,0:T(8,128)(2,1)S(1)} %get-tuple-element.30.g2_ref, bf16[640,1024]{1,0:T(8,128)(2,1)S(1)} %get-tuple-element.35.p_ref, bf16[640,1024]{1,0:T(8,128)(2,1)S(1)} %get-tuple-element.36.ds_ref, ...), custom_call_target="tpu_custom_call" | custom-call | flops 1000000000 | bytes 2000000 | tf_op jit(solution)/shard_map/pallas_call | solution.py:180
  23.8 1.7 %collective-permute-done.6 = bf16[128,256]{1,0:T(8,128)(2,1)S(1)} collective-permute-done((bf16[128,256]{1,0:T(8,128)(2,1)S(1)}, bf16[128,256]{1,0:T(8,128)(2,1)S(1)}, u32[]{:S(2)}, u32[]{:S(2)}) %collective-permute-start.6) | collective-permute-done | bytes 65568 | tf_op jit(solution)/shard_map/ppermute | solution.py:46
  25.5 2.2 %collective-permute-done.7 = bf16[128,256]{1,0:T(8,128)(2,1)S(1)} collective-permute-done((bf16[128,256]{1,0:T(8,128)(2,1)S(1)}, bf16[128,256]{1,0:T(8,128)(2,1)S(1)}, u32[]{:S(2)}, u32[]{:S(2)}) %collective-permute-start.7) | collective-permute-done | bytes 65568 | tf_op jit(solution)/shard_map/ppermute | solution.py:46
  27.8 2.3 %collective-permute-start.8 = (bf16[64,256]{1,0:T(8,128)(2,1)S(1)}, bf16[64,256]{1,0:T(8,128)(2,1)S(1)}, u32[]{:S(2)}, u32[]{:S(2)}) collective-permute-start(bf16[64,256]{1,0:T(8,128)(2,1)S(1)} %slice.35), channel_id=1, source_target_pairs={{0,1},{1,0},{2,3},{3,2},{4,5},{5,4},{6,7},{7,6},{8,9},{9,8},{10,11... | collective-permute-start | bytes 98312 | tf_op jit(solution)/shard_map/ppermute | solution.py:37
  30.1 0.9 %collective-permute-done.8 = bf16[64,256]{1,0:T(8,128)(2,1)S(1)} collective-permute-done((bf16[64,256]{1,0:T(8,128)(2,1)S(1)}, bf16[64,256]{1,0:T(8,128)(2,1)S(1)}, u32[]{:S(2)}, u32[]{:S(2)}) %collective-permute-start.8) | collective-permute-done | bytes 32800 | tf_op jit(solution)/shard_map/ppermute | solution.py:37
  31.0 0.6 %fusion.2 = (bf16[64,128]{1,0:T(8,128)(2,1)}, bf16[64,128]{1,0:T(8,128)(2,1)}) fusion(bf16[64,256]{1,0:T(8,128)(2,1)S(1)} %fusion), kind=kLoop, calls=%fused_computation.9 | loop fusion | bytes 65536 | tf_op jit(solution)/shard_map/slice | solution.py:227
  (15 shorter events, 0.1 us)
Async XLA Ops:
  0.6 1.8 %collective-permute-start = (bf16[64,128]{1,0:T(8,128)(2,1)}, bf16[64,128]{1,0:T(8,128)(2,1)S(1)}, u32[]{:S(2)}, u32[]{:S(2)}) collective-permute-start(bf16[64,128]{1,0:T(8,128)(2,1)} %param.7), channel_id=1, source_target_pairs={{0,1},{1,0},{2,3},{3,2},{4,5},{5,4},{6,7},{7,6},{8,9},{9,8},{10,11... | collective-permute-start | bytes 49160 | tf_op jit(solution)/shard_map/ppermute | solution.py:37
  1.4 1.4 %collective-permute-start.1 = (bf16[64,128]{1,0:T(8,128)(2,1)}, bf16[64,128]{1,0:T(8,128)(2,1)S(1)}, u32[]{:S(2)}, u32[]{:S(2)}) collective-permute-start(bf16[64,128]{1,0:T(8,128)(2,1)} %param.8), channel_id=1, source_target_pairs={{0,1},{1,0},{2,3},{3,2},{4,5},{5,4},{6,7},{7,6},{8,9},{9,8},{10,11... | collective-permute-start | bytes 49160 | tf_op jit(solution)/shard_map/ppermute | solution.py:37
  2.2 7.4 %copy-start = (bf16[64,2048]{1,0:T(8,128)(2,1)S(1)}, bf16[64,2048]{1,0:T(8,128)(2,1)}, u32[]{:S(2)}) copy-start(bf16[64,2048]{1,0:T(8,128)(2,1)} %q_hbm.1) | copy-start | bytes 786436
  2.2 7.4 %copy-start.1 = (bf16[64,2048]{1,0:T(8,128)(2,1)S(1)}, bf16[64,2048]{1,0:T(8,128)(2,1)}, u32[]{:S(2)}) copy-start(bf16[64,2048]{1,0:T(8,128)(2,1)} %o_hbm.1) | copy-start | bytes 786436
  2.2 7.4 %copy-start.2 = (bf16[64,2048]{1,0:T(8,128)(2,1)S(1)}, bf16[64,2048]{1,0:T(8,128)(2,1)}, u32[]{:S(2)}) copy-start(bf16[64,2048]{1,0:T(8,128)(2,1)} %g_hbm.1) | copy-start | bytes 786436
  2.3 7.4 %copy-start.3 = (s32[64]{0:T(128)S(1)}, s32[64]{0:T(128)}, u32[]{:S(2)}) copy-start(s32[64]{0:T(128)} %param.11) | copy-start | bytes 772
  2.8 7.6 %collective-permute-start.2 = (bf16[128,256]{1,0:T(8,128)(2,1)S(1)}, bf16[128,256]{1,0:T(8,128)(2,1)S(1)}, u32[]{:S(2)}, u32[]{:S(2)}) collective-permute-start(bf16[128,256]{1,0:T(8,128)(2,1)S(1)} %shard_map.85.w_ref), channel_id=1, source_target_pairs={{0,4},{1,7},{2,6},{3,17},{4,16},{5,19},{6,18},{7,21},{16,20},{17,2... | collective-permute-start | bytes 196616 | tf_op jit(solution)/shard_map/ppermute | solution.py:46
  8.4 4.0 %collective-permute-start.3 = (bf16[128,256]{1,0:T(8,128)(2,1)S(1)}, bf16[128,256]{1,0:T(8,128)(2,1)S(1)}, u32[]{:S(2)}, u32[]{:S(2)}) collective-permute-start(bf16[128,256]{1,0:T(8,128)(2,1)S(1)} %shard_map.85.w_ref), channel_id=1, source_target_pairs={{0,2},{1,17},{2,4},{3,19},{4,6},{5,21},{6,16},{7,23},{16,18},{17,3... | collective-permute-start | bytes 196616 | tf_op jit(solution)/shard_map/ppermute | solution.py:46
  12.5 2.3 %collective-permute-start.4 = (bf16[256,256]{1,0:T(8,128)(2,1)S(1)}, bf16[256,256]{1,0:T(8,128)(2,1)S(1)}, u32[]{:S(2)}, u32[]{:S(2)}) collective-permute-start(bf16[256,256]{1,0:T(8,128)(2,1)S(1)} %constant_dynamic-update-slice_fusion.z_ref), channel_id=1, source_target_pairs={{0,1},{1,0},{2,3},{3,2},{4,5},{5,4},{6,7},{7,6},{8,9},{9,8},{10,11... | collective-permute-start | bytes 393224 | tf_op jit(solution)/shard_map/ppermute | solution.py:37
  16.9 1.4 %collective-permute-start.5 = (bf16[256,256]{1,0:T(8,128)(2,1)S(1)}, bf16[256,256]{1,0:T(8,128)(2,1)S(1)}, u32[]{:S(2)}, u32[]{:S(2)}) collective-permute-start(bf16[256,256]{1,0:T(8,128)(2,1)S(1)} %get-tuple-element.40), channel_id=1, source_target_pairs={{0,1},{1,0},{2,3},{3,2},{4,5},{5,4},{6,7},{7,6},{8,9},{9,8},{10,11... | collective-permute-start | bytes 393224 | tf_op jit(solution)/shard_map/ppermute | solution.py:37
  18.4 7.1 %collective-permute-start.6 = (bf16[128,256]{1,0:T(8,128)(2,1)S(1)}, bf16[128,256]{1,0:T(8,128)(2,1)S(1)}, u32[]{:S(2)}, u32[]{:S(2)}) collective-permute-start(bf16[128,256]{1,0:T(8,128)(2,1)S(1)} %get-tuple-element.41), channel_id=1, source_target_pairs={{0,12},{1,11},{2,14},{3,13},{4,0},{5,15},{6,2},{7,1},{16,4},{17,3}... | collective-permute-start | bytes 196616 | tf_op jit(solution)/shard_map/ppermute | solution.py:46
  18.5 9.2 %collective-permute-start.7 = (bf16[128,256]{1,0:T(8,128)(2,1)S(1)}, bf16[128,256]{1,0:T(8,128)(2,1)S(1)}, u32[]{:S(2)}, u32[]{:S(2)}) collective-permute-start(bf16[128,256]{1,0:T(8,128)(2,1)S(1)} %get-tuple-element.42), channel_id=1, source_target_pairs={{0,14},{1,9},{2,0},{3,11},{4,2},{5,13},{6,4},{7,15},{16,6},{17,1},... | collective-permute-start | bytes 196616 | tf_op jit(solution)/shard_map/ppermute | solution.py:46
  27.8 3.2 %collective-permute-start.8 = (bf16[64,256]{1,0:T(8,128)(2,1)S(1)}, bf16[64,256]{1,0:T(8,128)(2,1)S(1)}, u32[]{:S(2)}, u32[]{:S(2)}) collective-permute-start(bf16[64,256]{1,0:T(8,128)(2,1)S(1)} %slice.35), channel_id=1, source_target_pairs={{0,1},{1,0},{2,3},{3,2},{4,5},{5,4},{6,7},{7,6},{8,9},{9,8},{10,11... | collective-permute-start | bytes 98312 | tf_op jit(solution)/shard_map/ppermute | solution.py:37

commit v3 on v1

v3 whole, which is shorter than its diff:
```python
import functools
import math

import jax
import jax.numpy as jnp
from jax import lax
from jax.experimental import pallas as pl
from jax.experimental.pallas import tpu as pltpu
from jax.sharding import PartitionSpec as P

DH = 128
HQ = 16
ROWS = 64
CHUNKS = 256
CHIPS = CHUNKS // 2
HALF_CHUNKS = 8
HALVES = CHUNKS // HALF_CHUNKS
COLS = HQ * ROWS
CHIP_ROWS = 2 * ROWS
PAST = 2 * CHIP_ROWS
TILE = 256
TILES = COLS // TILE
NEG = -1e30
SCALING = 1.0 / math.sqrt(DH)
EXP2_SCALING = SCALING * math.log2(math.e)
AXES = ("blk", "uly")
STEPS = ((1, 4), (2, 3))
CROSS = (1, 1)
PIECES = (0, 352, 704, COLS)
KEY_COLS, VALUE_COLS = slice(0, DH), slice(DH, 2 * DH)


def device_of(chunk):
    half, place = divmod(chunk, HALF_CHUNKS)
    if half < HALVES // 2:
        return half * 16 + place
    return (HALVES - 1 - half) * 16 + 8 + place


def swap_cores(x):
    return lax.ppermute(x, "uly", [(i, i ^ 1) for i in range(16)])


def move_chips(x, number, forward):
    steps, cross = STEPS[number], CROSS[number]
    pairs = []
    for chunk in range(CHUNKS):
        chip, core = divmod(chunk, 2)
        target = (chip + steps[core]) % CHIPS
        pair = (device_of(chunk), device_of(2 * target + (core ^ cross)))
        pairs.append(pair if forward else pair[::-1])
    return lax.ppermute(x, AXES, pairs)


def dot(a, b, contract):
    return lax.dot_general(a, b, (contract, ((), ())), preferred_element_type=jnp.float32)


def dot_nt(a, b):
    return dot(a, b, ((1,), (1,)))


def dot_nn(a, b):
    return dot(a, b, ((1,), (0,)))


def dot_tn(a, b):
    return dot(a, b, ((0,), (0,)))


def pack_kernel(mine_ref, other_k_ref, other_v_ref, w_ref):
    w_ref[:ROWS, :] = mine_ref[...]
    w_ref[ROWS:, :DH] = other_k_ref[...]
    w_ref[ROWS:, DH:] = other_v_ref[...]


def folded(x, op):
    return op(x.reshape(x.shape[0] // 8, 8, x.shape[1]), axis=0)


def tiles():
    for tile in range(2 * TILES):
        side, at = divmod(tile, TILES)
        yield slice(tile * TILE, (tile + 1) * TILE), side, slice(at * TILE, (at + 1) * TILE)


def scored(keys, query, bias):
    scores = dot_nt(keys, query) + jnp.concatenate([bias, bias], axis=1)
    top = jnp.max(folded(scores, jnp.max), axis=0, keepdims=True)
    weights = jnp.exp2((scores - top) * EXP2_SCALING)
    return weights, top, jnp.sum(folded(weights, jnp.sum), axis=0, keepdims=True)


def prepare_kernel(q_ref, o_ref, g_ref, partner_q_ref, partner_g_ref, len_ref, mine_ref,
                   q2_ref, g2_ref, dot_ref, bias_ref, e_ref, top_ref, sum_ref):
    blk = lax.axis_index("blk")
    uly = lax.axis_index("uly")
    core = lax.rem(uly, 2)
    place = lax.rem(uly, HALF_CHUNKS)
    half = jnp.where(uly < HALF_CHUNKS, blk, HALVES - 1 - blk)
    chunk = half * HALF_CHUNKS + place
    chip = chunk // 2

    ones = jnp.ones((8, DH), jnp.bfloat16)
    for h in range(HQ):
        cols = slice(h * DH, (h + 1) * DH)
        rows = slice(h * ROWS, (h + 1) * ROWS)
        grad = g_ref[:, cols]
        q2_ref[rows, :] = q_ref[:, cols]
        g2_ref[rows, :] = grad
        partner_rows = slice(COLS + h * ROWS, COLS + (h + 1) * ROWS)
        q2_ref[partner_rows, :] = partner_q_ref[:, cols]
        g2_ref[partner_rows, :] = partner_g_ref[:, cols]
        prod = grad.astype(jnp.float32) * o_ref[:, cols].astype(jnp.float32)
        high = prod.astype(jnp.bfloat16)
        low = (prod - high.astype(jnp.float32)).astype(jnp.bfloat16)
        dot_ref[:, rows] = (dot_nt(ones, high) + dot_nt(ones, low))[0:1]

    lens = jnp.broadcast_to(len_ref[...].astype(jnp.float32), (64, 64))
    doc = lax.broadcasted_iota(jnp.int32, (64, 64), 0)
    other = lax.broadcasted_iota(jnp.int32, (64, 64), 1)
    starts = jnp.sum(jnp.where(other < doc, lens, 0.0), axis=1, keepdims=True).astype(jnp.int32)
    lane = lax.broadcasted_iota(jnp.int32, (1, DH), 1)
    index = lax.broadcasted_iota(jnp.int32, (ROWS, DH), 0)
    chunks = []
    for steps, cross in zip(STEPS, CROSS):
        source = 1 - core if cross else core
        past = 2 * (chip - jnp.where(source == 0, steps[0], steps[1]))
        chunks += [past + source, past + 1 - source]
    own_bias = []
    for side in range(2):
        mine = chunk if side == 0 else 2 * chip + 1 - core
        here = mine * ROWS + lax.rem(lane, ROWS)
        first = jnp.max(jnp.where(starts <= here, starts, 0), axis=0, keepdims=True)

        def bias_of(key_chunk):
            where = key_chunk * ROWS + index
            return jnp.where((where >= first) & (where <= here), 0.0, NEG)

        for part, key_chunk in enumerate(chunks):
            at = side * PAST + part * ROWS
            bias_ref[at : at + ROWS, :] = bias_of(key_chunk)
        own_bias.append(bias_of(chunk))
    for cols, side, _ in tiles():
        e_ref[:, cols], top_ref[:, cols], sum_ref[:, cols] = scored(
            mine_ref[:, KEY_COLS], q2_ref[cols, :], own_bias[side]
        )


GROUPS = (slice(0, CHIP_ROWS), slice(CHIP_ROWS, PAST))


def score_kernel(q_ref, bias_ref, a_ref, b_ref, own_top_ref, own_sum_ref, e_ref, tops_ref, stats_ref):
    for cols, side, rows in tiles():
        query = q_ref[cols, :]
        tops, sums = [own_top_ref[:, cols]], [own_sum_ref[:, cols]]
        for i, (group, ref) in enumerate(zip(GROUPS, (a_ref, b_ref))):
            bias = bias_ref[side * PAST + group.start : side * PAST + group.stop, :]
            e_ref[group, cols], top, total = scored(ref[:, KEY_COLS], query, bias)
            tops_ref[i : i + 1, cols] = top
            tops.append(top)
            sums.append(total)
        most = functools.reduce(jnp.maximum, tops)
        stats_ref[2 * side : 2 * side + 1, rows] = most
        stats_ref[2 * side + 1 : 2 * side + 2, rows] = sum(
            x * jnp.exp2((top - most) * EXP2_SCALING) for x, top in zip(sums, tops)
        )


def slope_kernel(g_ref, dot_ref, partner_dot_ref, a_ref, b_ref, u_ref):
    for cols, side, rows in tiles():
        grad = g_ref[cols, :]
        row_dot = (dot_ref, partner_dot_ref)[side][:, rows]
        for group, ref in zip(GROUPS, (a_ref, b_ref)):
            u_ref[group, cols] = dot_nt(ref[:, VALUE_COLS], grad) - row_dot


def main_kernel(q_ref, g_ref, e_ref, u_ref, tops_ref, stats_ref, far_ref,
                a_ref, b_ref, ds_ref, norm_ref, p_ref):
    for cols, side, rows in tiles():
        near, far = 2 * side, 2 - 2 * side
        top = stats_ref[near : near + 1, rows]
        far_top = far_ref[far : far + 1, rows]
        most = jnp.maximum(top, far_top)
        total = stats_ref[near + 1 : near + 2, rows] * jnp.exp2(
            (top - most) * EXP2_SCALING
        ) + far_ref[far + 1 : far + 2, rows] * jnp.exp2((far_top - most) * EXP2_SCALING)
        norm_ref[0:1, cols] = most
        norm_ref[1:2, cols] = total
        for i, group in enumerate(GROUPS):
            factor = jnp.exp2((tops_ref[i : i + 1, cols] - most) * EXP2_SCALING) / total
            weights = e_ref[group, cols] * factor
            ds_ref[group, cols] = (weights * u_ref[group, cols]).astype(jnp.bfloat16)
            p_ref[group, cols] = weights.astype(jnp.bfloat16)
    for ref, group in zip((a_ref, b_ref), GROUPS):
        ref[:, KEY_COLS] = (dot_nn(ds_ref[group, :], q_ref[...]) * SCALING).astype(jnp.bfloat16)
        ref[:, VALUE_COLS] = dot_nn(p_ref[group, :], g_ref[...]).astype(jnp.bfloat16)


def finish_kernel(q_ref, g_ref, dot_ref, partner_dot_ref, own_e_ref, own_top_ref, norm_ref, ds_ref,
                  mine_ref, a_ref, b_ref, dq_ref, own_ref, *rest):
    *piece_refs, own_p_ref, own_ds_ref = rest
    past_keys = jnp.concatenate([a_ref[:, KEY_COLS], b_ref[:, KEY_COLS]], axis=0)
    for cols, side, rows in reversed(list(tiles())):
        row_dot = (dot_ref, partner_dot_ref)[side][:, rows]
        slopes = dot_nt(mine_ref[:, VALUE_COLS], g_ref[cols, :]) - row_dot
        factor = jnp.exp2((own_top_ref[:, cols] - norm_ref[0:1, cols]) * EXP2_SCALING)
        weights = own_e_ref[:, cols] * (factor / norm_ref[1:2, cols])
        own_ds = (weights * slopes).astype(jnp.bfloat16)
        own_p_ref[:, cols] = weights.astype(jnp.bfloat16)
        own_ds_ref[:, cols] = own_ds
        grads = (dot_tn(past_keys, ds_ref[:, cols]) + dot_tn(mine_ref[:, KEY_COLS], own_ds)) * SCALING
        for j in range(TILE // DH):
            pair = grads[:, j * DH : (j + 1) * DH].T
            at = rows.start + j * DH
            if side == 0:
                dq_ref[at : at + DH, :] = pair
                continue
            for start, ref in zip(PIECES, piece_refs):
                low, high = max(at, start), min(at + DH, start + ref.shape[0])
                if low < high:
                    ref[low - start : high - start, :] = pair[low - at : high - at].astype(jnp.bfloat16)
    own_ref[:, KEY_COLS] = dot_nn(own_ds_ref[...], q_ref[...]) * SCALING
    own_ref[:, VALUE_COLS] = dot_nn(own_p_ref[...], g_ref[...])


def add_kernel(dq_ref, *refs):
    *piece_refs, sum_ref = refs
    for h in range(HQ):
        total = dq_ref[h * ROWS : (h + 1) * ROWS, :]
        low = h * ROWS
        parts = []
        for start, ref in zip(PIECES, piece_refs):
            first, last = max(low, start), min(low + ROWS, start + ref.shape[0])
            if first < last:
                parts.append(ref[first - start : last - start, :].astype(jnp.float32))
        partner = parts[0] if len(parts) == 1 else jnp.concatenate(parts, axis=0)
        sum_ref[:, h * DH : (h + 1) * DH] = (total + partner).astype(jnp.bfloat16)


def call(kernel, outs, scratch=(), flops=10**9):
    vmem = pl.BlockSpec(memory_space=pltpu.VMEM)
    return lambda *args: pl.pallas_call(
        kernel,
        out_shape=outs,
        in_specs=[vmem] * len(args),
        out_specs=[vmem] * len(outs),
        scratch_shapes=list(scratch),
        compiler_params=pltpu.CompilerParams(vmem_limit_bytes=24 * 1024 * 1024),
        cost_estimate=pl.CostEstimate(flops=flops, bytes_accessed=flops // 500, transcendentals=0),
    )(*args)


def on_device(query_rows, key_rows, value_rows, saved_out, out_grad, doc_lengths):
    shape = jax.ShapeDtypeStruct
    bf16, f32 = jnp.bfloat16, jnp.float32
    together = lax.optimization_barrier
    other = (swap_cores(key_rows), swap_cores(value_rows))
    partner = (swap_cores(query_rows), swap_cores(out_grad))
    mine = jnp.concatenate([key_rows, value_rows], axis=1)
    other, mine = together((other, mine))
    own = call(pack_kernel, [shape((CHIP_ROWS, 2 * DH), bf16)])(mine, *other)[0]
    fetched = [move_chips(own, number, True) for number in range(2)]
    columns = 2 * COLS
    prepared = call(
        prepare_kernel,
        [shape((columns, DH), bf16), shape((columns, DH), bf16), shape((1, COLS), f32),
         shape((2 * PAST, DH), f32), shape((ROWS, columns), f32), shape((1, columns), f32),
         shape((1, columns), f32)],
    )(query_rows, saved_out, out_grad, *partner, doc_lengths.reshape(1, 64), mine)
    far_dot = swap_cores(prepared[2])
    fetched, far_dot, prepared = together((fetched, far_dot, prepared))
    q2, g2, row_dot, bias, own_weights, own_top, own_sum = prepared
    weights, tops, stats = call(
        score_kernel, [shape((PAST, columns), f32), shape((2, columns), f32), shape((4, COLS), f32)]
    )(q2, bias, *fetched, own_top, own_sum)
    far_stats = swap_cores(stats)
    slopes = call(slope_kernel, [shape((PAST, columns), f32)])(g2, row_dot, far_dot, *fetched)[0]
    far_stats, slopes = together((far_stats, slopes))
    part_a, part_b, ds, norm = call(
        main_kernel,
        [shape((CHIP_ROWS, 2 * DH), bf16), shape((CHIP_ROWS, 2 * DH), bf16),
         shape((PAST, columns), bf16), shape((2, columns), f32)],
        [pltpu.VMEM((PAST, columns), bf16)],
    )(q2, g2, weights, slopes, tops, stats, far_stats)
    back = [move_chips(part, number, False) for number, part in enumerate((part_a, part_b))]
    query_grad, own_sums, *pieces = call(
        finish_kernel,
        [shape((COLS, DH), f32), shape((ROWS, 2 * DH), f32)]
        + [shape((high - low, DH), bf16) for low, high in zip(PIECES, PIECES[1:])],
        [pltpu.VMEM((ROWS, columns), bf16)] * 2,
    )(q2, g2, row_dot, far_dot, own_weights, own_top, norm, ds, mine, *fetched)
    pieces = [swap_cores(piece) for piece in pieces]
    totals = back[1].astype(f32) + back[0].astype(f32)
    far_totals = swap_cores(totals[ROWS:].astype(bf16))
    totals, query_grad = together((totals, query_grad))
    query_grad = call(add_kernel, [shape((ROWS, HQ * DH), bf16)])(query_grad, *pieces)[0]
    far_totals, query_grad = together((far_totals, query_grad))
    result = totals[:ROWS] + own_sums + far_totals.astype(f32)
    result = result.astype(bf16)
    return (query_grad, result[:, :DH], result[:, DH:])


def solution(mesh):
    placed = P(AXES, None)
    return jax.shard_map(
        on_device,
        mesh=mesh,
        in_specs=(placed,) * 5 + (P(),),
        out_specs=(placed,) * 3,
        check_vma=False,
    )
```

time: 42.6 us -> 29.6 us (0.69)
  the two profiles are of different devices: /device:TPU:55 before, /device:TPU:39 now
where the time goes in v3:
time: 29.6 us; the launch traced here: 29.3 us
  starting transfers between devices  17.1 us (58%)
  waiting for transfers between devices  5.22 us (18%)
  Pallas kernels  4.78 us (16%)
  between operations  0.8 us (3%)
  other arithmetic  0.77 us (3%)
  local copies, waits for them, and re-layouts  0.64 us (2%)
    ppermute x4, starting transfers between devices, move_chips(): return lax.ppermute(x, AXES, pairs)  14.6 us
    pallas_call x7, Pallas kernels, call(): pl.pallas_call(kernel, out_shape=outs, in_specs=[vmem] * len(args), out_s...  4.78 us
    ppermute x4, waiting for transfers between devices, move_chips(): return lax.ppermute(x, AXES, pairs)  3.01 us
    ppermute x10, starting transfers between devices, swap_cores(): return lax.ppermute(x, 'uly', [(i, i ^ 1) for i in range(16)])  2.49 us
    ppermute x10, waiting for transfers between devices, swap_cores(): return lax.ppermute(x, 'uly', [(i, i ^ 1) for i in range(16)])  2.21 us
    concatenate x1, other arithmetic, on_device(): mine = jnp.concatenate([key_rows, value_rows], axis=1)  0.74 us
    slice x1, local copies, waits for them, and re-layouts, on_device(): return (query_grad, result[:, :DH], result[:, DH:])  0.62 us
  transfers between devices with their start and end apart: 14, of which 7 were waited for; matrix products, arithmetic and copies ran while one was open for 3% of the time, Pallas kernels for 11%

profile of v3, /device:TPU:39, one launch (start us, length us, event | category | flops | bytes accessed | tf_op | source)
XLA Modules:
  0.0 29.3 jit_solution(7108280476935709644)
XLA Ops:
  0.7 0.8 %collective-permute-start.4 = (bf16[64,2048]{1,0:T(8,128)(2,1)}, bf16[64,2048]{1,0:T(8,128)(2,1)S(1)}, u32[]{:S(2)}, u32[]{:S(2)}) collective-permute-start(bf16[64,2048]{1,0:T(8,128)(2,1)} %q_ref.1), channel_id=1, source_target_pairs={{0,1},{1,0},{2,3},{3,2},{4,5},{5,4},{6,7},{7,6},{8,9},{9,8},{10,11... | collective-permute-start | bytes 786440 | tf_op jit(solution)/shard_map/ppermute | solution.py:41
  1.5 0.4 %collective-permute-start = (bf16[64,128]{1,0:T(8,128)(2,1)}, bf16[64,128]{1,0:T(8,128)(2,1)S(1)}, u32[]{:S(2)}, u32[]{:S(2)}) collective-permute-start(bf16[64,128]{1,0:T(8,128)(2,1)} %param.7), channel_id=1, source_target_pairs={{0,1},{1,0},{2,3},{3,2},{4,5},{5,4},{6,7},{7,6},{8,9},{9,8},{10,11... | collective-permute-start | bytes 49160 | tf_op jit(solution)/shard_map/ppermute | solution.py:41
  2.0 0.7 %pad_maximum_fusion.mine_ref = bf16[64,256]{1,0:T(8,128)(2,1)S(1)} fusion(bf16[64,128]{1,0:T(8,128)(2,1)} %param.8, bf16[64,128]{1,0:T(8,128)(2,1)} %param.7), kind=kLoop, calls=%fused_computation.3 | loop fusion | flops 65536 | bytes 65536 | tf_op jit(solution)/shard_map/concatenate | solution.py:260
  2.8 0.4 %collective-permute-done.other_k_ref = bf16[64,128]{1,0:T(8,128)(2,1)S(1)} collective-permute-done((bf16[64,128]{1,0:T(8,128)(2,1)}, bf16[64,128]{1,0:T(8,128)(2,1)S(1)}, u32[]{:S(2)}, u32[]{:S(2)}) %collective-permute-start) | collective-permute-done | bytes 16416 | tf_op jit(solution)/shard_map/ppermute | solution.py:41
  3.2 0.1 collective-permute-done.1.other_v_ref
  3.4 3.0 %collective-permute-start.3 = (bf16[128,256]{1,0:T(8,128)(2,1)S(1)}, bf16[128,256]{1,0:T(8,128)(2,1)S(1)}, u32[]{:S(2)}, u32[]{:S(2)}) collective-permute-start(bf16[128,256]{1,0:T(8,128)(2,1)S(1)} %shard_map.85), channel_id=1, source_target_pairs={{0,5},{1,6},{2,7},{3,16},{4,17},{5,18},{6,19},{7,20},{16,21},{17,2... | collective-permute-start | bytes 196616 | tf_op jit(solution)/shard_map/ppermute | solution.py:52
  6.3 5.7 %collective-permute-start.2 = (bf16[128,256]{1,0:T(8,128)(2,1)S(1)}, bf16[128,256]{1,0:T(8,128)(2,1)S(1)}, u32[]{:S(2)}, u32[]{:S(2)}) collective-permute-start(bf16[128,256]{1,0:T(8,128)(2,1)S(1)} %shard_map.85), channel_id=1, source_target_pairs={{0,3},{1,16},{2,5},{3,18},{4,7},{5,20},{6,17},{7,22},{16,19},{17,3... | collective-permute-start | bytes 196616 | tf_op jit(solution)/shard_map/ppermute | solution.py:52
  12.1 0.7 %shard_map.86 = (bf16[2048,128]{1,0:T(8,128)(2,1)S(1)}, bf16[2048,128]{1,0:T(8,128)(2,1)S(1)}, f32[1,1024]{1,0:T(1,128)S(1)}, f32[512,128]{1,0:T(8,128)S(1)}, f3...) custom-call(bf16[64,2048]{1,0:T(8,128)(2,1)S(1)} %copy-done, bf16[64,2048]{1,0:T(8,128)(2,1)S(1)} %copy-done.1, ...), custom_call_target="tpu_custom_call" | custom-call | flops 1000000000 | bytes 2000000 | tf_op jit(solution)/shard_map/pallas_call | solution.py:243
  12.8 0.5 %collective-permute-done.2.a_ref = bf16[128,256]{1,0:T(8,128)(2,1)S(1)} collective-permute-done((bf16[128,256]{1,0:T(8,128)(2,1)S(1)}, bf16[128,256]{1,0:T(8,128)(2,1)S(1)}, u32[]{:S(2)}, u32[]{:S(2)}) %collective-permute-start.2) | collective-permute-done | bytes 65568 | tf_op jit(solution)/shard_map/ppermute | solution.py:52
  13.3 0.6 %collective-permute-done.6.partner_dot_ref = f32[1,1024]{1,0:T(1,128)S(1)} collective-permute-done((f32[1,1024]{1,0:T(1,128)S(1)}, f32[1,1024]{1,0:T(1,128)S(1)}, u32[]{:S(2)}, u32[]{:S(2)}) %collective-permute-start.6) | collective-permute-done | bytes 4128 | tf_op jit(solution)/shard_map/ppermute | solution.py:41
  14.0 0.8 %shard_map.87 = (f32[256,2048]{1,0:T(8,128)S(1)}, f32[2,2048]{1,0:T(2,128)S(1)}, f32[4,1024]{1,0:T(4,128)S(1)}) custom-call(bf16[2048,128]{1,0:T(8,128)(2,1)S(1)} %get-tuple-element.51.q_ref, f32[512,128]{1,0:T(8,128)S(1)} %get-tuple-element.53.bias_ref, bf16[128,256]{1,0:T(8,128)(2,1)S(1)} %collective-permute-done.2.a_ref, ...), custom_call_target="tpu_custom_call" | custom-call | flops 1000000000 | bytes 2000000 | tf_op jit(solution)/shard_map/pallas_call | solution.py:243
  14.8 0.2 collective-permute-start.7
  15.1 0.4 %shard_map.88.u_ref = f32[256,2048]{1,0:T(8,128)S(1)} custom-call(bf16[2048,128]{1,0:T(8,128)(2,1)S(1)} %get-tuple-element.52.g_ref, f32[1,1024]{1,0:T(1,128)S(1)} %get-tuple-element.60.dot_ref, f32[1,1024]{1,0:T(1,128)S(1)} %collective-permute-done.6.partner_dot_ref, bf16[128,256]{1,0:T(8,128)(2,1)S(1)} %collective-permute-done.2.a_ref, ...), custom_call_target="tpu_custom_call" | custom-call | flops 1000000000 | bytes 2000000 | tf_op jit(solution)/shard_map/pallas_call | solution.py:243
  15.5 0.6 %collective-permute-done.7.far_ref = f32[4,1024]{1,0:T(4,128)S(1)} collective-permute-done((f32[4,1024]{1,0:T(4,128)S(1)}, f32[4,1024]{1,0:T(4,128)S(1)}, u32[]{:S(2)}, u32[]{:S(2)}) %collective-permute-start.7) | collective-permute-done | bytes 16416 | tf_op jit(solution)/shard_map/ppermute | solution.py:41
  16.1 0.9 %shard_map.89 = (bf16[128,256]{1,0:T(8,128)(2,1)S(1)}, bf16[128,256]{1,0:T(8,128)(2,1)S(1)}, bf16[256,2048]{1,0:T(8,128)(2,1)S(1)}, f32[2,2048]{1,0:T(2,128)S(1)}) custom-call(bf16[2048,128]{1,0:T(8,128)(2,1)S(1)} %get-tuple-element.51.q_ref, bf16[2048,128]{1,0:T(8,128)(2,1)S(1)} %get-tuple-element.52.g_ref, f32[256,2048]{1,0:T(8,128)S(1)} %get-tuple-element.58.e_ref, ...), custom_call_target="tpu_custom_call" | custom-call | flops 1000000000 | bytes 2000000 | tf_op jit(solution)/shard_map/pallas_call | solution.py:243
  17.0 2.4 %collective-permute-start.8 = (bf16[128,256]{1,0:T(8,128)(2,1)S(1)}, bf16[128,256]{1,0:T(8,128)(2,1)S(1)}, u32[]{:S(2)}, u32[]{:S(2)}) collective-permute-start(bf16[128,256]{1,0:T(8,128)(2,1)S(1)} %get-tuple-element.65), channel_id=1, source_target_pairs={{5,0},{6,1},{7,2},{16,3},{17,4},{18,5},{19,6},{20,7},{21,16},{22,1... | collective-permute-start | bytes 196616 | tf_op jit(solution)/shard_map/ppermute | solution.py:52
  19.3 3.6 %collective-permute-start.9 = (bf16[128,256]{1,0:T(8,128)(2,1)S(1)}, bf16[128,256]{1,0:T(8,128)(2,1)S(1)}, u32[]{:S(2)}, u32[]{:S(2)}) collective-permute-start(bf16[128,256]{1,0:T(8,128)(2,1)S(1)} %get-tuple-element.66), channel_id=1, source_target_pairs={{3,0},{16,1},{5,2},{18,3},{7,4},{20,5},{17,6},{22,7},{19,16},{32,1... | collective-permute-start | bytes 196616 | tf_op jit(solution)/shard_map/ppermute | solution.py:52
  22.9 1.2 %shard_map.90 = (f32[1024,128]{1,0:T(8,128)S(1)}, f32[64,256]{1,0:T(8,128)S(1)}, bf16[352,128]{1,0:T(8,128)(2,1)S(1)}, bf16[352,128]{1,0:T(8,128)(2,1)S(1)}, bf16[320,128]{1,0:T(8,128)(2,1)S(1)}) custom-call(bf16[2048,128]{1,0:T(8,128)(2,1)S(1)} %get-tuple-element.51.q_ref, bf16[2048,128]{1,0:T(8,128)(2,1)S(1)} %get-tuple-element.52.g_ref, ...), custom_call_target="tpu_custom_call" | custom-call | flops 1000000000 | bytes 2000000 | tf_op jit(solution)/shard_map/pallas_call | solution.py:243
  24.2 0.5 %collective-permute-start.11 = (bf16[352,128]{1,0:T(8,128)(2,1)S(1)}, bf16[352,128]{1,0:T(8,128)(2,1)S(1)}, u32[]{:S(2)}, u32[]{:S(2)}) collective-permute-start(bf16[352,128]{1,0:T(8,128)(2,1)S(1)} %get-tuple-element.72), channel_id=1, source_target_pairs={{0,1},{1,0},{2,3},{3,2},{4,5},{5,4},{6,7},{7,6},{8,9},{9,8},{10,11... | collective-permute-start | bytes 270344 | tf_op jit(solution)/shard_map/ppermute | solution.py:41
  24.7 0.1 collective-permute-start.12
  24.8 2.5 %collective-permute-done.9 = bf16[128,256]{1,0:T(8,128)(2,1)S(1)} collective-permute-done((bf16[128,256]{1,0:T(8,128)(2,1)S(1)}, bf16[128,256]{1,0:T(8,128)(2,1)S(1)}, u32[]{:S(2)}, u32[]{:S(2)}) %collective-permute-start.9) | collective-permute-done | bytes 65568 | tf_op jit(solution)/shard_map/ppermute | solution.py:52
  27.5 0.8 %shard_map.91 = bf16[64,2048]{1,0:T(8,128)(2,1)} custom-call(f32[1024,128]{1,0:T(8,128)S(1)} %get-tuple-element.71.dq_ref, bf16[352,128]{1,0:T(8,128)(2,1)S(1)} %collective-permute-done.11.refs_0_, bf16[352,128]{1,0:T(8,128)(2,1)S(1)} %collective-permute-done.12.refs_1_, bf16[320,128]{1,0:T(8,128)(2,1)S(1)} %collective-permute-done.13.refs_2_), custom_call_target="tpu_custom_call" | custom-call | flops 1000000000 | bytes 2000000 | tf_op jit(solution)/shard_map/pallas_call | solution.py:243
  28.3 0.4 %collective-permute-done.10 = bf16[64,256]{1,0:T(8,128)(2,1)S(1)} collective-permute-done((bf16[64,256]{1,0:T(8,128)(2,1)S(1)}, bf16[64,256]{1,0:T(8,128)(2,1)S(1)}, u32[]{:S(2)}, u32[]{:S(2)}) %collective-permute-start.10) | collective-permute-done | bytes 32800 | tf_op jit(solution)/shard_map/ppermute | solution.py:41
  28.7 0.6 %fusion = (bf16[64,128]{1,0:T(8,128)(2,1)}, bf16[64,128]{1,0:T(8,128)(2,1)}) fusion(bf16[64,256]{1,0:T(8,128)(2,1)S(1)} %add_convert_fusion), kind=kLoop, calls=%fused_computation.4 | loop fusion | bytes 65536 | tf_op jit(solution)/shard_map/slice | solution.py:301
  (24 shorter events, 0.6 us)
Async XLA Ops:
  0.6 11.4 %copy-start = (bf16[64,2048]{1,0:T(8,128)(2,1)S(1)}, bf16[64,2048]{1,0:T(8,128)(2,1)}, u32[]{:S(2)}) copy-start(bf16[64,2048]{1,0:T(8,128)(2,1)} %q_ref.1) | copy-start | bytes 786436
  0.6 11.4 %copy-start.2 = (bf16[64,2048]{1,0:T(8,128)(2,1)S(1)}, bf16[64,2048]{1,0:T(8,128)(2,1)}, u32[]{:S(2)}) copy-start(bf16[64,2048]{1,0:T(8,128)(2,1)} %g_ref.1) | copy-start | bytes 786436
  0.7 11.4 %copy-start.3 = (s32[64]{0:T(128)S(1)}, s32[64]{0:T(128)}, u32[]{:S(2)}) copy-start(s32[64]{0:T(128)} %param.11) | copy-start | bytes 772
  0.7 11.4 %copy-start.1 = (bf16[64,2048]{1,0:T(8,128)(2,1)S(1)}, bf16[64,2048]{1,0:T(8,128)(2,1)}, u32[]{:S(2)}) copy-start(bf16[64,2048]{1,0:T(8,128)(2,1)} %o_ref.1) | copy-start | bytes 786436
  0.7 11.3 %collective-permute-start.4 = (bf16[64,2048]{1,0:T(8,128)(2,1)}, bf16[64,2048]{1,0:T(8,128)(2,1)S(1)}, u32[]{:S(2)}, u32[]{:S(2)}) collective-permute-start(bf16[64,2048]{1,0:T(8,128)(2,1)} %q_ref.1), channel_id=1, source_target_pairs={{0,1},{1,0},{2,3},{3,2},{4,5},{5,4},{6,7},{7,6},{8,9},{9,8},{10,11... | collective-permute-start | bytes 786440 | tf_op jit(solution)/shard_map/ppermute | solution.py:41
  1.4 10.6 %collective-permute-start.5 = (bf16[64,2048]{1,0:T(8,128)(2,1)}, bf16[64,2048]{1,0:T(8,128)(2,1)S(1)}, u32[]{:S(2)}, u32[]{:S(2)}) collective-permute-start(bf16[64,2048]{1,0:T(8,128)(2,1)} %g_ref.1), channel_id=1, source_target_pairs={{0,1},{1,0},{2,3},{3,2},{4,5},{5,4},{6,7},{7,6},{8,9},{9,8},{10,11... | collective-permute-start | bytes 786440 | tf_op jit(solution)/shard_map/ppermute | solution.py:41
  1.5 1.7 %collective-permute-start = (bf16[64,128]{1,0:T(8,128)(2,1)}, bf16[64,128]{1,0:T(8,128)(2,1)S(1)}, u32[]{:S(2)}, u32[]{:S(2)}) collective-permute-start(bf16[64,128]{1,0:T(8,128)(2,1)} %param.7), channel_id=1, source_target_pairs={{0,1},{1,0},{2,3},{3,2},{4,5},{5,4},{6,7},{7,6},{8,9},{9,8},{10,11... | collective-permute-start | bytes 49160 | tf_op jit(solution)/shard_map/ppermute | solution.py:41
  1.9 1.4 %collective-permute-start.1 = (bf16[64,128]{1,0:T(8,128)(2,1)}, bf16[64,128]{1,0:T(8,128)(2,1)S(1)}, u32[]{:S(2)}, u32[]{:S(2)}) collective-permute-start(bf16[64,128]{1,0:T(8,128)(2,1)} %param.8), channel_id=1, source_target_pairs={{0,1},{1,0},{2,3},{3,2},{4,5},{5,4},{6,7},{7,6},{8,9},{9,8},{10,11... | collective-permute-start | bytes 49160 | tf_op jit(solution)/shard_map/ppermute | solution.py:41
  3.4 9.5 %collective-permute-start.3 = (bf16[128,256]{1,0:T(8,128)(2,1)S(1)}, bf16[128,256]{1,0:T(8,128)(2,1)S(1)}, u32[]{:S(2)}, u32[]{:S(2)}) collective-permute-start(bf16[128,256]{1,0:T(8,128)(2,1)S(1)} %shard_map.85), channel_id=1, source_target_pairs={{0,5},{1,6},{2,7},{3,16},{4,17},{5,18},{6,19},{7,20},{16,21},{17,2... | collective-permute-start | bytes 196616 | tf_op jit(solution)/shard_map/ppermute | solution.py:52
  6.3 7.0 %collective-permute-start.2 = (bf16[128,256]{1,0:T(8,128)(2,1)S(1)}, bf16[128,256]{1,0:T(8,128)(2,1)S(1)}, u32[]{:S(2)}, u32[]{:S(2)}) collective-permute-start(bf16[128,256]{1,0:T(8,128)(2,1)S(1)} %shard_map.85), channel_id=1, source_target_pairs={{0,3},{1,16},{2,5},{3,18},{4,7},{5,20},{6,17},{7,22},{16,19},{17,3... | collective-permute-start | bytes 196616 | tf_op jit(solution)/shard_map/ppermute | solution.py:52
  12.7 1.3 %collective-permute-start.6 = (f32[1,1024]{1,0:T(1,128)S(1)}, f32[1,1024]{1,0:T(1,128)S(1)}, u32[]{:S(2)}, u32[]{:S(2)}) collective-permute-start(f32[1,1024]{1,0:T(1,128)S(1)} %get-tuple-element.60.dot_ref), channel_id=1, source_target_pairs={{0,1},{1,0},{2,3},{3,2},{4,5},{5,4},{6,7},{7,6},{8,9},{9,8},{10,11... | collective-permute-start | bytes 12296 | tf_op jit(solution)/shard_map/ppermute | solution.py:41
  14.8 1.3 %collective-permute-start.7 = (f32[4,1024]{1,0:T(4,128)S(1)}, f32[4,1024]{1,0:T(4,128)S(1)}, u32[]{:S(2)}, u32[]{:S(2)}) collective-permute-start(f32[4,1024]{1,0:T(4,128)S(1)} %get-tuple-element.59.stats_ref), channel_id=1, source_target_pairs={{0,1},{1,0},{2,3},{3,2},{4,5},{5,4},{6,7},{7,6},{8,9},{9,8},{10,11... | collective-permute-start | bytes 49160 | tf_op jit(solution)/shard_map/ppermute | solution.py:41
  17.0 7.9 %collective-permute-start.8 = (bf16[128,256]{1,0:T(8,128)(2,1)S(1)}, bf16[128,256]{1,0:T(8,128)(2,1)S(1)}, u32[]{:S(2)}, u32[]{:S(2)}) collective-permute-start(bf16[128,256]{1,0:T(8,128)(2,1)S(1)} %get-tuple-element.65), channel_id=1, source_target_pairs={{5,0},{6,1},{7,2},{16,3},{17,4},{18,5},{19,6},{20,7},{21,16},{22,1... | collective-permute-start | bytes 196616 | tf_op jit(solution)/shard_map/ppermute | solution.py:52
  19.3 8.0 %collective-permute-start.9 = (bf16[128,256]{1,0:T(8,128)(2,1)S(1)}, bf16[128,256]{1,0:T(8,128)(2,1)S(1)}, u32[]{:S(2)}, u32[]{:S(2)}) collective-permute-start(bf16[128,256]{1,0:T(8,128)(2,1)S(1)} %get-tuple-element.66), channel_id=1, source_target_pairs={{3,0},{16,1},{5,2},{18,3},{7,4},{20,5},{17,6},{22,7},{19,16},{32,1... | collective-permute-start | bytes 196616 | tf_op jit(solution)/shard_map/ppermute | solution.py:52
  24.1 3.3 %collective-permute-start.13 = (bf16[320,128]{1,0:T(8,128)(2,1)S(1)}, bf16[320,128]{1,0:T(8,128)(2,1)S(1)}, u32[]{:S(2)}, u32[]{:S(2)}) collective-permute-start(bf16[320,128]{1,0:T(8,128)(2,1)S(1)} %get-tuple-element.74), channel_id=1, source_target_pairs={{0,1},{1,0},{2,3},{3,2},{4,5},{5,4},{6,7},{7,6},{8,9},{9,8},{10,11... | collective-permute-start | bytes 245768 | tf_op jit(solution)/shard_map/ppermute | solution.py:41
  24.2 3.3 %collective-permute-start.11 = (bf16[352,128]{1,0:T(8,128)(2,1)S(1)}, bf16[352,128]{1,0:T(8,128)(2,1)S(1)}, u32[]{:S(2)}, u32[]{:S(2)}) collective-permute-start(bf16[352,128]{1,0:T(8,128)(2,1)S(1)} %get-tuple-element.72), channel_id=1, source_target_pairs={{0,1},{1,0},{2,3},{3,2},{4,5},{5,4},{6,7},{7,6},{8,9},{9,8},{10,11... | collective-permute-start | bytes 270344 | tf_op jit(solution)/shard_map/ppermute | solution.py:41
  24.7 2.8 %collective-permute-start.12 = (bf16[352,128]{1,0:T(8,128)(2,1)S(1)}, bf16[352,128]{1,0:T(8,128)(2,1)S(1)}, u32[]{:S(2)}, u32[]{:S(2)}) collective-permute-start(bf16[352,128]{1,0:T(8,128)(2,1)S(1)} %get-tuple-element.73), channel_id=1, source_target_pairs={{0,1},{1,0},{2,3},{3,2},{4,5},{5,4},{6,7},{7,6},{8,9},{9,8},{10,11... | collective-permute-start | bytes 270344 | tf_op jit(solution)/shard_map/ppermute | solution.py:41
  27.4 1.3 %collective-permute-start.10 = (bf16[64,256]{1,0:T(8,128)(2,1)S(1)}, bf16[64,256]{1,0:T(8,128)(2,1)S(1)}, u32[]{:S(2)}, u32[]{:S(2)}) collective-permute-start(bf16[64,256]{1,0:T(8,128)(2,1)S(1)} %slice.22), channel_id=1, source_target_pairs={{0,1},{1,0},{2,3},{3,2},{4,5},{5,4},{6,7},{7,6},{8,9},{9,8},{10,11... | collective-permute-start | bytes 98312 | tf_op jit(solution)/shard_map/ppermute | solution.py:41

commit v4 on v3

--- a/solution.py
+++ b/solution.py
@@ -84,14 +84,19 @@
         yield slice(tile * TILE, (tile + 1) * TILE), side, slice(at * TILE, (at + 1) * TILE)
 
 
-def scored(keys, query, bias):
-    scores = dot_nt(keys, query) + jnp.concatenate([bias, bias], axis=1)
+def query_tile(queries, side):
+    row = lax.rem(lax.broadcasted_iota(jnp.int32, (TILE, DH), 0), ROWS) + side * ROWS
+    lane = lax.broadcasted_iota(jnp.int32, (TILE, DH), 1)
+    return jnp.concatenate([queries, (row == lane).astype(jnp.bfloat16)], axis=1)
+
+
+def scored(scores):
     top = jnp.max(folded(scores, jnp.max), axis=0, keepdims=True)
     weights = jnp.exp2((scores - top) * EXP2_SCALING)
     return weights, top, jnp.sum(folded(weights, jnp.sum), axis=0, keepdims=True)
 
 
-def prepare_kernel(q_ref, o_ref, g_ref, partner_q_ref, partner_g_ref, len_ref, mine_ref,
+def prepare_kernel(q_ref, o_ref, g_ref, len_ref, own_ref,
                    q2_ref, g2_ref, dot_ref, bias_ref, e_ref, top_ref, sum_ref):
     blk = lax.axis_index("blk")
     uly = lax.axis_index("uly")
@@ -108,9 +113,6 @@
         grad = g_ref[:, cols]
         q2_ref[rows, :] = q_ref[:, cols]
         g2_ref[rows, :] = grad
-        partner_rows = slice(COLS + h * ROWS, COLS + (h + 1) * ROWS)
-        q2_ref[partner_rows, :] = partner_q_ref[:, cols]
-        g2_ref[partner_rows, :] = partner_g_ref[:, cols]
         prod = grad.astype(jnp.float32) * o_ref[:, cols].astype(jnp.float32)
         high = prod.astype(jnp.bfloat16)
         low = (prod - high.astype(jnp.float32)).astype(jnp.bfloat16)
@@ -121,45 +123,49 @@
     other = lax.broadcasted_iota(jnp.int32, (64, 64), 1)
     starts = jnp.sum(jnp.where(other < doc, lens, 0.0), axis=1, keepdims=True).astype(jnp.int32)
     lane = lax.broadcasted_iota(jnp.int32, (1, DH), 1)
+    here = jnp.where(lane < ROWS, chunk, 2 * chip + 1 - core) * ROWS + lax.rem(lane, ROWS)
+    first = jnp.max(jnp.where(starts <= here, starts, 0), axis=0, keepdims=True)
     index = lax.broadcasted_iota(jnp.int32, (ROWS, DH), 0)
     chunks = []
     for steps, cross in zip(STEPS, CROSS):
         source = 1 - core if cross else core
         past = 2 * (chip - jnp.where(source == 0, steps[0], steps[1]))
         chunks += [past + source, past + 1 - source]
-    own_bias = []
-    for side in range(2):
-        mine = chunk if side == 0 else 2 * chip + 1 - core
-        here = mine * ROWS + lax.rem(lane, ROWS)
-        first = jnp.max(jnp.where(starts <= here, starts, 0), axis=0, keepdims=True)
-
-        def bias_of(key_chunk):
-            where = key_chunk * ROWS + index
-            return jnp.where((where >= first) & (where <= here), 0.0, NEG)
-
-        for part, key_chunk in enumerate(chunks):
-            at = side * PAST + part * ROWS
-            bias_ref[at : at + ROWS, :] = bias_of(key_chunk)
-        own_bias.append(bias_of(chunk))
-    for cols, side, _ in tiles():
+    for part, key_chunk in enumerate(chunks + [chunk, 2 * chip + 1 - core]):
+        where = key_chunk * ROWS + index
+        bias = jnp.where((where >= first) & (where <= here), 0.0, NEG).astype(jnp.bfloat16)
+        bias_ref[part * ROWS : (part + 1) * ROWS, :] = bias
+    keys = jnp.concatenate([own_ref[:, KEY_COLS], bias_ref[PAST:, :]], axis=1)
+    for tile in range(TILES):
+        cols = slice(tile * TILE, (tile + 1) * TILE)
         e_ref[:, cols], top_ref[:, cols], sum_ref[:, cols] = scored(
-            mine_ref[:, KEY_COLS], q2_ref[cols, :], own_bias[side]
+            dot_nt(keys, query_tile(q2_ref[cols, :], 0))
         )
 
 
+def keys_kernel(a_ref, b_ref, bias_ref, keys_ref):
+    for ref, group in zip((a_ref, b_ref), GROUPS):
+        keys_ref[group, :DH] = ref[:, KEY_COLS]
+    keys_ref[:, DH:] = bias_ref[:PAST, :]
+
+
 GROUPS = (slice(0, CHIP_ROWS), slice(CHIP_ROWS, PAST))
 
 
-def score_kernel(q_ref, bias_ref, a_ref, b_ref, own_top_ref, own_sum_ref, e_ref, tops_ref, stats_ref):
+def score_kernel(q_ref, partner_q_ref, keys_ref, own_top_ref, own_sum_ref,
+                 e_ref, tops_ref, stats_ref):
     for cols, side, rows in tiles():
-        query = q_ref[cols, :]
-        tops, sums = [own_top_ref[:, cols]], [own_sum_ref[:, cols]]
-        for i, (group, ref) in enumerate(zip(GROUPS, (a_ref, b_ref))):
-            bias = bias_ref[side * PAST + group.start : side * PAST + group.stop, :]
-            e_ref[group, cols], top, total = scored(ref[:, KEY_COLS], query, bias)
+        query = query_tile((q_ref, partner_q_ref)[side][rows, :], side)
+        scores = dot_nt(keys_ref[...], query)
+        tops, sums = [], []
+        for i, group in enumerate(GROUPS):
+            e_ref[group, cols], top, total = scored(scores[group])
             tops_ref[i : i + 1, cols] = top
             tops.append(top)
             sums.append(total)
+        if side == 0:
+            tops.append(own_top_ref[:, rows])
+            sums.append(own_sum_ref[:, rows])
         most = functools.reduce(jnp.maximum, tops)
         stats_ref[2 * side : 2 * side + 1, rows] = most
         stats_ref[2 * side + 1 : 2 * side + 2, rows] = sum(
@@ -167,15 +173,18 @@
         )
 
 
-def slope_kernel(g_ref, dot_ref, partner_dot_ref, a_ref, b_ref, u_ref):
+def slope_kernel(g_ref, partner_g_ref, dot_ref, partner_dot_ref, a_ref, b_ref, u_ref):
+    values = jnp.concatenate([a_ref[:, VALUE_COLS], b_ref[:, VALUE_COLS]], axis=0)
     for cols, side, rows in tiles():
-        grad = g_ref[cols, :]
-        row_dot = (dot_ref, partner_dot_ref)[side][:, rows]
-        for group, ref in zip(GROUPS, (a_ref, b_ref)):
-            u_ref[group, cols] = dot_nt(ref[:, VALUE_COLS], grad) - row_dot
-
-
-def main_kernel(q_ref, g_ref, e_ref, u_ref, tops_ref, stats_ref, far_ref,
+        grad = (g_ref, partner_g_ref)[side][rows, :]
+        u_ref[:, cols] = dot_nt(values, grad) - (dot_ref, partner_dot_ref)[side][:, rows]
+
+
+def dot_sides(left_ref, own_ref, partner_ref):
+    return dot_nn(left_ref[:, :COLS], own_ref[...]) + dot_nn(left_ref[:, COLS:], partner_ref[...])
+
+
+def main_kernel(q_ref, partner_q_ref, g_ref, partner_g_ref, e_ref, u_ref, tops_ref, stats_ref, far_ref,
                 a_ref, b_ref, ds_ref, norm_ref, p_ref):
     for cols, side, rows in tiles():
         near, far = 2 * side, 2 - 2 * side
@@ -192,24 +201,28 @@
             weights = e_ref[group, cols] * factor
             ds_ref[group, cols] = (weights * u_ref[group, cols]).astype(jnp.bfloat16)
             p_ref[group, cols] = weights.astype(jnp.bfloat16)
+    key_grads = (dot_sides(ds_ref, q_ref, partner_q_ref) * SCALING).astype(jnp.bfloat16)
+    value_grads = dot_sides(p_ref, g_ref, partner_g_ref).astype(jnp.bfloat16)
     for ref, group in zip((a_ref, b_ref), GROUPS):
-        ref[:, KEY_COLS] = (dot_nn(ds_ref[group, :], q_ref[...]) * SCALING).astype(jnp.bfloat16)
-        ref[:, VALUE_COLS] = dot_nn(p_ref[group, :], g_ref[...]).astype(jnp.bfloat16)
-
-
-def finish_kernel(q_ref, g_ref, dot_ref, partner_dot_ref, own_e_ref, own_top_ref, norm_ref, ds_ref,
-                  mine_ref, a_ref, b_ref, dq_ref, own_ref, *rest):
+        ref[:, KEY_COLS] = key_grads[group]
+        ref[:, VALUE_COLS] = value_grads[group]
+
+
+def finish_kernel(q_ref, g_ref, dot_ref, own_e_ref, own_top_ref, norm_ref, ds_ref, own_ref, a_ref, b_ref,
+                  dq_ref, own_sum_ref, *rest):
     *piece_refs, own_p_ref, own_ds_ref = rest
     past_keys = jnp.concatenate([a_ref[:, KEY_COLS], b_ref[:, KEY_COLS]], axis=0)
     for cols, side, rows in reversed(list(tiles())):
-        row_dot = (dot_ref, partner_dot_ref)[side][:, rows]
-        slopes = dot_nt(mine_ref[:, VALUE_COLS], g_ref[cols, :]) - row_dot
-        factor = jnp.exp2((own_top_ref[:, cols] - norm_ref[0:1, cols]) * EXP2_SCALING)
-        weights = own_e_ref[:, cols] * (factor / norm_ref[1:2, cols])
-        own_ds = (weights * slopes).astype(jnp.bfloat16)
-        own_p_ref[:, cols] = weights.astype(jnp.bfloat16)
-        own_ds_ref[:, cols] = own_ds
-        grads = (dot_tn(past_keys, ds_ref[:, cols]) + dot_tn(mine_ref[:, KEY_COLS], own_ds)) * SCALING
+        grads = dot_tn(past_keys, ds_ref[:, cols])
+        if side == 0:
+            slopes = dot_nt(own_ref[:, VALUE_COLS], g_ref[rows, :]) - dot_ref[:, rows]
+            factor = jnp.exp2((own_top_ref[:, rows] - norm_ref[0:1, rows]) * EXP2_SCALING)
+            weights = own_e_ref[:, rows] * (factor / norm_ref[1:2, rows])
+            own_ds = (weights * slopes).astype(jnp.bfloat16)
+            own_p_ref[:, rows] = weights.astype(jnp.bfloat16)
+            own_ds_ref[:, rows] = own_ds
+            grads = grads + dot_tn(own_ref[:, KEY_COLS], own_ds)
+        grads = grads * SCALING
         for j in range(TILE // DH):
             pair = grads[:, j * DH : (j + 1) * DH].T
             at = rows.start + j * DH
@@ -220,8 +233,8 @@
                 low, high = max(at, start), min(at + DH, start + ref.shape[0])
                 if low < high:
                     ref[low - start : high - start, :] = pair[low - at : high - at].astype(jnp.bfloat16)
-    own_ref[:, KEY_COLS] = dot_nn(own_ds_ref[...], q_ref[...]) * SCALING
-    own_ref[:, VALUE_COLS] = dot_nn(own_p_ref[...], g_ref[...])
+    own_sum_ref[:, KEY_COLS] = dot_nn(own_ds_ref[...], q_ref[...]) * SCALING
+    own_sum_ref[:, VALUE_COLS] = dot_nn(own_p_ref[...], g_ref[...])
 
 
 def add_kernel(dq_ref, *refs):
@@ -256,47 +269,47 @@
     bf16, f32 = jnp.bfloat16, jnp.float32
     together = lax.optimization_barrier
     other = (swap_cores(key_rows), swap_cores(value_rows))
-    partner = (swap_cores(query_rows), swap_cores(out_grad))
     mine = jnp.concatenate([key_rows, value_rows], axis=1)
     other, mine = together((other, mine))
     own = call(pack_kernel, [shape((CHIP_ROWS, 2 * DH), bf16)])(mine, *other)[0]
     fetched = [move_chips(own, number, True) for number in range(2)]
     columns = 2 * COLS
-    prepared = call(
+    q2, g2, row_dot, bias, own_weights, own_top, own_sum = call(
         prepare_kernel,
-        [shape((columns, DH), bf16), shape((columns, DH), bf16), shape((1, COLS), f32),
-         shape((2 * PAST, DH), f32), shape((ROWS, columns), f32), shape((1, columns), f32),
-         shape((1, columns), f32)],
-    )(query_rows, saved_out, out_grad, *partner, doc_lengths.reshape(1, 64), mine)
-    far_dot = swap_cores(prepared[2])
-    fetched, far_dot, prepared = together((fetched, far_dot, prepared))
-    q2, g2, row_dot, bias, own_weights, own_top, own_sum = prepared
+        [shape((COLS, DH), bf16), shape((COLS, DH), bf16), shape((1, COLS), f32),
+         shape((PAST + CHIP_ROWS, DH), bf16), shape((CHIP_ROWS, COLS), f32), shape((1, COLS), f32),
+         shape((1, COLS), f32)],
+    )(query_rows, saved_out, out_grad, doc_lengths.reshape(1, 64), own)
+    keys = call(keys_kernel, [shape((PAST, 2 * DH), bf16)], flops=3 * 10**9)(*fetched, bias)[0]
+    q3, g3, far_dot = (swap_cores(x) for x in (q2, g2, row_dot))
     weights, tops, stats = call(
         score_kernel, [shape((PAST, columns), f32), shape((2, columns), f32), shape((4, COLS), f32)]
-    )(q2, bias, *fetched, own_top, own_sum)
+    )(q2, q3, keys, own_top, own_sum)
     far_stats = swap_cores(stats)
-    slopes = call(slope_kernel, [shape((PAST, columns), f32)])(g2, row_dot, far_dot, *fetched)[0]
+    slopes = call(slope_kernel, [shape((PAST, columns), f32)])(
+        g2, g3, row_dot, far_dot, *fetched
+    )[0]
     far_stats, slopes = together((far_stats, slopes))
     part_a, part_b, ds, norm = call(
         main_kernel,
         [shape((CHIP_ROWS, 2 * DH), bf16), shape((CHIP_ROWS, 2 * DH), bf16),
          shape((PAST, columns), bf16), shape((2, columns), f32)],
         [pltpu.VMEM((PAST, columns), bf16)],
-    )(q2, g2, weights, slopes, tops, stats, far_stats)
+    )(q2, q3, g2, g3, weights, slopes, tops, stats, far_stats)
     back = [move_chips(part, number, False) for number, part in enumerate((part_a, part_b))]
     query_grad, own_sums, *pieces = call(
         finish_kernel,
-        [shape((COLS, DH), f32), shape((ROWS, 2 * DH), f32)]
+        [shape((COLS, DH), f32), shape((CHIP_ROWS, 2 * DH), f32)]
         + [shape((high - low, DH), bf16) for low, high in zip(PIECES, PIECES[1:])],
-        [pltpu.VMEM((ROWS, columns), bf16)] * 2,
-    )(q2, g2, row_dot, far_dot, own_weights, own_top, norm, ds, mine, *fetched)
+        [pltpu.VMEM((CHIP_ROWS, COLS), bf16)] * 2,
+    )(q2, g2, row_dot, own_weights, own_top, norm, ds, own, *fetched)
     pieces = [swap_cores(piece) for piece in pieces]
-    totals = back[1].astype(f32) + back[0].astype(f32)
+    totals = back[1].astype(f32) + back[0].astype(f32) + own_sums
     far_totals = swap_cores(totals[ROWS:].astype(bf16))
     totals, query_grad = together((totals, query_grad))
     query_grad = call(add_kernel, [shape((ROWS, HQ * DH), bf16)])(query_grad, *pieces)[0]
     far_totals, query_grad = together((far_totals, query_grad))
-    result = totals[:ROWS] + own_sums + far_totals.astype(f32)
+    result = totals[:ROWS] + far_totals.astype(f32)
     result = result.astype(bf16)
     return (query_grad, result[:, :DH], result[:, DH:])
 

time: 29.6 us -> 28.9 us (0.976)
  Pallas kernels: 4.78 us -> 4.44 us
    ppermute x4, starting transfers between devices: 14.6 us -> 14.1 us  [move_chips(): return lax.ppermute(x, AXES, pairs)]
    pallas_call x7 -> x8, Pallas kernels: 4.78 us -> 4.44 us  [call(): pl.pallas_call(kernel, out_shape=outs, in_specs=[vmem] * len(args), out_s...]
    ppermute x10, starting transfers between devices: 2.49 us -> 2.79 us  [swap_cores(): return lax.ppermute(x, 'uly', [(i, i ^ 1) for i in range(16)])]
  transfers between devices with their start and end apart: 14 -> 14, of which waited for: 7 -> 6; matrix products, arithmetic and copies ran while one was open for 3% -> 3% of each run, Pallas kernels for 11% -> 12%
where the time goes in v4:
time: 28.9 us; the launch traced here: 28.8 us
  starting transfers between devices  16.9 us (58%)
  waiting for transfers between devices  5.3 us (18%)
  Pallas kernels  4.44 us (15%)
  other arithmetic  0.77 us (3%)
  between operations  0.77 us (3%)
  local copies, waits for them, and re-layouts  0.64 us (2%)
    ppermute x4, starting transfers between devices, move_chips(): return lax.ppermute(x, AXES, pairs)  14.1 us
    pallas_call x8, Pallas kernels, call(): pl.pallas_call(kernel, out_shape=outs, in_specs=[vmem] * len(args), out_s...  4.44 us
    ppermute x4, waiting for transfers between devices, move_chips(): return lax.ppermute(x, AXES, pairs)  2.92 us
    ppermute x10, starting transfers between devices, swap_cores(): return lax.ppermute(x, 'uly', [(i, i ^ 1) for i in range(16)])  2.79 us
    ppermute x10, waiting for transfers between devices, swap_cores(): return lax.ppermute(x, 'uly', [(i, i ^ 1) for i in range(16)])  2.38 us
    concatenate x1, other arithmetic, on_device(): mine = jnp.concatenate([key_rows, value_rows], axis=1)  0.74 us
    slice x1, local copies, waits for them, and re-layouts, on_device(): return (query_grad, result[:, :DH], result[:, DH:])  0.62 us
  transfers between devices with their start and end apart: 14, of which 6 were waited for; matrix products, arithmetic and copies ran while one was open for 3% of the time, Pallas kernels for 12%

profile of v4, /device:TPU:39, one launch (start us, length us, event | category | flops | bytes accessed | tf_op | source)
XLA Modules:
  0.0 28.8 jit_solution(14224717463054415053)
XLA Ops:
  0.7 0.8 %collective-permute-start = (bf16[64,128]{1,0:T(8,128)(2,1)}, bf16[64,128]{1,0:T(8,128)(2,1)S(1)}, u32[]{:S(2)}, u32[]{:S(2)}) collective-permute-start(bf16[64,128]{1,0:T(8,128)(2,1)} %param.7), channel_id=1, source_target_pairs={{0,1},{1,0},{2,3},{3,2},{4,5},{5,4},{6,7},{7,6},{8,9},{9,8},{10,11... | collective-permute-start | bytes 49160 | tf_op jit(solution)/shard_map/ppermute | solution.py:41
  1.5 0.7 %pad_maximum_fusion.mine_ref = bf16[64,256]{1,0:T(8,128)(2,1)S(1)} fusion(bf16[64,128]{1,0:T(8,128)(2,1)} %param.8, bf16[64,128]{1,0:T(8,128)(2,1)} %param.7), kind=kLoop, calls=%fused_computation.3 | loop fusion | flops 65536 | bytes 65536 | tf_op jit(solution)/shard_map/concatenate | solution.py:272
  2.3 0.2 collective-permute-done.other_k_ref
  2.5 0.3 %collective-permute-done.1.other_v_ref = bf16[64,128]{1,0:T(8,128)(2,1)S(1)} collective-permute-done((bf16[64,128]{1,0:T(8,128)(2,1)}, bf16[64,128]{1,0:T(8,128)(2,1)S(1)}, u32[]{:S(2)}, u32[]{:S(2)}) %collective-permute-start.1) | collective-permute-done | bytes 16416 | tf_op jit(solution)/shard_map/ppermute | solution.py:41
  2.8 2.9 %collective-permute-start.5 = (bf16[128,256]{1,0:T(8,128)(2,1)S(1)}, bf16[128,256]{1,0:T(8,128)(2,1)S(1)}, u32[]{:S(2)}, u32[]{:S(2)}) collective-permute-start(bf16[128,256]{1,0:T(8,128)(2,1)S(1)} %shard_map.85.own_ref), channel_id=1, source_target_pairs={{0,5},{1,6},{2,7},{3,16},{4,17},{5,18},{6,19},{7,20},{16,21},{17,2... | collective-permute-start | bytes 196616 | tf_op jit(solution)/shard_map/ppermute | solution.py:52
  5.7 5.8 %collective-permute-start.4 = (bf16[128,256]{1,0:T(8,128)(2,1)S(1)}, bf16[128,256]{1,0:T(8,128)(2,1)S(1)}, u32[]{:S(2)}, u32[]{:S(2)}) collective-permute-start(bf16[128,256]{1,0:T(8,128)(2,1)S(1)} %shard_map.85.own_ref), channel_id=1, source_target_pairs={{0,3},{1,16},{2,5},{3,18},{4,7},{5,20},{6,17},{7,22},{16,19},{17,3... | collective-permute-start | bytes 196616 | tf_op jit(solution)/shard_map/ppermute | solution.py:52
  11.5 0.7 %shard_map.86 = (bf16[1024,128]{1,0:T(8,128)(2,1)S(1)}, bf16[1024,128]{1,0:T(8,128)(2,1)S(1)}, f32[1,1024]{1,0:T(1,128)S(1)}, bf16[384,128]{1,0:T(8,128)(2,1)S(1...) custom-call(bf16[64,2048]{1,0:T(8,128)(2,1)S(1)} %copy-done, ...), custom_call_target="tpu_custom_call" | custom-call | flops 1000000000 | bytes 2000000 | tf_op jit(solution)/shard_map/pallas_call | solution.py:256
  12.3 0.5 %collective-permute-start.2 = (bf16[1024,128]{1,0:T(8,128)(2,1)S(1)}, bf16[1024,128]{1,0:T(8,128)(2,1)S(1)}, u32[]{:S(2)}, u32[]{:S(2)}) collective-permute-start(bf16[1024,128]{1,0:T(8,128)(2,1)S(1)} %get-tuple-element.34.q_ref), channel_id=1, source_target_pairs={{0,1},{1,0},{2,3},{3,2},{4,5},{5,4},{6,7},{7,6},{8,9},{9,8},{10,11... | collective-permute-start | bytes 786440 | tf_op jit(solution)/shard_map/ppermute | solution.py:41
  12.8 0.1 collective-permute-start.3
  12.9 1.0 %collective-permute-done.2.partner_q_ref = bf16[1024,128]{1,0:T(8,128)(2,1)S(1)} collective-permute-done((bf16[1024,128]{1,0:T(8,128)(2,1)S(1)}, bf16[1024,128]{1,0:T(8,128)(2,1)S(1)}, u32[]{:S(2)}, u32[]{:S(2)}) %collective-permute-start.2) | collective-permute-done | bytes 262176 | tf_op jit(solution)/shard_map/ppermute | solution.py:41
  13.9 0.8 %shard_map.88 = (f32[256,2048]{1,0:T(8,128)S(1)}, f32[2,2048]{1,0:T(2,128)S(1)}, f32[4,1024]{1,0:T(4,128)S(1)}) custom-call(bf16[1024,128]{1,0:T(8,128)(2,1)S(1)} %get-tuple-element.34.q_ref, bf16[1024,128]{1,0:T(8,128)(2,1)S(1)} %collective-permute-done.2.partner_q_ref, bf16[256,256]{1,0:T(8,128)(2,1)S(1)} %shard_map.87.keys_ref, ...), custom_call_target="tpu_custom_call" | custom-call | flops 1000000000 | bytes 2000000 | tf_op jit(solution)/shard_map/pallas_call | solution.py:256
  14.7 0.5 %collective-permute-start.6 = (f32[4,1024]{1,0:T(4,128)S(1)}, f32[4,1024]{1,0:T(4,128)S(1)}, u32[]{:S(2)}, u32[]{:S(2)}) collective-permute-start(f32[4,1024]{1,0:T(4,128)S(1)} %get-tuple-element.40.stats_ref), channel_id=1, source_target_pairs={{0,1},{1,0},{2,3},{3,2},{4,5},{5,4},{6,7},{7,6},{8,9},{9,8},{10,11... | collective-permute-start | bytes 49160 | tf_op jit(solution)/shard_map/ppermute | solution.py:41
  15.2 0.4 %shard_map.89.u_ref = f32[256,2048]{1,0:T(8,128)S(1)} custom-call(bf16[1024,128]{1,0:T(8,128)(2,1)S(1)} %get-tuple-element.35.g_ref, bf16[1024,128]{1,0:T(8,128)(2,1)S(1)} %collective-permute-done.3.partner_g_ref, f32[1,1024]{1,0:T(1,128)S(1)} %get-tuple-element.41.dot_ref, f32[1,1024]{1,0:T(1,128)S(1)} %collective-permute-done.7.partner_dot_ref, ...), custom_call_target="tpu_custom_call" | custom-call | flops 1000000000 | bytes 2000000 | tf_op jit(solution)/shard_map/pallas_call | solution.py:256
  15.6 0.4 %collective-permute-done.6.far_ref = f32[4,1024]{1,0:T(4,128)S(1)} collective-permute-done((f32[4,1024]{1,0:T(4,128)S(1)}, f32[4,1024]{1,0:T(4,128)S(1)}, u32[]{:S(2)}, u32[]{:S(2)}) %collective-permute-start.6) | collective-permute-done | bytes 16416 | tf_op jit(solution)/shard_map/ppermute | solution.py:41
  16.0 0.8 %shard_map.90 = (bf16[128,256]{1,0:T(8,128)(2,1)S(1)}, bf16[128,256]{1,0:T(8,128)(2,1)S(1)}, bf16[256,2048]{1,0:T(8,128)(2,1)S(1)}, f32[2,2048]{1,0:T(2,128)S(1)}) custom-call(bf16[1024,128]{1,0:T(8,128)(2,1)S(1)} %get-tuple-element.34.q_ref, bf16[1024,128]{1,0:T(8,128)(2,1)S(1)} %collective-permute-done.2.partner_q_ref, ...), custom_call_target="tpu_custom_call" | custom-call | flops 1000000000 | bytes 2000000 | tf_op jit(solution)/shard_map/pallas_call | solution.py:256
  16.9 2.2 %collective-permute-start.8 = (bf16[128,256]{1,0:T(8,128)(2,1)S(1)}, bf16[128,256]{1,0:T(8,128)(2,1)S(1)}, u32[]{:S(2)}, u32[]{:S(2)}) collective-permute-start(bf16[128,256]{1,0:T(8,128)(2,1)S(1)} %get-tuple-element.45), channel_id=1, source_target_pairs={{5,0},{6,1},{7,2},{16,3},{17,4},{18,5},{19,6},{20,7},{21,16},{22,1... | collective-permute-start | bytes 196616 | tf_op jit(solution)/shard_map/ppermute | solution.py:52
  19.0 3.3 %collective-permute-start.9 = (bf16[128,256]{1,0:T(8,128)(2,1)S(1)}, bf16[128,256]{1,0:T(8,128)(2,1)S(1)}, u32[]{:S(2)}, u32[]{:S(2)}) collective-permute-start(bf16[128,256]{1,0:T(8,128)(2,1)S(1)} %get-tuple-element.46), channel_id=1, source_target_pairs={{3,0},{16,1},{5,2},{18,3},{7,4},{20,5},{17,6},{22,7},{19,16},{32,1... | collective-permute-start | bytes 196616 | tf_op jit(solution)/shard_map/ppermute | solution.py:52
  22.3 0.9 %shard_map.91 = (f32[1024,128]{1,0:T(8,128)S(1)}, f32[128,256]{1,0:T(8,128)S(1)}, bf16[352,128]{1,0:T(8,128)(2,1)S(1)}, bf16[352,128]{1,0:T(8,128)(2,1)S(1)}, bf16[320,128]{1,0:T(8,128)(2,1)S(1)}) custom-call(bf16[1024,128]{1,0:T(8,128)(2,1)S(1)} %get-tuple-element.34.q_ref, bf16[1024,128]{1,0:T(8,128)(2,1)S(1)} %get-tuple-element.35.g_ref, ...), custom_call_target="tpu_custom_call" | custom-call | flops 1000000000 | bytes 2000000 | tf_op jit(solution)/shard_map/pallas_call | solution.py:256
  23.3 0.5 %collective-permute-start.11 = (bf16[352,128]{1,0:T(8,128)(2,1)S(1)}, bf16[352,128]{1,0:T(8,128)(2,1)S(1)}, u32[]{:S(2)}, u32[]{:S(2)}) collective-permute-start(bf16[352,128]{1,0:T(8,128)(2,1)S(1)} %get-tuple-element.53), channel_id=1, source_target_pairs={{0,1},{1,0},{2,3},{3,2},{4,5},{5,4},{6,7},{7,6},{8,9},{9,8},{10,11... | collective-permute-start | bytes 270344 | tf_op jit(solution)/shard_map/ppermute | solution.py:41
  23.8 0.1 collective-permute-start.12
  23.9 2.9 %collective-permute-done.9 = bf16[128,256]{1,0:T(8,128)(2,1)S(1)} collective-permute-done((bf16[128,256]{1,0:T(8,128)(2,1)S(1)}, bf16[128,256]{1,0:T(8,128)(2,1)S(1)}, u32[]{:S(2)}, u32[]{:S(2)}) %collective-permute-start.9) | collective-permute-done | bytes 65568 | tf_op jit(solution)/shard_map/ppermute | solution.py:52
  27.0 0.8 %shard_map.92 = bf16[64,2048]{1,0:T(8,128)(2,1)} custom-call(f32[1024,128]{1,0:T(8,128)S(1)} %get-tuple-element.52.dq_ref, bf16[352,128]{1,0:T(8,128)(2,1)S(1)} %collective-permute-done.11.refs_0_, bf16[352,128]{1,0:T(8,128)(2,1)S(1)} %collective-permute-done.12.refs_1_, bf16[320,128]{1,0:T(8,128)(2,1)S(1)} %collective-permute-done.13.refs_2_), custom_call_target="tpu_custom_call" | custom-call | flops 1000000000 | bytes 2000000 | tf_op jit(solution)/shard_map/pallas_call | solution.py:256
  27.8 0.4 %collective-permute-done.10 = bf16[64,256]{1,0:T(8,128)(2,1)S(1)} collective-permute-done((bf16[64,256]{1,0:T(8,128)(2,1)S(1)}, bf16[64,256]{1,0:T(8,128)(2,1)S(1)}, u32[]{:S(2)}, u32[]{:S(2)}) %collective-permute-start.10) | collective-permute-done | bytes 32800 | tf_op jit(solution)/shard_map/ppermute | solution.py:41
  28.2 0.6 %fusion = (bf16[64,128]{1,0:T(8,128)(2,1)}, bf16[64,128]{1,0:T(8,128)(2,1)}) fusion(bf16[64,256]{1,0:T(8,128)(2,1)S(1)} %add_convert_fusion), kind=kLoop, calls=%fused_computation.4 | loop fusion | bytes 65536 | tf_op jit(solution)/shard_map/slice | solution.py:314
  (25 shorter events, 0.5 us)
Async XLA Ops:
  0.6 10.9 %copy-start.3 = (s32[64]{0:T(128)S(1)}, s32[64]{0:T(128)}, u32[]{:S(2)}) copy-start(s32[64]{0:T(128)} %param.11) | copy-start | bytes 772
  0.6 10.9 %copy-start.2 = (bf16[64,2048]{1,0:T(8,128)(2,1)S(1)}, bf16[64,2048]{1,0:T(8,128)(2,1)}, u32[]{:S(2)}) copy-start(bf16[64,2048]{1,0:T(8,128)(2,1)} %g_ref.1) | copy-start | bytes 786436
  0.7 10.9 %copy-start.1 = (bf16[64,2048]{1,0:T(8,128)(2,1)S(1)}, bf16[64,2048]{1,0:T(8,128)(2,1)}, u32[]{:S(2)}) copy-start(bf16[64,2048]{1,0:T(8,128)(2,1)} %o_ref.1) | copy-start | bytes 786436
  0.7 10.8 %copy-start = (bf16[64,2048]{1,0:T(8,128)(2,1)S(1)}, bf16[64,2048]{1,0:T(8,128)(2,1)}, u32[]{:S(2)}) copy-start(bf16[64,2048]{1,0:T(8,128)(2,1)} %q_ref.1) | copy-start | bytes 786436
  0.7 1.8 %collective-permute-start = (bf16[64,128]{1,0:T(8,128)(2,1)}, bf16[64,128]{1,0:T(8,128)(2,1)S(1)}, u32[]{:S(2)}, u32[]{:S(2)}) collective-permute-start(bf16[64,128]{1,0:T(8,128)(2,1)} %param.7), channel_id=1, source_target_pairs={{0,1},{1,0},{2,3},{3,2},{4,5},{5,4},{6,7},{7,6},{8,9},{9,8},{10,11... | collective-permute-start | bytes 49160 | tf_op jit(solution)/shard_map/ppermute | solution.py:41
  1.4 1.4 %collective-permute-start.1 = (bf16[64,128]{1,0:T(8,128)(2,1)}, bf16[64,128]{1,0:T(8,128)(2,1)S(1)}, u32[]{:S(2)}, u32[]{:S(2)}) collective-permute-start(bf16[64,128]{1,0:T(8,128)(2,1)} %param.8), channel_id=1, source_target_pairs={{0,1},{1,0},{2,3},{3,2},{4,5},{5,4},{6,7},{7,6},{8,9},{9,8},{10,11... | collective-permute-start | bytes 49160 | tf_op jit(solution)/shard_map/ppermute | solution.py:41
  2.8 10.0 %collective-permute-start.5 = (bf16[128,256]{1,0:T(8,128)(2,1)S(1)}, bf16[128,256]{1,0:T(8,128)(2,1)S(1)}, u32[]{:S(2)}, u32[]{:S(2)}) collective-permute-start(bf16[128,256]{1,0:T(8,128)(2,1)S(1)} %shard_map.85.own_ref), channel_id=1, source_target_pairs={{0,5},{1,6},{2,7},{3,16},{4,17},{5,18},{6,19},{7,20},{16,21},{17,2... | collective-permute-start | bytes 196616 | tf_op jit(solution)/shard_map/ppermute | solution.py:52
  5.7 7.2 %collective-permute-start.4 = (bf16[128,256]{1,0:T(8,128)(2,1)S(1)}, bf16[128,256]{1,0:T(8,128)(2,1)S(1)}, u32[]{:S(2)}, u32[]{:S(2)}) collective-permute-start(bf16[128,256]{1,0:T(8,128)(2,1)S(1)} %shard_map.85.own_ref), channel_id=1, source_target_pairs={{0,3},{1,16},{2,5},{3,18},{4,7},{5,20},{6,17},{7,22},{16,19},{17,3... | collective-permute-start | bytes 196616 | tf_op jit(solution)/shard_map/ppermute | solution.py:52
  12.2 3.0 %collective-permute-start.7 = (f32[1,1024]{1,0:T(1,128)S(1)}, f32[1,1024]{1,0:T(1,128)S(1)}, u32[]{:S(2)}, u32[]{:S(2)}) collective-permute-start(f32[1,1024]{1,0:T(1,128)S(1)} %get-tuple-element.41.dot_ref), channel_id=1, source_target_pairs={{0,1},{1,0},{2,3},{3,2},{4,5},{5,4},{6,7},{7,6},{8,9},{9,8},{10,11... | collective-permute-start | bytes 12296 | tf_op jit(solution)/shard_map/ppermute | solution.py:41
  12.3 1.7 %collective-permute-start.2 = (bf16[1024,128]{1,0:T(8,128)(2,1)S(1)}, bf16[1024,128]{1,0:T(8,128)(2,1)S(1)}, u32[]{:S(2)}, u32[]{:S(2)}) collective-permute-start(bf16[1024,128]{1,0:T(8,128)(2,1)S(1)} %get-tuple-element.34.q_ref), channel_id=1, source_target_pairs={{0,1},{1,0},{2,3},{3,2},{4,5},{5,4},{6,7},{7,6},{8,9},{9,8},{10,11... | collective-permute-start | bytes 786440 | tf_op jit(solution)/shard_map/ppermute | solution.py:41
  12.8 2.4 %collective-permute-start.3 = (bf16[1024,128]{1,0:T(8,128)(2,1)S(1)}, bf16[1024,128]{1,0:T(8,128)(2,1)S(1)}, u32[]{:S(2)}, u32[]{:S(2)}) collective-permute-start(bf16[1024,128]{1,0:T(8,128)(2,1)S(1)} %get-tuple-element.35.g_ref), channel_id=1, source_target_pairs={{0,1},{1,0},{2,3},{3,2},{4,5},{5,4},{6,7},{7,6},{8,9},{9,8},{10,11... | collective-permute-start | bytes 786440 | tf_op jit(solution)/shard_map/ppermute | solution.py:41
  14.7 1.3 %collective-permute-start.6 = (f32[4,1024]{1,0:T(4,128)S(1)}, f32[4,1024]{1,0:T(4,128)S(1)}, u32[]{:S(2)}, u32[]{:S(2)}) collective-permute-start(f32[4,1024]{1,0:T(4,128)S(1)} %get-tuple-element.40.stats_ref), channel_id=1, source_target_pairs={{0,1},{1,0},{2,3},{3,2},{4,5},{5,4},{6,7},{7,6},{8,9},{9,8},{10,11... | collective-permute-start | bytes 49160 | tf_op jit(solution)/shard_map/ppermute | solution.py:41
  16.9 7.0 %collective-permute-start.8 = (bf16[128,256]{1,0:T(8,128)(2,1)S(1)}, bf16[128,256]{1,0:T(8,128)(2,1)S(1)}, u32[]{:S(2)}, u32[]{:S(2)}) collective-permute-start(bf16[128,256]{1,0:T(8,128)(2,1)S(1)} %get-tuple-element.45), channel_id=1, source_target_pairs={{5,0},{6,1},{7,2},{16,3},{17,4},{18,5},{19,6},{20,7},{21,16},{22,1... | collective-permute-start | bytes 196616 | tf_op jit(solution)/shard_map/ppermute | solution.py:52
  19.0 7.8 %collective-permute-start.9 = (bf16[128,256]{1,0:T(8,128)(2,1)S(1)}, bf16[128,256]{1,0:T(8,128)(2,1)S(1)}, u32[]{:S(2)}, u32[]{:S(2)}) collective-permute-start(bf16[128,256]{1,0:T(8,128)(2,1)S(1)} %get-tuple-element.46), channel_id=1, source_target_pairs={{3,0},{16,1},{5,2},{18,3},{7,4},{20,5},{17,6},{22,7},{19,16},{32,1... | collective-permute-start | bytes 196616 | tf_op jit(solution)/shard_map/ppermute | solution.py:52
  23.2 3.8 %collective-permute-start.13 = (bf16[320,128]{1,0:T(8,128)(2,1)S(1)}, bf16[320,128]{1,0:T(8,128)(2,1)S(1)}, u32[]{:S(2)}, u32[]{:S(2)}) collective-permute-start(bf16[320,128]{1,0:T(8,128)(2,1)S(1)} %get-tuple-element.55), channel_id=1, source_target_pairs={{0,1},{1,0},{2,3},{3,2},{4,5},{5,4},{6,7},{7,6},{8,9},{9,8},{10,11... | collective-permute-start | bytes 245768 | tf_op jit(solution)/shard_map/ppermute | solution.py:41
  23.3 3.7 %collective-permute-start.11 = (bf16[352,128]{1,0:T(8,128)(2,1)S(1)}, bf16[352,128]{1,0:T(8,128)(2,1)S(1)}, u32[]{:S(2)}, u32[]{:S(2)}) collective-permute-start(bf16[352,128]{1,0:T(8,128)(2,1)S(1)} %get-tuple-element.53), channel_id=1, source_target_pairs={{0,1},{1,0},{2,3},{3,2},{4,5},{5,4},{6,7},{7,6},{8,9},{9,8},{10,11... | collective-permute-start | bytes 270344 | tf_op jit(solution)/shard_map/ppermute | solution.py:41
  23.8 3.2 %collective-permute-start.12 = (bf16[352,128]{1,0:T(8,128)(2,1)S(1)}, bf16[352,128]{1,0:T(8,128)(2,1)S(1)}, u32[]{:S(2)}, u32[]{:S(2)}) collective-permute-start(bf16[352,128]{1,0:T(8,128)(2,1)S(1)} %get-tuple-element.54), channel_id=1, source_target_pairs={{0,1},{1,0},{2,3},{3,2},{4,5},{5,4},{6,7},{7,6},{8,9},{9,8},{10,11... | collective-permute-start | bytes 270344 | tf_op jit(solution)/shard_map/ppermute | solution.py:41
  26.9 1.3 %collective-permute-start.10 = (bf16[64,256]{1,0:T(8,128)(2,1)S(1)}, bf16[64,256]{1,0:T(8,128)(2,1)S(1)}, u32[]{:S(2)}, u32[]{:S(2)}) collective-permute-start(bf16[64,256]{1,0:T(8,128)(2,1)S(1)} %slice.22), channel_id=1, source_target_pairs={{0,1},{1,0},{2,3},{3,2},{4,5},{5,4},{6,7},{7,6},{8,9},{9,8},{10,11... | collective-permute-start | bytes 98312 | tf_op jit(solution)/shard_map/ppermute | solution.py:41

commit v5 on v4

--- a/solution.py
+++ b/solution.py
@@ -24,7 +24,7 @@
 SCALING = 1.0 / math.sqrt(DH)
 EXP2_SCALING = SCALING * math.log2(math.e)
 AXES = ("blk", "uly")
-STEPS = ((1, 4), (2, 3))
+STEPS = ((1, 4), (3, 2))
 CROSS = (1, 1)
 PIECES = (0, 352, 704, COLS)
 KEY_COLS, VALUE_COLS = slice(0, DH), slice(DH, 2 * DH)
@@ -85,9 +85,10 @@
 
 
 def query_tile(queries, side):
-    row = lax.rem(lax.broadcasted_iota(jnp.int32, (TILE, DH), 0), ROWS) + side * ROWS
-    lane = lax.broadcasted_iota(jnp.int32, (TILE, DH), 1)
-    return jnp.concatenate([queries, (row == lane).astype(jnp.bfloat16)], axis=1)
+    row = lax.rem(lax.broadcasted_iota(jnp.int32, (DH, DH), 0), ROWS) + side * ROWS
+    lane = lax.broadcasted_iota(jnp.int32, (DH, DH), 1)
+    hot = (row == lane).astype(jnp.bfloat16)
+    return jnp.concatenate([queries, jnp.concatenate([hot] * (queries.shape[0] // DH), axis=0)], axis=1)
 
 
 def scored(scores):
@@ -154,12 +155,14 @@
 
 def score_kernel(q_ref, partner_q_ref, keys_ref, own_top_ref, own_sum_ref,
                  e_ref, tops_ref, stats_ref):
-    for cols, side, rows in tiles():
-        query = query_tile((q_ref, partner_q_ref)[side][rows, :], side)
-        scores = dot_nt(keys_ref[...], query)
+    for side, ref in enumerate((q_ref, partner_q_ref)):
+        e_ref[:, side * COLS : (side + 1) * COLS] = dot_nt(keys_ref[...], query_tile(ref[...], side))
+    for at in range(0, 2 * COLS, DH):
+        side, start = divmod(at, COLS)
+        cols, rows = slice(at, at + DH), slice(start, start + DH)
         tops, sums = [], []
         for i, group in enumerate(GROUPS):
-            e_ref[group, cols], top, total = scored(scores[group])
+            e_ref[group, cols], top, total = scored(e_ref[group, cols])
             tops_ref[i : i + 1, cols] = top
             tops.append(top)
             sums.append(total)
@@ -186,21 +189,23 @@
 
 def main_kernel(q_ref, partner_q_ref, g_ref, partner_g_ref, e_ref, u_ref, tops_ref, stats_ref, far_ref,
                 a_ref, b_ref, ds_ref, norm_ref, p_ref):
-    for cols, side, rows in tiles():
+    for side in range(2):
         near, far = 2 * side, 2 - 2 * side
-        top = stats_ref[near : near + 1, rows]
-        far_top = far_ref[far : far + 1, rows]
+        top, far_top = stats_ref[near : near + 1, :], far_ref[far : far + 1, :]
         most = jnp.maximum(top, far_top)
-        total = stats_ref[near + 1 : near + 2, rows] * jnp.exp2(
+        total = stats_ref[near + 1 : near + 2, :] * jnp.exp2(
             (top - most) * EXP2_SCALING
-        ) + far_ref[far + 1 : far + 2, rows] * jnp.exp2((far_top - most) * EXP2_SCALING)
-        norm_ref[0:1, cols] = most
-        norm_ref[1:2, cols] = total
-        for i, group in enumerate(GROUPS):
-            factor = jnp.exp2((tops_ref[i : i + 1, cols] - most) * EXP2_SCALING) / total
-            weights = e_ref[group, cols] * factor
-            ds_ref[group, cols] = (weights * u_ref[group, cols]).astype(jnp.bfloat16)
-            p_ref[group, cols] = weights.astype(jnp.bfloat16)
+        ) + far_ref[far + 1 : far + 2, :] * jnp.exp2((far_top - most) * EXP2_SCALING)
+        columns = slice(side * COLS, (side + 1) * COLS)
+        norm_ref[0:1, columns] = most
+        norm_ref[1:2, columns] = total
+        factors = jnp.exp2((tops_ref[:, columns] - most) * EXP2_SCALING) * (1.0 / total)
+        for start in range(0, COLS, TILE):
+            cols = slice(side * COLS + start, side * COLS + start + TILE)
+            for i, group in enumerate(GROUPS):
+                weights = e_ref[group, cols] * factors[i : i + 1, start : start + TILE]
+                ds_ref[group, cols] = (weights * u_ref[group, cols]).astype(jnp.bfloat16)
+                p_ref[group, cols] = weights.astype(jnp.bfloat16)
     key_grads = (dot_sides(ds_ref, q_ref, partner_q_ref) * SCALING).astype(jnp.bfloat16)
     value_grads = dot_sides(p_ref, g_ref, partner_g_ref).astype(jnp.bfloat16)
     for ref, group in zip((a_ref, b_ref), GROUPS):

time: 28.9 us -> 28.9 us (level)
  waiting for transfers between devices: 5.3 us -> 6.31 us
  starting transfers between devices: 16.9 us -> 15.9 us
    ppermute x4, waiting for transfers between devices: 2.92 us -> 3.93 us  [move_chips(): return lax.ppermute(x, AXES, pairs)]
    ppermute x4, starting transfers between devices: 14.1 us -> 13.1 us  [move_chips(): return lax.ppermute(x, AXES, pairs)]
where the time goes in v5:
time: 28.9 us; the launch traced here: 28.7 us
  starting transfers between devices  15.9 us (55%)
  waiting for transfers between devices  6.31 us (22%)
  Pallas kernels  4.35 us (15%)
  other arithmetic  0.77 us (3%)
  between operations  0.76 us (3%)
  local copies, waits for them, and re-layouts  0.64 us (2%)
    ppermute x4, starting transfers between devices, move_chips(): return lax.ppermute(x, AXES, pairs)  13.1 us
    pallas_call x8, Pallas kernels, call(): pl.pallas_call(kernel, out_shape=outs, in_specs=[vmem] * len(args), out_s...  4.35 us
    ppermute x4, waiting for transfers between devices, move_chips(): return lax.ppermute(x, AXES, pairs)  3.93 us
    ppermute x10, starting transfers between devices, swap_cores(): return lax.ppermute(x, 'uly', [(i, i ^ 1) for i in range(16)])  2.8 us
    ppermute x10, waiting for transfers between devices, swap_cores(): return lax.ppermute(x, 'uly', [(i, i ^ 1) for i in range(16)])  2.38 us
    concatenate x1, other arithmetic, on_device(): mine = jnp.concatenate([key_rows, value_rows], axis=1)  0.74 us
    slice x1, local copies, waits for them, and re-layouts, on_device(): return (query_grad, result[:, :DH], result[:, DH:])  0.62 us
  transfers between devices with their start and end apart: 14, of which 6 were waited for; matrix products, arithmetic and copies ran while one was open for 3% of the time, Pallas kernels for 12%

profile of v5, /device:TPU:39, one launch (start us, length us, event | category | flops | bytes accessed | tf_op | source)
XLA Modules:
  0.0 28.7 jit_solution(17325111725507280277)
XLA Ops:
  0.7 0.8 %collective-permute-start = (bf16[64,128]{1,0:T(8,128)(2,1)}, bf16[64,128]{1,0:T(8,128)(2,1)S(1)}, u32[]{:S(2)}, u32[]{:S(2)}) collective-permute-start(bf16[64,128]{1,0:T(8,128)(2,1)} %param.7), channel_id=1, source_target_pairs={{0,1},{1,0},{2,3},{3,2},{4,5},{5,4},{6,7},{7,6},{8,9},{9,8},{10,11... | collective-permute-start | bytes 49160 | tf_op jit(solution)/shard_map/ppermute | solution.py:41
  1.5 0.7 %pad_maximum_fusion.mine_ref = bf16[64,256]{1,0:T(8,128)(2,1)S(1)} fusion(bf16[64,128]{1,0:T(8,128)(2,1)} %param.8, bf16[64,128]{1,0:T(8,128)(2,1)} %param.7), kind=kLoop, calls=%fused_computation.3 | loop fusion | flops 65536 | bytes 65536 | tf_op jit(solution)/shard_map/concatenate | solution.py:277
  2.3 0.2 collective-permute-done.other_k_ref
  2.5 0.3 %collective-permute-done.1.other_v_ref = bf16[64,128]{1,0:T(8,128)(2,1)S(1)} collective-permute-done((bf16[64,128]{1,0:T(8,128)(2,1)}, bf16[64,128]{1,0:T(8,128)(2,1)S(1)}, u32[]{:S(2)}, u32[]{:S(2)}) %collective-permute-start.1) | collective-permute-done | bytes 16416 | tf_op jit(solution)/shard_map/ppermute | solution.py:41
  2.8 3.0 %collective-permute-start.5 = (bf16[128,256]{1,0:T(8,128)(2,1)S(1)}, bf16[128,256]{1,0:T(8,128)(2,1)S(1)}, u32[]{:S(2)}, u32[]{:S(2)}) collective-permute-start(bf16[128,256]{1,0:T(8,128)(2,1)S(1)} %shard_map.85.own_ref), channel_id=1, source_target_pairs={{0,7},{1,4},{2,17},{3,6},{4,19},{5,16},{6,21},{7,18},{16,23},{17,2... | collective-permute-start | bytes 196616 | tf_op jit(solution)/shard_map/ppermute | solution.py:52
  5.9 5.4 %collective-permute-start.4 = (bf16[128,256]{1,0:T(8,128)(2,1)S(1)}, bf16[128,256]{1,0:T(8,128)(2,1)S(1)}, u32[]{:S(2)}, u32[]{:S(2)}) collective-permute-start(bf16[128,256]{1,0:T(8,128)(2,1)S(1)} %shard_map.85.own_ref), channel_id=1, source_target_pairs={{0,3},{1,16},{2,5},{3,18},{4,7},{5,20},{6,17},{7,22},{16,19},{17,3... | collective-permute-start | bytes 196616 | tf_op jit(solution)/shard_map/ppermute | solution.py:52
  11.3 0.7 %shard_map.86 = (bf16[1024,128]{1,0:T(8,128)(2,1)S(1)}, bf16[1024,128]{1,0:T(8,128)(2,1)S(1)}, f32[1,1024]{1,0:T(1,128)S(1)}, bf16[384,128]{1,0:T(8,128)(2,1)S(1...) custom-call(bf16[64,2048]{1,0:T(8,128)(2,1)S(1)} %copy-done, ...), custom_call_target="tpu_custom_call" | custom-call | flops 1000000000 | bytes 2000000 | tf_op jit(solution)/shard_map/pallas_call | solution.py:261
  12.1 0.5 %collective-permute-start.2 = (bf16[1024,128]{1,0:T(8,128)(2,1)S(1)}, bf16[1024,128]{1,0:T(8,128)(2,1)S(1)}, u32[]{:S(2)}, u32[]{:S(2)}) collective-permute-start(bf16[1024,128]{1,0:T(8,128)(2,1)S(1)} %get-tuple-element.34.q_ref), channel_id=1, source_target_pairs={{0,1},{1,0},{2,3},{3,2},{4,5},{5,4},{6,7},{7,6},{8,9},{9,8},{10,11... | collective-permute-start | bytes 786440 | tf_op jit(solution)/shard_map/ppermute | solution.py:41
  12.6 0.1 collective-permute-start.3
  12.7 1.0 %collective-permute-done.2.partner_q_ref = bf16[1024,128]{1,0:T(8,128)(2,1)S(1)} collective-permute-done((bf16[1024,128]{1,0:T(8,128)(2,1)S(1)}, bf16[1024,128]{1,0:T(8,128)(2,1)S(1)}, u32[]{:S(2)}, u32[]{:S(2)}) %collective-permute-start.2) | collective-permute-done | bytes 262176 | tf_op jit(solution)/shard_map/ppermute | solution.py:41
  13.8 0.7 %shard_map.88 = (f32[256,2048]{1,0:T(8,128)S(1)}, f32[2,2048]{1,0:T(2,128)S(1)}, f32[4,1024]{1,0:T(4,128)S(1)}) custom-call(bf16[1024,128]{1,0:T(8,128)(2,1)S(1)} %get-tuple-element.34.q_ref, bf16[1024,128]{1,0:T(8,128)(2,1)S(1)} %collective-permute-done.2.partner_q_ref, bf16[256,256]{1,0:T(8,128)(2,1)S(1)} %shard_map.87.keys_ref, ...), custom_call_target="tpu_custom_call" | custom-call | flops 1000000000 | bytes 2000000 | tf_op jit(solution)/shard_map/pallas_call | solution.py:261
  14.5 0.5 %collective-permute-start.6 = (f32[4,1024]{1,0:T(4,128)S(1)}, f32[4,1024]{1,0:T(4,128)S(1)}, u32[]{:S(2)}, u32[]{:S(2)}) collective-permute-start(f32[4,1024]{1,0:T(4,128)S(1)} %get-tuple-element.40.stats_ref), channel_id=1, source_target_pairs={{0,1},{1,0},{2,3},{3,2},{4,5},{5,4},{6,7},{7,6},{8,9},{9,8},{10,11... | collective-permute-start | bytes 49160 | tf_op jit(solution)/shard_map/ppermute | solution.py:41
  15.0 0.4 %shard_map.89.u_ref = f32[256,2048]{1,0:T(8,128)S(1)} custom-call(bf16[1024,128]{1,0:T(8,128)(2,1)S(1)} %get-tuple-element.35.g_ref, bf16[1024,128]{1,0:T(8,128)(2,1)S(1)} %collective-permute-done.3.partner_g_ref, f32[1,1024]{1,0:T(1,128)S(1)} %get-tuple-element.41.dot_ref, f32[1,1024]{1,0:T(1,128)S(1)} %collective-permute-done.7.partner_dot_ref, ...), custom_call_target="tpu_custom_call" | custom-call | flops 1000000000 | bytes 2000000 | tf_op jit(solution)/shard_map/pallas_call | solution.py:261
  15.4 0.4 %collective-permute-done.6.far_ref = f32[4,1024]{1,0:T(4,128)S(1)} collective-permute-done((f32[4,1024]{1,0:T(4,128)S(1)}, f32[4,1024]{1,0:T(4,128)S(1)}, u32[]{:S(2)}, u32[]{:S(2)}) %collective-permute-start.6) | collective-permute-done | bytes 16416 | tf_op jit(solution)/shard_map/ppermute | solution.py:41
  15.8 0.8 %shard_map.90 = (bf16[128,256]{1,0:T(8,128)(2,1)S(1)}, bf16[128,256]{1,0:T(8,128)(2,1)S(1)}, bf16[256,2048]{1,0:T(8,128)(2,1)S(1)}, f32[2,2048]{1,0:T(2,128)S(1)}) custom-call(bf16[1024,128]{1,0:T(8,128)(2,1)S(1)} %get-tuple-element.34.q_ref, bf16[1024,128]{1,0:T(8,128)(2,1)S(1)} %collective-permute-done.2.partner_q_ref, ...), custom_call_target="tpu_custom_call" | custom-call | flops 1000000000 | bytes 2000000 | tf_op jit(solution)/shard_map/pallas_call | solution.py:261
  16.6 2.2 %collective-permute-start.8 = (bf16[128,256]{1,0:T(8,128)(2,1)S(1)}, bf16[128,256]{1,0:T(8,128)(2,1)S(1)}, u32[]{:S(2)}, u32[]{:S(2)}) collective-permute-start(bf16[128,256]{1,0:T(8,128)(2,1)S(1)} %get-tuple-element.45), channel_id=1, source_target_pairs={{7,0},{4,1},{17,2},{6,3},{19,4},{16,5},{21,6},{18,7},{23,16},{20,1... | collective-permute-start | bytes 196616 | tf_op jit(solution)/shard_map/ppermute | solution.py:52
  18.8 2.4 %collective-permute-start.9 = (bf16[128,256]{1,0:T(8,128)(2,1)S(1)}, bf16[128,256]{1,0:T(8,128)(2,1)S(1)}, u32[]{:S(2)}, u32[]{:S(2)}) collective-permute-start(bf16[128,256]{1,0:T(8,128)(2,1)S(1)} %get-tuple-element.46), channel_id=1, source_target_pairs={{3,0},{16,1},{5,2},{18,3},{7,4},{20,5},{17,6},{22,7},{19,16},{32,1... | collective-permute-start | bytes 196616 | tf_op jit(solution)/shard_map/ppermute | solution.py:52
  21.2 0.9 %shard_map.91 = (f32[1024,128]{1,0:T(8,128)S(1)}, f32[128,256]{1,0:T(8,128)S(1)}, bf16[352,128]{1,0:T(8,128)(2,1)S(1)}, bf16[352,128]{1,0:T(8,128)(2,1)S(1)}, bf16[320,128]{1,0:T(8,128)(2,1)S(1)}) custom-call(bf16[1024,128]{1,0:T(8,128)(2,1)S(1)} %get-tuple-element.34.q_ref, bf16[1024,128]{1,0:T(8,128)(2,1)S(1)} %get-tuple-element.35.g_ref, ...), custom_call_target="tpu_custom_call" | custom-call | flops 1000000000 | bytes 2000000 | tf_op jit(solution)/shard_map/pallas_call | solution.py:261
  22.1 0.1 collective-permute-start.13
  22.3 0.5 %collective-permute-start.11 = (bf16[352,128]{1,0:T(8,128)(2,1)S(1)}, bf16[352,128]{1,0:T(8,128)(2,1)S(1)}, u32[]{:S(2)}, u32[]{:S(2)}) collective-permute-start(bf16[352,128]{1,0:T(8,128)(2,1)S(1)} %get-tuple-element.53), channel_id=1, source_target_pairs={{0,1},{1,0},{2,3},{3,2},{4,5},{5,4},{6,7},{7,6},{8,9},{9,8},{10,11... | collective-permute-start | bytes 270344 | tf_op jit(solution)/shard_map/ppermute | solution.py:41
  22.8 3.9 %collective-permute-done.9 = bf16[128,256]{1,0:T(8,128)(2,1)S(1)} collective-permute-done((bf16[128,256]{1,0:T(8,128)(2,1)S(1)}, bf16[128,256]{1,0:T(8,128)(2,1)S(1)}, u32[]{:S(2)}, u32[]{:S(2)}) %collective-permute-start.9) | collective-permute-done | bytes 65568 | tf_op jit(solution)/shard_map/ppermute | solution.py:52
  26.9 0.8 %shard_map.92 = bf16[64,2048]{1,0:T(8,128)(2,1)} custom-call(f32[1024,128]{1,0:T(8,128)S(1)} %get-tuple-element.52.dq_ref, bf16[352,128]{1,0:T(8,128)(2,1)S(1)} %collective-permute-done.11.refs_0_, bf16[352,128]{1,0:T(8,128)(2,1)S(1)} %collective-permute-done.12.refs_1_, bf16[320,128]{1,0:T(8,128)(2,1)S(1)} %collective-permute-done.13.refs_2_), custom_call_target="tpu_custom_call" | custom-call | flops 1000000000 | bytes 2000000 | tf_op jit(solution)/shard_map/pallas_call | solution.py:261
  27.7 0.4 %collective-permute-done.10 = bf16[64,256]{1,0:T(8,128)(2,1)S(1)} collective-permute-done((bf16[64,256]{1,0:T(8,128)(2,1)S(1)}, bf16[64,256]{1,0:T(8,128)(2,1)S(1)}, u32[]{:S(2)}, u32[]{:S(2)}) %collective-permute-start.10) | collective-permute-done | bytes 32800 | tf_op jit(solution)/shard_map/ppermute | solution.py:41
  28.1 0.6 %fusion = (bf16[64,128]{1,0:T(8,128)(2,1)}, bf16[64,128]{1,0:T(8,128)(2,1)}) fusion(bf16[64,256]{1,0:T(8,128)(2,1)S(1)} %add_convert_fusion), kind=kLoop, calls=%fused_computation.4 | loop fusion | bytes 65536 | tf_op jit(solution)/shard_map/slice | solution.py:319
  (25 shorter events, 0.5 us)
Async XLA Ops:
  0.6 10.7 %copy-start.3 = (s32[64]{0:T(128)S(1)}, s32[64]{0:T(128)}, u32[]{:S(2)}) copy-start(s32[64]{0:T(128)} %param.11) | copy-start | bytes 772
  0.6 10.7 %copy-start.2 = (bf16[64,2048]{1,0:T(8,128)(2,1)S(1)}, bf16[64,2048]{1,0:T(8,128)(2,1)}, u32[]{:S(2)}) copy-start(bf16[64,2048]{1,0:T(8,128)(2,1)} %g_ref.1) | copy-start | bytes 786436
  0.7 10.7 %copy-start.1 = (bf16[64,2048]{1,0:T(8,128)(2,1)S(1)}, bf16[64,2048]{1,0:T(8,128)(2,1)}, u32[]{:S(2)}) copy-start(bf16[64,2048]{1,0:T(8,128)(2,1)} %o_ref.1) | copy-start | bytes 786436
  0.7 10.7 %copy-start = (bf16[64,2048]{1,0:T(8,128)(2,1)S(1)}, bf16[64,2048]{1,0:T(8,128)(2,1)}, u32[]{:S(2)}) copy-start(bf16[64,2048]{1,0:T(8,128)(2,1)} %q_ref.1) | copy-start | bytes 786436
  0.7 1.8 %collective-permute-start = (bf16[64,128]{1,0:T(8,128)(2,1)}, bf16[64,128]{1,0:T(8,128)(2,1)S(1)}, u32[]{:S(2)}, u32[]{:S(2)}) collective-permute-start(bf16[64,128]{1,0:T(8,128)(2,1)} %param.7), channel_id=1, source_target_pairs={{0,1},{1,0},{2,3},{3,2},{4,5},{5,4},{6,7},{7,6},{8,9},{9,8},{10,11... | collective-permute-start | bytes 49160 | tf_op jit(solution)/shard_map/ppermute | solution.py:41
  1.4 1.4 %collective-permute-start.1 = (bf16[64,128]{1,0:T(8,128)(2,1)}, bf16[64,128]{1,0:T(8,128)(2,1)S(1)}, u32[]{:S(2)}, u32[]{:S(2)}) collective-permute-start(bf16[64,128]{1,0:T(8,128)(2,1)} %param.8), channel_id=1, source_target_pairs={{0,1},{1,0},{2,3},{3,2},{4,5},{5,4},{6,7},{7,6},{8,9},{9,8},{10,11... | collective-permute-start | bytes 49160 | tf_op jit(solution)/shard_map/ppermute | solution.py:41
  2.8 9.9 %collective-permute-start.5 = (bf16[128,256]{1,0:T(8,128)(2,1)S(1)}, bf16[128,256]{1,0:T(8,128)(2,1)S(1)}, u32[]{:S(2)}, u32[]{:S(2)}) collective-permute-start(bf16[128,256]{1,0:T(8,128)(2,1)S(1)} %shard_map.85.own_ref), channel_id=1, source_target_pairs={{0,7},{1,4},{2,17},{3,6},{4,19},{5,16},{6,21},{7,18},{16,23},{17,2... | collective-permute-start | bytes 196616 | tf_op jit(solution)/shard_map/ppermute | solution.py:52
  5.9 6.8 %collective-permute-start.4 = (bf16[128,256]{1,0:T(8,128)(2,1)S(1)}, bf16[128,256]{1,0:T(8,128)(2,1)S(1)}, u32[]{:S(2)}, u32[]{:S(2)}) collective-permute-start(bf16[128,256]{1,0:T(8,128)(2,1)S(1)} %shard_map.85.own_ref), channel_id=1, source_target_pairs={{0,3},{1,16},{2,5},{3,18},{4,7},{5,20},{6,17},{7,22},{16,19},{17,3... | collective-permute-start | bytes 196616 | tf_op jit(solution)/shard_map/ppermute | solution.py:52
  12.0 2.9 %collective-permute-start.7 = (f32[1,1024]{1,0:T(1,128)S(1)}, f32[1,1024]{1,0:T(1,128)S(1)}, u32[]{:S(2)}, u32[]{:S(2)}) collective-permute-start(f32[1,1024]{1,0:T(1,128)S(1)} %get-tuple-element.41.dot_ref), channel_id=1, source_target_pairs={{0,1},{1,0},{2,3},{3,2},{4,5},{5,4},{6,7},{7,6},{8,9},{9,8},{10,11... | collective-permute-start | bytes 12296 | tf_op jit(solution)/shard_map/ppermute | solution.py:41
  12.1 1.7 %collective-permute-start.2 = (bf16[1024,128]{1,0:T(8,128)(2,1)S(1)}, bf16[1024,128]{1,0:T(8,128)(2,1)S(1)}, u32[]{:S(2)}, u32[]{:S(2)}) collective-permute-start(bf16[1024,128]{1,0:T(8,128)(2,1)S(1)} %get-tuple-element.34.q_ref), channel_id=1, source_target_pairs={{0,1},{1,0},{2,3},{3,2},{4,5},{5,4},{6,7},{7,6},{8,9},{9,8},{10,11... | collective-permute-start | bytes 786440 | tf_op jit(solution)/shard_map/ppermute | solution.py:41
  12.6 2.4 %collective-permute-start.3 = (bf16[1024,128]{1,0:T(8,128)(2,1)S(1)}, bf16[1024,128]{1,0:T(8,128)(2,1)S(1)}, u32[]{:S(2)}, u32[]{:S(2)}) collective-permute-start(bf16[1024,128]{1,0:T(8,128)(2,1)S(1)} %get-tuple-element.35.g_ref), channel_id=1, source_target_pairs={{0,1},{1,0},{2,3},{3,2},{4,5},{5,4},{6,7},{7,6},{8,9},{9,8},{10,11... | collective-permute-start | bytes 786440 | tf_op jit(solution)/shard_map/ppermute | solution.py:41
  14.5 1.3 %collective-permute-start.6 = (f32[4,1024]{1,0:T(4,128)S(1)}, f32[4,1024]{1,0:T(4,128)S(1)}, u32[]{:S(2)}, u32[]{:S(2)}) collective-permute-start(f32[4,1024]{1,0:T(4,128)S(1)} %get-tuple-element.40.stats_ref), channel_id=1, source_target_pairs={{0,1},{1,0},{2,3},{3,2},{4,5},{5,4},{6,7},{7,6},{8,9},{9,8},{10,11... | collective-permute-start | bytes 49160 | tf_op jit(solution)/shard_map/ppermute | solution.py:41
  16.6 6.2 %collective-permute-start.8 = (bf16[128,256]{1,0:T(8,128)(2,1)S(1)}, bf16[128,256]{1,0:T(8,128)(2,1)S(1)}, u32[]{:S(2)}, u32[]{:S(2)}) collective-permute-start(bf16[128,256]{1,0:T(8,128)(2,1)S(1)} %get-tuple-element.45), channel_id=1, source_target_pairs={{7,0},{4,1},{17,2},{6,3},{19,4},{16,5},{21,6},{18,7},{23,16},{20,1... | collective-permute-start | bytes 196616 | tf_op jit(solution)/shard_map/ppermute | solution.py:52
  18.8 8.0 %collective-permute-start.9 = (bf16[128,256]{1,0:T(8,128)(2,1)S(1)}, bf16[128,256]{1,0:T(8,128)(2,1)S(1)}, u32[]{:S(2)}, u32[]{:S(2)}) collective-permute-start(bf16[128,256]{1,0:T(8,128)(2,1)S(1)} %get-tuple-element.46), channel_id=1, source_target_pairs={{3,0},{16,1},{5,2},{18,3},{7,4},{20,5},{17,6},{22,7},{19,16},{32,1... | collective-permute-start | bytes 196616 | tf_op jit(solution)/shard_map/ppermute | solution.py:52
  22.1 4.8 %collective-permute-start.13 = (bf16[320,128]{1,0:T(8,128)(2,1)S(1)}, bf16[320,128]{1,0:T(8,128)(2,1)S(1)}, u32[]{:S(2)}, u32[]{:S(2)}) collective-permute-start(bf16[320,128]{1,0:T(8,128)(2,1)S(1)} %get-tuple-element.55), channel_id=1, source_target_pairs={{0,1},{1,0},{2,3},{3,2},{4,5},{5,4},{6,7},{7,6},{8,9},{9,8},{10,11... | collective-permute-start | bytes 245768 | tf_op jit(solution)/shard_map/ppermute | solution.py:41
  22.3 4.6 %collective-permute-start.11 = (bf16[352,128]{1,0:T(8,128)(2,1)S(1)}, bf16[352,128]{1,0:T(8,128)(2,1)S(1)}, u32[]{:S(2)}, u32[]{:S(2)}) collective-permute-start(bf16[352,128]{1,0:T(8,128)(2,1)S(1)} %get-tuple-element.53), channel_id=1, source_target_pairs={{0,1},{1,0},{2,3},{3,2},{4,5},{5,4},{6,7},{7,6},{8,9},{9,8},{10,11... | collective-permute-start | bytes 270344 | tf_op jit(solution)/shard_map/ppermute | solution.py:41
  22.7 4.2 %collective-permute-start.12 = (bf16[352,128]{1,0:T(8,128)(2,1)S(1)}, bf16[352,128]{1,0:T(8,128)(2,1)S(1)}, u32[]{:S(2)}, u32[]{:S(2)}) collective-permute-start(bf16[352,128]{1,0:T(8,128)(2,1)S(1)} %get-tuple-element.54), channel_id=1, source_target_pairs={{0,1},{1,0},{2,3},{3,2},{4,5},{5,4},{6,7},{7,6},{8,9},{9,8},{10,11... | collective-permute-start | bytes 270344 | tf_op jit(solution)/shard_map/ppermute | solution.py:41
  26.8 1.3 %collective-permute-start.10 = (bf16[64,256]{1,0:T(8,128)(2,1)S(1)}, bf16[64,256]{1,0:T(8,128)(2,1)S(1)}, u32[]{:S(2)}, u32[]{:S(2)}) collective-permute-start(bf16[64,256]{1,0:T(8,128)(2,1)S(1)} %slice.22), channel_id=1, source_target_pairs={{0,1},{1,0},{2,3},{3,2},{4,5},{5,4},{6,7},{7,6},{8,9},{9,8},{10,11... | collective-permute-start | bytes 98312 | tf_op jit(solution)/shard_map/ppermute | solution.py:41

commit v6 on v5

--- a/solution.py
+++ b/solution.py
@@ -24,8 +24,10 @@
 SCALING = 1.0 / math.sqrt(DH)
 EXP2_SCALING = SCALING * math.log2(math.e)
 AXES = ("blk", "uly")
-STEPS = ((1, 4), (3, 2))
-CROSS = (1, 1)
+MOVES = (
+    ((1, 4), (0, 0, 0, 1), (1, 0, 0, 0)),
+    ((3, 2), (0, 1, 0, 0), (0, 0, 1, 0)),
+)
 PIECES = (0, 352, 704, COLS)
 KEY_COLS, VALUE_COLS = slice(0, DH), slice(DH, 2 * DH)
 
@@ -42,14 +44,22 @@
 
 
 def move_chips(x, number, forward):
-    steps, cross = STEPS[number], CROSS[number]
+    steps, sends, takes = MOVES[number]
     pairs = []
-    for chunk in range(CHUNKS):
-        chip, core = divmod(chunk, 2)
-        target = (chip + steps[core]) % CHIPS
-        pair = (device_of(chunk), device_of(2 * target + (core ^ cross)))
-        pairs.append(pair if forward else pair[::-1])
+    for chip in range(CHIPS):
+        for other, step in enumerate(steps):
+            target = (chip + step) % CHIPS
+            source = 2 * chip + (sends[chip % 4] ^ other)
+            pair = (device_of(source), device_of(2 * target + (takes[target % 4] ^ other)))
+            pairs.append(pair if forward else pair[::-1])
     return lax.ppermute(x, AXES, pairs)
+
+
+def entry(table, index):
+    value = table[3]
+    for i in range(3):
+        value = jnp.where(index == i, table[i], value)
+    return value
 
 
 def dot(a, b, contract):
@@ -97,8 +107,13 @@
     return weights, top, jnp.sum(folded(weights, jnp.sum), axis=0, keepdims=True)
 
 
-def prepare_kernel(q_ref, o_ref, g_ref, len_ref, own_ref,
-                   q2_ref, g2_ref, dot_ref, bias_ref, e_ref, top_ref, sum_ref):
+def layout_kernel(q_ref, q2_ref):
+    for h in range(HQ):
+        q2_ref[h * ROWS : (h + 1) * ROWS, :] = q_ref[:, h * DH : (h + 1) * DH]
+
+
+def prepare_kernel(q2_ref, o_ref, g_ref, len_ref, own_ref,
+                   g2_ref, dot_ref, bias_ref, e_ref, top_ref, sum_ref):
     blk = lax.axis_index("blk")
     uly = lax.axis_index("uly")
     core = lax.rem(uly, 2)
@@ -112,7 +127,6 @@
         cols = slice(h * DH, (h + 1) * DH)
         rows = slice(h * ROWS, (h + 1) * ROWS)
         grad = g_ref[:, cols]
-        q2_ref[rows, :] = q_ref[:, cols]
         g2_ref[rows, :] = grad
         prod = grad.astype(jnp.float32) * o_ref[:, cols].astype(jnp.float32)
         high = prod.astype(jnp.bfloat16)
@@ -128,9 +142,15 @@
     first = jnp.max(jnp.where(starts <= here, starts, 0), axis=0, keepdims=True)
     index = lax.broadcasted_iota(jnp.int32, (ROWS, DH), 0)
     chunks = []
-    for steps, cross in zip(STEPS, CROSS):
-        source = 1 - core if cross else core
-        past = 2 * (chip - jnp.where(source == 0, steps[0], steps[1]))
+    place = lax.rem(chip, 4)
+    for (first_step, second_step), sends, takes in MOVES:
+        is_first = core == entry(takes, place)
+        source = jnp.where(
+            is_first,
+            entry([sends[(y - first_step) % 4] for y in range(4)], place),
+            entry([1 - sends[(y - second_step) % 4] for y in range(4)], place),
+        )
+        past = 2 * (chip - jnp.where(is_first, first_step, second_step))
         chunks += [past + source, past + 1 - source]
     for part, key_chunk in enumerate(chunks + [chunk, 2 * chip + 1 - core]):
         where = key_chunk * ROWS + index
@@ -279,13 +299,15 @@
     own = call(pack_kernel, [shape((CHIP_ROWS, 2 * DH), bf16)])(mine, *other)[0]
     fetched = [move_chips(own, number, True) for number in range(2)]
     columns = 2 * COLS
-    q2, g2, row_dot, bias, own_weights, own_top, own_sum = call(
+    q2 = call(layout_kernel, [shape((COLS, DH), bf16)], flops=10**8)(query_rows)[0]
+    g2, row_dot, bias, own_weights, own_top, own_sum = call(
         prepare_kernel,
-        [shape((COLS, DH), bf16), shape((COLS, DH), bf16), shape((1, COLS), f32),
+        [shape((COLS, DH), bf16), shape((1, COLS), f32),
          shape((PAST + CHIP_ROWS, DH), bf16), shape((CHIP_ROWS, COLS), f32), shape((1, COLS), f32),
          shape((1, COLS), f32)],
-    )(query_rows, saved_out, out_grad, doc_lengths.reshape(1, 64), own)
-    keys = call(keys_kernel, [shape((PAST, 2 * DH), bf16)], flops=3 * 10**9)(*fetched, bias)[0]
+        flops=10**8,
+    )(q2, saved_out, out_grad, doc_lengths.reshape(1, 64), own)
+    keys = call(keys_kernel, [shape((PAST, 2 * DH), bf16)], flops=4 * 10**9)(*fetched, bias)[0]
     q3, g3, far_dot = (swap_cores(x) for x in (q2, g2, row_dot))
     weights, tops, stats = call(
         score_kernel, [shape((PAST, columns), f32), shape((2, columns), f32), shape((4, COLS), f32)]

time: 28.9 us -> 28.8 us (level)
  waiting for transfers between devices: 6.31 us -> 5.44 us
  starting transfers between devices: 15.9 us -> 16.6 us
    ppermute x10, waiting for transfers between devices: 2.38 us -> 1.54 us  [swap_cores(): return lax.ppermute(x, 'uly', [(i, i ^ 1) for i in range(16)])]
    ppermute x10, starting transfers between devices: 2.8 us -> 3.4 us  [swap_cores(): return lax.ppermute(x, 'uly', [(i, i ^ 1) for i in range(16)])]
    pallas_call x8 -> x9, Pallas kernels: 4.35 us -> 4.37 us  [call(): pl.pallas_call(kernel, out_shape=outs, in_specs=[vmem] * len(args), out_s...]
  transfers between devices with their start and end apart: 14 -> 14, of which waited for: 6 -> 7; matrix products, arithmetic and copies ran while one was open for 3% -> 3% of each run, Pallas kernels for 12% -> 12%
where the time goes in v6:
time: 28.8 us; the launch traced here: 28.6 us
  starting transfers between devices  16.6 us (58%)
  waiting for transfers between devices  5.44 us (19%)
  Pallas kernels  4.37 us (15%)
  other arithmetic  0.77 us (3%)
  between operations  0.77 us (3%)
  local copies, waits for them, and re-layouts  0.64 us (2%)
    ppermute x4, starting transfers between devices, move_chips(): return lax.ppermute(x, AXES, pairs)  13.2 us
    pallas_call x9, Pallas kernels, call(): pl.pallas_call(kernel, out_shape=outs, in_specs=[vmem] * len(args), out_s...  4.37 us
    ppermute x4, waiting for transfers between devices, move_chips(): return lax.ppermute(x, AXES, pairs)  3.9 us
    ppermute x10, starting transfers between devices, swap_cores(): return lax.ppermute(x, 'uly', [(i, i ^ 1) for i in range(16)])  3.4 us
    ppermute x10, waiting for transfers between devices, swap_cores(): return lax.ppermute(x, 'uly', [(i, i ^ 1) for i in range(16)])  1.54 us
    concatenate x1, other arithmetic, on_device(): mine = jnp.concatenate([key_rows, value_rows], axis=1)  0.74 us
    slice x1, local copies, waits for them, and re-layouts, on_device(): return (query_grad, result[:, :DH], result[:, DH:])  0.62 us
  transfers between devices with their start and end apart: 14, of which 7 were waited for; matrix products, arithmetic and copies ran while one was open for 3% of the time, Pallas kernels for 12%

profile of v6, /device:TPU:39, one launch (start us, length us, event | category | flops | bytes accessed | tf_op | source)
XLA Modules:
  0.0 28.6 jit_solution(13272450501086570669)
XLA Ops:
  0.6 0.8 %collective-permute-start.1 = (bf16[64,128]{1,0:T(8,128)(2,1)}, bf16[64,128]{1,0:T(8,128)(2,1)S(1)}, u32[]{:S(2)}, u32[]{:S(2)}) collective-permute-start(bf16[64,128]{1,0:T(8,128)(2,1)} %param.7), channel_id=1, source_target_pairs={{0,1},{1,0},{2,3},{3,2},{4,5},{5,4},{6,7},{7,6},{8,9},{9,8},{10,11... | collective-permute-start | bytes 49160 | tf_op jit(solution)/shard_map/ppermute | solution.py:43
  1.5 0.7 %pad_maximum_fusion.mine_ref = bf16[64,256]{1,0:T(8,128)(2,1)S(1)} fusion(bf16[64,128]{1,0:T(8,128)(2,1)} %param.8, bf16[64,128]{1,0:T(8,128)(2,1)} %param.7), kind=kLoop, calls=%fused_computation.3 | loop fusion | flops 65536 | bytes 65536 | tf_op jit(solution)/shard_map/concatenate | solution.py:297
  2.3 0.2 collective-permute-done.1.other_k_ref
  2.5 0.3 %collective-permute-done.2.other_v_ref = bf16[64,128]{1,0:T(8,128)(2,1)S(1)} collective-permute-done((bf16[64,128]{1,0:T(8,128)(2,1)}, bf16[64,128]{1,0:T(8,128)(2,1)S(1)}, u32[]{:S(2)}, u32[]{:S(2)}) %collective-permute-start.2) | collective-permute-done | bytes 16416 | tf_op jit(solution)/shard_map/ppermute | solution.py:43
  2.8 3.1 %collective-permute-start.5 = (bf16[128,256]{1,0:T(8,128)(2,1)S(1)}, bf16[128,256]{1,0:T(8,128)(2,1)S(1)}, u32[]{:S(2)}, u32[]{:S(2)}) collective-permute-start(bf16[128,256]{1,0:T(8,128)(2,1)S(1)} %shard_map.86.own_ref), channel_id=1, source_target_pairs={{0,6},{1,4},{3,16},{2,7},{4,18},{5,17},{6,21},{7,19},{16,22},{17,2... | collective-permute-start | bytes 196616 | tf_op jit(solution)/shard_map/ppermute | solution.py:55
  5.9 5.5 %collective-permute-start.4 = (bf16[128,256]{1,0:T(8,128)(2,1)S(1)}, bf16[128,256]{1,0:T(8,128)(2,1)S(1)}, u32[]{:S(2)}, u32[]{:S(2)}) collective-permute-start(bf16[128,256]{1,0:T(8,128)(2,1)S(1)} %shard_map.86.own_ref), channel_id=1, source_target_pairs={{0,2},{1,16},{2,4},{3,19},{4,6},{5,21},{7,17},{6,23},{16,18},{17,3... | collective-permute-start | bytes 196616 | tf_op jit(solution)/shard_map/ppermute | solution.py:55
  11.5 0.7 %shard_map.87 = (bf16[1024,128]{1,0:T(8,128)(2,1)S(1)}, f32[1,1024]{1,0:T(1,128)S(1)}, bf16[384,128]{1,0:T(8,128)(2,1)S(1)}, f32[128,1024]{1,0:T(8,128)S(1)}, f3...) custom-call(bf16[1024,128]{1,0:T(8,128)(2,1)S(1)} %shard_map.85.q2_ref.q_ref, bf16[64,2048]{1,0:T(8,128)(2,1)S(1)} %copy-done, ...), custom_call_target="tpu_custom_call" | custom-call | flops 100000000 | bytes 200000 | tf_op jit(solution)/shard_map/pallas_call | solution.py:281
  12.2 0.6 %collective-permute-start.7 = (f32[1,1024]{1,0:T(1,128)S(1)}, f32[1,1024]{1,0:T(1,128)S(1)}, u32[]{:S(2)}, u32[]{:S(2)}) collective-permute-start(f32[1,1024]{1,0:T(1,128)S(1)} %get-tuple-element.39.dot_ref), channel_id=1, source_target_pairs={{0,1},{1,0},{2,3},{3,2},{4,5},{5,4},{6,7},{7,6},{8,9},{9,8},{10,11... | collective-permute-start | bytes 12296 | tf_op jit(solution)/shard_map/ppermute | solution.py:43
  12.9 0.1 collective-permute-done.partner_q_ref
  13.0 0.7 %shard_map.89 = (f32[256,2048]{1,0:T(8,128)S(1)}, f32[2,2048]{1,0:T(2,128)S(1)}, f32[4,1024]{1,0:T(4,128)S(1)}) custom-call(bf16[1024,128]{1,0:T(8,128)(2,1)S(1)} %shard_map.85.q2_ref.q_ref, bf16[1024,128]{1,0:T(8,128)(2,1)S(1)} %collective-permute-done.partner_q_ref, bf16[256,256]{1,0:T(8,128)(2,1)S(1)} %shard_map.88.keys_ref, ...), custom_call_target="tpu_custom_call" | custom-call | flops 1000000000 | bytes 2000000 | tf_op jit(solution)/shard_map/pallas_call | solution.py:281
  13.7 0.4 %collective-permute-start.6 = (f32[4,1024]{1,0:T(4,128)S(1)}, f32[4,1024]{1,0:T(4,128)S(1)}, u32[]{:S(2)}, u32[]{:S(2)}) collective-permute-start(f32[4,1024]{1,0:T(4,128)S(1)} %get-tuple-element.38.stats_ref), channel_id=1, source_target_pairs={{0,1},{1,0},{2,3},{3,2},{4,5},{5,4},{6,7},{7,6},{8,9},{9,8},{10,11... | collective-permute-start | bytes 49160 | tf_op jit(solution)/shard_map/ppermute | solution.py:43
  14.1 0.2 collective-permute-done.3.partner_g_ref
  14.3 0.4 %shard_map.90.u_ref = f32[256,2048]{1,0:T(8,128)S(1)} custom-call(bf16[1024,128]{1,0:T(8,128)(2,1)S(1)} %get-tuple-element.33.g_ref, bf16[1024,128]{1,0:T(8,128)(2,1)S(1)} %collective-permute-done.3.partner_g_ref, f32[1,1024]{1,0:T(1,128)S(1)} %get-tuple-element.39.dot_ref, f32[1,1024]{1,0:T(1,128)S(1)} %collective-permute-done.7.partner_dot_ref, ...), custom_call_target="tpu_custom_call" | custom-call | flops 1000000000 | bytes 2000000 | tf_op jit(solution)/shard_map/pallas_call | solution.py:281
  14.7 0.3 %collective-permute-done.6.far_ref = f32[4,1024]{1,0:T(4,128)S(1)} collective-permute-done((f32[4,1024]{1,0:T(4,128)S(1)}, f32[4,1024]{1,0:T(4,128)S(1)}, u32[]{:S(2)}, u32[]{:S(2)}) %collective-permute-start.6) | collective-permute-done | bytes 16416 | tf_op jit(solution)/shard_map/ppermute | solution.py:43
  15.0 0.8 %shard_map.91 = (bf16[128,256]{1,0:T(8,128)(2,1)S(1)}, bf16[128,256]{1,0:T(8,128)(2,1)S(1)}, bf16[256,2048]{1,0:T(8,128)(2,1)S(1)}, f32[2,2048]{1,0:T(2,128)S(1)}) custom-call(bf16[1024,128]{1,0:T(8,128)(2,1)S(1)} %shard_map.85.q2_ref.q_ref, bf16[1024,128]{1,0:T(8,128)(2,1)S(1)} %collective-permute-done.partner_q_ref, ...), custom_call_target="tpu_custom_call" | custom-call | flops 1000000000 | bytes 2000000 | tf_op jit(solution)/shard_map/pallas_call | solution.py:281
  15.8 2.9 %collective-permute-start.8 = (bf16[128,256]{1,0:T(8,128)(2,1)S(1)}, bf16[128,256]{1,0:T(8,128)(2,1)S(1)}, u32[]{:S(2)}, u32[]{:S(2)}) collective-permute-start(bf16[128,256]{1,0:T(8,128)(2,1)S(1)} %get-tuple-element.43), channel_id=1, source_target_pairs={{6,0},{4,1},{16,3},{7,2},{18,4},{17,5},{21,6},{19,7},{22,16},{20,1... | collective-permute-start | bytes 196616 | tf_op jit(solution)/shard_map/ppermute | solution.py:55
  18.8 1.8 %collective-permute-start.9 = (bf16[128,256]{1,0:T(8,128)(2,1)S(1)}, bf16[128,256]{1,0:T(8,128)(2,1)S(1)}, u32[]{:S(2)}, u32[]{:S(2)}) collective-permute-start(bf16[128,256]{1,0:T(8,128)(2,1)S(1)} %get-tuple-element.44), channel_id=1, source_target_pairs={{2,0},{16,1},{4,2},{19,3},{6,4},{21,5},{17,7},{23,6},{18,16},{32,1... | collective-permute-start | bytes 196616 | tf_op jit(solution)/shard_map/ppermute | solution.py:55
  20.5 0.9 %shard_map.92 = (f32[1024,128]{1,0:T(8,128)S(1)}, f32[128,256]{1,0:T(8,128)S(1)}, bf16[352,128]{1,0:T(8,128)(2,1)S(1)}, bf16[352,128]{1,0:T(8,128)(2,1)S(1)}, bf16[320,128]{1,0:T(8,128)(2,1)S(1)}) custom-call(bf16[1024,128]{1,0:T(8,128)(2,1)S(1)} %shard_map.85.q2_ref.q_ref, bf16[1024,128]{1,0:T(8,128)(2,1)S(1)} %get-tuple-element.33.g_ref, ...), custom_call_target="tpu_custom_call" | custom-call | flops 1000000000 | bytes 2000000 | tf_op jit(solution)/shard_map/pallas_call | solution.py:281
  21.4 0.8 %collective-permute-start.13 = (bf16[320,128]{1,0:T(8,128)(2,1)S(1)}, bf16[320,128]{1,0:T(8,128)(2,1)S(1)}, u32[]{:S(2)}, u32[]{:S(2)}) collective-permute-start(bf16[320,128]{1,0:T(8,128)(2,1)S(1)} %get-tuple-element.53), channel_id=1, source_target_pairs={{0,1},{1,0},{2,3},{3,2},{4,5},{5,4},{6,7},{7,6},{8,9},{9,8},{10,11... | collective-permute-start | bytes 245768 | tf_op jit(solution)/shard_map/ppermute | solution.py:43
  22.4 0.4 %collective-permute-start.12 = (bf16[352,128]{1,0:T(8,128)(2,1)S(1)}, bf16[352,128]{1,0:T(8,128)(2,1)S(1)}, u32[]{:S(2)}, u32[]{:S(2)}) collective-permute-start(bf16[352,128]{1,0:T(8,128)(2,1)S(1)} %get-tuple-element.52), channel_id=1, source_target_pairs={{0,1},{1,0},{2,3},{3,2},{4,5},{5,4},{6,7},{7,6},{8,9},{9,8},{10,11... | collective-permute-start | bytes 270344 | tf_op jit(solution)/shard_map/ppermute | solution.py:43
  22.8 3.9 %collective-permute-done.9 = bf16[128,256]{1,0:T(8,128)(2,1)S(1)} collective-permute-done((bf16[128,256]{1,0:T(8,128)(2,1)S(1)}, bf16[128,256]{1,0:T(8,128)(2,1)S(1)}, u32[]{:S(2)}, u32[]{:S(2)}) %collective-permute-start.9) | collective-permute-done | bytes 65568 | tf_op jit(solution)/shard_map/ppermute | solution.py:55
  26.8 0.8 %shard_map.93 = bf16[64,2048]{1,0:T(8,128)(2,1)} custom-call(f32[1024,128]{1,0:T(8,128)S(1)} %get-tuple-element.50.dq_ref, bf16[352,128]{1,0:T(8,128)(2,1)S(1)} %collective-permute-done.11.refs_0_, bf16[352,128]{1,0:T(8,128)(2,1)S(1)} %collective-permute-done.12.refs_1_, bf16[320,128]{1,0:T(8,128)(2,1)S(1)} %collective-permute-done.13.refs_2_), custom_call_target="tpu_custom_call" | custom-call | flops 1000000000 | bytes 2000000 | tf_op jit(solution)/shard_map/pallas_call | solution.py:281
  27.6 0.4 %collective-permute-done.10 = bf16[64,256]{1,0:T(8,128)(2,1)S(1)} collective-permute-done((bf16[64,256]{1,0:T(8,128)(2,1)S(1)}, bf16[64,256]{1,0:T(8,128)(2,1)S(1)}, u32[]{:S(2)}, u32[]{:S(2)}) %collective-permute-start.10) | collective-permute-done | bytes 32800 | tf_op jit(solution)/shard_map/ppermute | solution.py:43
  28.0 0.6 %fusion = (bf16[64,128]{1,0:T(8,128)(2,1)}, bf16[64,128]{1,0:T(8,128)(2,1)}) fusion(bf16[64,256]{1,0:T(8,128)(2,1)S(1)} %add_convert_fusion), kind=kLoop, calls=%fused_computation.4 | loop fusion | bytes 65536 | tf_op jit(solution)/shard_map/slice | solution.py:341
  (26 shorter events, 0.6 us)
Async XLA Ops:
  0.6 10.7 %copy-start.2 = (bf16[64,2048]{1,0:T(8,128)(2,1)S(1)}, bf16[64,2048]{1,0:T(8,128)(2,1)}, u32[]{:S(2)}) copy-start(bf16[64,2048]{1,0:T(8,128)(2,1)} %q_ref.1) | copy-start | bytes 786436
  0.6 1.8 %collective-permute-start.1 = (bf16[64,128]{1,0:T(8,128)(2,1)}, bf16[64,128]{1,0:T(8,128)(2,1)S(1)}, u32[]{:S(2)}, u32[]{:S(2)}) collective-permute-start(bf16[64,128]{1,0:T(8,128)(2,1)} %param.7), channel_id=1, source_target_pairs={{0,1},{1,0},{2,3},{3,2},{4,5},{5,4},{6,7},{7,6},{8,9},{9,8},{10,11... | collective-permute-start | bytes 49160 | tf_op jit(solution)/shard_map/ppermute | solution.py:43
  1.4 1.4 %collective-permute-start.2 = (bf16[64,128]{1,0:T(8,128)(2,1)}, bf16[64,128]{1,0:T(8,128)(2,1)S(1)}, u32[]{:S(2)}, u32[]{:S(2)}) collective-permute-start(bf16[64,128]{1,0:T(8,128)(2,1)} %param.8), channel_id=1, source_target_pairs={{0,1},{1,0},{2,3},{3,2},{4,5},{5,4},{6,7},{7,6},{8,9},{9,8},{10,11... | collective-permute-start | bytes 49160 | tf_op jit(solution)/shard_map/ppermute | solution.py:43
  2.2 9.3 %copy-start = (bf16[64,2048]{1,0:T(8,128)(2,1)S(1)}, bf16[64,2048]{1,0:T(8,128)(2,1)}, u32[]{:S(2)}) copy-start(bf16[64,2048]{1,0:T(8,128)(2,1)} %o_ref.1) | copy-start | bytes 786436
  2.2 9.3 %copy-start.1 = (bf16[64,2048]{1,0:T(8,128)(2,1)S(1)}, bf16[64,2048]{1,0:T(8,128)(2,1)}, u32[]{:S(2)}) copy-start(bf16[64,2048]{1,0:T(8,128)(2,1)} %g_ref.1) | copy-start | bytes 786436
  2.2 9.3 %copy-start.3 = (s32[64]{0:T(128)S(1)}, s32[64]{0:T(128)}, u32[]{:S(2)}) copy-start(s32[64]{0:T(128)} %param.11) | copy-start | bytes 772
  2.8 10.0 %collective-permute-start.5 = (bf16[128,256]{1,0:T(8,128)(2,1)S(1)}, bf16[128,256]{1,0:T(8,128)(2,1)S(1)}, u32[]{:S(2)}, u32[]{:S(2)}) collective-permute-start(bf16[128,256]{1,0:T(8,128)(2,1)S(1)} %shard_map.86.own_ref), channel_id=1, source_target_pairs={{0,6},{1,4},{3,16},{2,7},{4,18},{5,17},{6,21},{7,19},{16,22},{17,2... | collective-permute-start | bytes 196616 | tf_op jit(solution)/shard_map/ppermute | solution.py:55
  5.9 7.0 %collective-permute-start.4 = (bf16[128,256]{1,0:T(8,128)(2,1)S(1)}, bf16[128,256]{1,0:T(8,128)(2,1)S(1)}, u32[]{:S(2)}, u32[]{:S(2)}) collective-permute-start(bf16[128,256]{1,0:T(8,128)(2,1)S(1)} %shard_map.86.own_ref), channel_id=1, source_target_pairs={{0,2},{1,16},{2,4},{3,19},{4,6},{5,21},{7,17},{6,23},{16,18},{17,3... | collective-permute-start | bytes 196616 | tf_op jit(solution)/shard_map/ppermute | solution.py:55
  11.4 1.6 %collective-permute-start = (bf16[1024,128]{1,0:T(8,128)(2,1)S(1)}, bf16[1024,128]{1,0:T(8,128)(2,1)S(1)}, u32[]{:S(2)}, u32[]{:S(2)}) collective-permute-start(bf16[1024,128]{1,0:T(8,128)(2,1)S(1)} %shard_map.85.q2_ref.q_ref), channel_id=1, source_target_pairs={{0,1},{1,0},{2,3},{3,2},{4,5},{5,4},{6,7},{7,6},{8,9},{9,8},{10,11... | collective-permute-start | bytes 786440 | tf_op jit(solution)/shard_map/ppermute | solution.py:43
  12.2 1.9 %collective-permute-start.7 = (f32[1,1024]{1,0:T(1,128)S(1)}, f32[1,1024]{1,0:T(1,128)S(1)}, u32[]{:S(2)}, u32[]{:S(2)}) collective-permute-start(f32[1,1024]{1,0:T(1,128)S(1)} %get-tuple-element.39.dot_ref), channel_id=1, source_target_pairs={{0,1},{1,0},{2,3},{3,2},{4,5},{5,4},{6,7},{7,6},{8,9},{9,8},{10,11... | collective-permute-start | bytes 12296 | tf_op jit(solution)/shard_map/ppermute | solution.py:43
  12.7 1.5 %collective-permute-start.3 = (bf16[1024,128]{1,0:T(8,128)(2,1)S(1)}, bf16[1024,128]{1,0:T(8,128)(2,1)S(1)}, u32[]{:S(2)}, u32[]{:S(2)}) collective-permute-start(bf16[1024,128]{1,0:T(8,128)(2,1)S(1)} %get-tuple-element.33.g_ref), channel_id=1, source_target_pairs={{0,1},{1,0},{2,3},{3,2},{4,5},{5,4},{6,7},{7,6},{8,9},{9,8},{10,11... | collective-permute-start | bytes 786440 | tf_op jit(solution)/shard_map/ppermute | solution.py:43
  13.7 1.3 %collective-permute-start.6 = (f32[4,1024]{1,0:T(4,128)S(1)}, f32[4,1024]{1,0:T(4,128)S(1)}, u32[]{:S(2)}, u32[]{:S(2)}) collective-permute-start(f32[4,1024]{1,0:T(4,128)S(1)} %get-tuple-element.38.stats_ref), channel_id=1, source_target_pairs={{0,1},{1,0},{2,3},{3,2},{4,5},{5,4},{6,7},{7,6},{8,9},{9,8},{10,11... | collective-permute-start | bytes 49160 | tf_op jit(solution)/shard_map/ppermute | solution.py:43
  15.8 7.0 %collective-permute-start.8 = (bf16[128,256]{1,0:T(8,128)(2,1)S(1)}, bf16[128,256]{1,0:T(8,128)(2,1)S(1)}, u32[]{:S(2)}, u32[]{:S(2)}) collective-permute-start(bf16[128,256]{1,0:T(8,128)(2,1)S(1)} %get-tuple-element.43), channel_id=1, source_target_pairs={{6,0},{4,1},{16,3},{7,2},{18,4},{17,5},{21,6},{19,7},{22,16},{20,1... | collective-permute-start | bytes 196616 | tf_op jit(solution)/shard_map/ppermute | solution.py:55
  18.8 7.9 %collective-permute-start.9 = (bf16[128,256]{1,0:T(8,128)(2,1)S(1)}, bf16[128,256]{1,0:T(8,128)(2,1)S(1)}, u32[]{:S(2)}, u32[]{:S(2)}) collective-permute-start(bf16[128,256]{1,0:T(8,128)(2,1)S(1)} %get-tuple-element.44), channel_id=1, source_target_pairs={{2,0},{16,1},{4,2},{19,3},{6,4},{21,5},{17,7},{23,6},{18,16},{32,1... | collective-permute-start | bytes 196616 | tf_op jit(solution)/shard_map/ppermute | solution.py:55
  21.4 5.4 %collective-permute-start.13 = (bf16[320,128]{1,0:T(8,128)(2,1)S(1)}, bf16[320,128]{1,0:T(8,128)(2,1)S(1)}, u32[]{:S(2)}, u32[]{:S(2)}) collective-permute-start(bf16[320,128]{1,0:T(8,128)(2,1)S(1)} %get-tuple-element.53), channel_id=1, source_target_pairs={{0,1},{1,0},{2,3},{3,2},{4,5},{5,4},{6,7},{7,6},{8,9},{9,8},{10,11... | collective-permute-start | bytes 245768 | tf_op jit(solution)/shard_map/ppermute | solution.py:43
  22.3 4.6 %collective-permute-start.11 = (bf16[352,128]{1,0:T(8,128)(2,1)S(1)}, bf16[352,128]{1,0:T(8,128)(2,1)S(1)}, u32[]{:S(2)}, u32[]{:S(2)}) collective-permute-start(bf16[352,128]{1,0:T(8,128)(2,1)S(1)} %get-tuple-element.51), channel_id=1, source_target_pairs={{0,1},{1,0},{2,3},{3,2},{4,5},{5,4},{6,7},{7,6},{8,9},{9,8},{10,11... | collective-permute-start | bytes 270344 | tf_op jit(solution)/shard_map/ppermute | solution.py:43
  22.4 4.5 %collective-permute-start.12 = (bf16[352,128]{1,0:T(8,128)(2,1)S(1)}, bf16[352,128]{1,0:T(8,128)(2,1)S(1)}, u32[]{:S(2)}, u32[]{:S(2)}) collective-permute-start(bf16[352,128]{1,0:T(8,128)(2,1)S(1)} %get-tuple-element.52), channel_id=1, source_target_pairs={{0,1},{1,0},{2,3},{3,2},{4,5},{5,4},{6,7},{7,6},{8,9},{9,8},{10,11... | collective-permute-start | bytes 270344 | tf_op jit(solution)/shard_map/ppermute | solution.py:43
  26.7 1.3 %collective-permute-start.10 = (bf16[64,256]{1,0:T(8,128)(2,1)S(1)}, bf16[64,256]{1,0:T(8,128)(2,1)S(1)}, u32[]{:S(2)}, u32[]{:S(2)}) collective-permute-start(bf16[64,256]{1,0:T(8,128)(2,1)S(1)} %slice.22), channel_id=1, source_target_pairs={{0,1},{1,0},{2,3},{3,2},{4,5},{5,4},{6,7},{7,6},{8,9},{9,8},{10,11... | collective-permute-start | bytes 98312 | tf_op jit(solution)/shard_map/ppermute | solution.py:43

commit v7 on v6

--- a/solution.py
+++ b/solution.py
@@ -173,8 +173,9 @@
 GROUPS = (slice(0, CHIP_ROWS), slice(CHIP_ROWS, PAST))
 
 
-def score_kernel(q_ref, partner_q_ref, keys_ref, own_top_ref, own_sum_ref,
+def score_kernel(q_ref, partner_q_ref, keys_ref, own_top_ref, own_sum_ref, dot_ref,
                  e_ref, tops_ref, stats_ref):
+    stats_ref[4:5, :] = dot_ref[...]
     for side, ref in enumerate((q_ref, partner_q_ref)):
         e_ref[:, side * COLS : (side + 1) * COLS] = dot_nt(keys_ref[...], query_tile(ref[...], side))
     for at in range(0, 2 * COLS, DH):
@@ -196,19 +197,32 @@
         )
 
 
-def slope_kernel(g_ref, partner_g_ref, dot_ref, partner_dot_ref, a_ref, b_ref, u_ref):
+def slope_kernel(g_ref, partner_g_ref, a_ref, b_ref, u_ref):
     values = jnp.concatenate([a_ref[:, VALUE_COLS], b_ref[:, VALUE_COLS]], axis=0)
     for cols, side, rows in tiles():
-        grad = (g_ref, partner_g_ref)[side][rows, :]
-        u_ref[:, cols] = dot_nt(values, grad) - (dot_ref, partner_dot_ref)[side][:, rows]
+        u_ref[:, cols] = dot_nt(values, (g_ref, partner_g_ref)[side][rows, :])
 
 
 def dot_sides(left_ref, own_ref, partner_ref):
     return dot_nn(left_ref[:, :COLS], own_ref[...]) + dot_nn(left_ref[:, COLS:], partner_ref[...])
 
 
+def weigh(e_ref, u_ref, factors, row_dots, side, group, ds_ref, p_ref):
+    for start in range(0, COLS, TILE):
+        cols = slice(side * COLS + start, side * COLS + start + TILE)
+        weights = e_ref[group, cols] * factors[:, start : start + TILE]
+        slopes = u_ref[group, cols] - row_dots[:, start : start + TILE]
+        ds_ref[:, cols] = (weights * slopes).astype(jnp.bfloat16)
+        p_ref[:, cols] = weights.astype(jnp.bfloat16)
+
+
+def key_sums(q_ref, partner_q_ref, g_ref, partner_g_ref, ds_ref, p_ref, part_ref):
+    part_ref[:, KEY_COLS] = (dot_sides(ds_ref, q_ref, partner_q_ref) * SCALING).astype(jnp.bfloat16)
+    part_ref[:, VALUE_COLS] = dot_sides(p_ref, g_ref, partner_g_ref).astype(jnp.bfloat16)
+
+
 def main_kernel(q_ref, partner_q_ref, g_ref, partner_g_ref, e_ref, u_ref, tops_ref, stats_ref, far_ref,
-                a_ref, b_ref, ds_ref, norm_ref, p_ref):
+                part_ref, ds_ref, norm_ref, factors_ref, p_ref):
     for side in range(2):
         near, far = 2 * side, 2 - 2 * side
         top, far_top = stats_ref[near : near + 1, :], far_ref[far : far + 1, :]
@@ -220,25 +234,32 @@
         norm_ref[0:1, columns] = most
         norm_ref[1:2, columns] = total
         factors = jnp.exp2((tops_ref[:, columns] - most) * EXP2_SCALING) * (1.0 / total)
-        for start in range(0, COLS, TILE):
-            cols = slice(side * COLS + start, side * COLS + start + TILE)
-            for i, group in enumerate(GROUPS):
-                weights = e_ref[group, cols] * factors[i : i + 1, start : start + TILE]
-                ds_ref[group, cols] = (weights * u_ref[group, cols]).astype(jnp.bfloat16)
-                p_ref[group, cols] = weights.astype(jnp.bfloat16)
-    key_grads = (dot_sides(ds_ref, q_ref, partner_q_ref) * SCALING).astype(jnp.bfloat16)
-    value_grads = dot_sides(p_ref, g_ref, partner_g_ref).astype(jnp.bfloat16)
-    for ref, group in zip((a_ref, b_ref), GROUPS):
-        ref[:, KEY_COLS] = key_grads[group]
-        ref[:, VALUE_COLS] = value_grads[group]
-
-
-def finish_kernel(q_ref, g_ref, dot_ref, own_e_ref, own_top_ref, norm_ref, ds_ref, own_ref, a_ref, b_ref,
+        row_dots = (stats_ref, far_ref)[side][4:5, :]
+        factors_ref[0:1, columns] = factors[0:1]
+        factors_ref[1:2, columns] = row_dots
+        weigh(e_ref, u_ref, factors[1:2], row_dots, side, GROUPS[1], ds_ref, p_ref)
+    key_sums(q_ref, partner_q_ref, g_ref, partner_g_ref, ds_ref, p_ref, part_ref)
+
+
+def rest_kernel(q_ref, partner_q_ref, g_ref, partner_g_ref, e_ref, u_ref, factors_ref,
+                part_ref, ds_ref, p_ref):
+    for side in range(2):
+        factors = factors_ref[:, side * COLS : (side + 1) * COLS]
+        weigh(e_ref, u_ref, factors[0:1], factors[1:2], side, GROUPS[0], ds_ref, p_ref)
+    key_sums(q_ref, partner_q_ref, g_ref, partner_g_ref, ds_ref, p_ref, part_ref)
+
+
+def total_kernel(back_ref, own_ref, total_ref):
+    total_ref[...] = back_ref[...].astype(jnp.float32) + own_ref[...]
+
+
+def finish_kernel(q_ref, g_ref, dot_ref, own_e_ref, own_top_ref, norm_ref, near_ds_ref, ds_ref, own_ref, a_ref, b_ref,
                   dq_ref, own_sum_ref, *rest):
     *piece_refs, own_p_ref, own_ds_ref = rest
     past_keys = jnp.concatenate([a_ref[:, KEY_COLS], b_ref[:, KEY_COLS]], axis=0)
     for cols, side, rows in reversed(list(tiles())):
-        grads = dot_tn(past_keys, ds_ref[:, cols])
+        ds = jnp.concatenate([near_ds_ref[:, cols], ds_ref[:, cols]], axis=0)
+        grads = dot_tn(past_keys, ds)
         if side == 0:
             slopes = dot_nt(own_ref[:, VALUE_COLS], g_ref[rows, :]) - dot_ref[:, rows]
             factor = jnp.exp2((own_top_ref[:, rows] - norm_ref[0:1, rows]) * EXP2_SCALING)
@@ -308,30 +329,35 @@
         flops=10**8,
     )(q2, saved_out, out_grad, doc_lengths.reshape(1, 64), own)
     keys = call(keys_kernel, [shape((PAST, 2 * DH), bf16)], flops=4 * 10**9)(*fetched, bias)[0]
-    q3, g3, far_dot = (swap_cores(x) for x in (q2, g2, row_dot))
+    q3, g3 = swap_cores(q2), swap_cores(g2)
     weights, tops, stats = call(
-        score_kernel, [shape((PAST, columns), f32), shape((2, columns), f32), shape((4, COLS), f32)]
-    )(q2, q3, keys, own_top, own_sum)
+        score_kernel, [shape((PAST, columns), f32), shape((2, columns), f32), shape((5, COLS), f32)]
+    )(q2, q3, keys, own_top, own_sum, row_dot)
     far_stats = swap_cores(stats)
-    slopes = call(slope_kernel, [shape((PAST, columns), f32)])(
-        g2, g3, row_dot, far_dot, *fetched
-    )[0]
+    slopes = call(slope_kernel, [shape((PAST, columns), f32)])(g2, g3, *fetched)[0]
     far_stats, slopes = together((far_stats, slopes))
-    part_a, part_b, ds, norm = call(
+    part_b, ds, norm, factors = call(
         main_kernel,
-        [shape((CHIP_ROWS, 2 * DH), bf16), shape((CHIP_ROWS, 2 * DH), bf16),
-         shape((PAST, columns), bf16), shape((2, columns), f32)],
-        [pltpu.VMEM((PAST, columns), bf16)],
+        [shape((CHIP_ROWS, 2 * DH), bf16), shape((CHIP_ROWS, columns), bf16), shape((2, columns), f32),
+         shape((2, columns), f32)],
+        [pltpu.VMEM((CHIP_ROWS, columns), bf16)],
     )(q2, q3, g2, g3, weights, slopes, tops, stats, far_stats)
+    part_a, near_ds = call(
+        rest_kernel,
+        [shape((CHIP_ROWS, 2 * DH), bf16), shape((CHIP_ROWS, columns), bf16)],
+        [pltpu.VMEM((CHIP_ROWS, columns), bf16)],
+    )(q2, q3, g2, g3, weights, slopes, factors)
     back = [move_chips(part, number, False) for number, part in enumerate((part_a, part_b))]
     query_grad, own_sums, *pieces = call(
         finish_kernel,
         [shape((COLS, DH), f32), shape((CHIP_ROWS, 2 * DH), f32)]
         + [shape((high - low, DH), bf16) for low, high in zip(PIECES, PIECES[1:])],
         [pltpu.VMEM((CHIP_ROWS, COLS), bf16)] * 2,
-    )(q2, g2, row_dot, own_weights, own_top, norm, ds, own, *fetched)
+        flops=10**8,
+    )(q2, g2, row_dot, own_weights, own_top, norm, near_ds, ds, own, *fetched)
     pieces = [swap_cores(piece) for piece in pieces]
-    totals = back[1].astype(f32) + back[0].astype(f32) + own_sums
+    totals = call(total_kernel, [shape((CHIP_ROWS, 2 * DH), f32)], flops=5 * 10**9)(back[1], own_sums)[0]
+    totals = totals + back[0].astype(f32)
     far_totals = swap_cores(totals[ROWS:].astype(bf16))
     totals, query_grad = together((totals, query_grad))
     query_grad = call(add_kernel, [shape((ROWS, HQ * DH), bf16)])(query_grad, *pieces)[0]

time: 28.8 us -> 28.5 us (0.990)
  waiting for transfers between devices: 5.44 us -> 5.12 us
    ppermute x4, waiting for transfers between devices: 3.9 us -> 3.29 us  [move_chips(): return lax.ppermute(x, AXES, pairs)]
    ppermute x10 -> x9, waiting for transfers between devices: 1.54 us -> 1.82 us  [swap_cores(): return lax.ppermute(x, 'uly', [(i, i ^ 1) for i in range(16)])]
    pallas_call x9 -> x11, Pallas kernels: 4.37 us -> 4.62 us  [call(): pl.pallas_call(kernel, out_shape=outs, in_specs=[vmem] * len(args), out_s...]
    ppermute x10 -> x9, starting transfers between devices: 3.4 us -> 3.17 us  [swap_cores(): return lax.ppermute(x, 'uly', [(i, i ^ 1) for i in range(16)])]
  transfers between devices with their start and end apart: 14 -> 13, of which waited for: 7 -> 6; matrix products, arithmetic and copies ran while one was open for 3% -> 3% of each run, Pallas kernels for 12% -> 14%
where the time goes in v7:
time: 28.5 us; the launch traced here: 28.4 us
  starting transfers between devices  16.5 us (58%)
  waiting for transfers between devices  5.12 us (18%)
  Pallas kernels  4.62 us (16%)
  between operations  0.78 us (3%)
  other arithmetic  0.77 us (3%)
  local copies, waits for them, and re-layouts  0.64 us (2%)
    ppermute x4, starting transfers between devices, move_chips(): return lax.ppermute(x, AXES, pairs)  13.3 us
    pallas_call x11, Pallas kernels, call(): pl.pallas_call(kernel, out_shape=outs, in_specs=[vmem] * len(args), out_s...  4.62 us
    ppermute x4, waiting for transfers between devices, move_chips(): return lax.ppermute(x, AXES, pairs)  3.29 us
    ppermute x9, starting transfers between devices, swap_cores(): return lax.ppermute(x, 'uly', [(i, i ^ 1) for i in range(16)])  3.17 us
    ppermute x9, waiting for transfers between devices, swap_cores(): return lax.ppermute(x, 'uly', [(i, i ^ 1) for i in range(16)])  1.82 us
    concatenate x1, other arithmetic, on_device(): mine = jnp.concatenate([key_rows, value_rows], axis=1)  0.74 us
    slice x1, local copies, waits for them, and re-layouts, on_device(): return (query_grad, result[:, :DH], result[:, DH:])  0.62 us
  transfers between devices with their start and end apart: 13, of which 6 were waited for; matrix products, arithmetic and copies ran while one was open for 3% of the time, Pallas kernels for 14%

profile of v7, /device:TPU:39, one launch (start us, length us, event | category | flops | bytes accessed | tf_op | source)
XLA Modules:
  0.0 28.4 jit_solution(15599037548685229898)
XLA Ops:
  0.6 0.8 %collective-permute-start.1 = (bf16[64,128]{1,0:T(8,128)(2,1)}, bf16[64,128]{1,0:T(8,128)(2,1)S(1)}, u32[]{:S(2)}, u32[]{:S(2)}) collective-permute-start(bf16[64,128]{1,0:T(8,128)(2,1)} %param.7), channel_id=1, source_target_pairs={{0,1},{1,0},{2,3},{3,2},{4,5},{5,4},{6,7},{7,6},{8,9},{9,8},{10,11... | collective-permute-start | bytes 49160 | tf_op jit(solution)/shard_map/ppermute | solution.py:43
  1.5 0.7 %pad_maximum_fusion.mine_ref = bf16[64,256]{1,0:T(8,128)(2,1)S(1)} fusion(bf16[64,128]{1,0:T(8,128)(2,1)} %param.8, bf16[64,128]{1,0:T(8,128)(2,1)} %param.7), kind=kLoop, calls=%fused_computation.3 | loop fusion | flops 65536 | bytes 65536 | tf_op jit(solution)/shard_map/concatenate | solution.py:318
  2.3 0.2 collective-permute-done.1.other_k_ref
  2.5 0.3 %collective-permute-done.2.other_v_ref = bf16[64,128]{1,0:T(8,128)(2,1)S(1)} collective-permute-done((bf16[64,128]{1,0:T(8,128)(2,1)}, bf16[64,128]{1,0:T(8,128)(2,1)S(1)}, u32[]{:S(2)}, u32[]{:S(2)}) %collective-permute-start.2) | collective-permute-done | bytes 16416 | tf_op jit(solution)/shard_map/ppermute | solution.py:43
  2.8 3.1 %collective-permute-start.5 = (bf16[128,256]{1,0:T(8,128)(2,1)S(1)}, bf16[128,256]{1,0:T(8,128)(2,1)S(1)}, u32[]{:S(2)}, u32[]{:S(2)}) collective-permute-start(bf16[128,256]{1,0:T(8,128)(2,1)S(1)} %shard_map.86.own_ref), channel_id=1, source_target_pairs={{0,6},{1,4},{3,16},{2,7},{4,18},{5,17},{6,21},{7,19},{16,22},{17,2... | collective-permute-start | bytes 196616 | tf_op jit(solution)/shard_map/ppermute | solution.py:55
  5.9 5.5 %collective-permute-start.4 = (bf16[128,256]{1,0:T(8,128)(2,1)S(1)}, bf16[128,256]{1,0:T(8,128)(2,1)S(1)}, u32[]{:S(2)}, u32[]{:S(2)}) collective-permute-start(bf16[128,256]{1,0:T(8,128)(2,1)S(1)} %shard_map.86.own_ref), channel_id=1, source_target_pairs={{0,2},{1,16},{2,4},{3,19},{4,6},{5,21},{7,17},{6,23},{16,18},{17,3... | collective-permute-start | bytes 196616 | tf_op jit(solution)/shard_map/ppermute | solution.py:55
  11.5 0.7 %shard_map.87 = (bf16[1024,128]{1,0:T(8,128)(2,1)S(1)}, f32[1,1024]{1,0:T(1,128)S(1)}, bf16[384,128]{1,0:T(8,128)(2,1)S(1)}, f32[128,1024]{1,0:T(8,128)S(1)}, f3...) custom-call(bf16[1024,128]{1,0:T(8,128)(2,1)S(1)} %shard_map.85.q2_ref.q_ref, bf16[64,2048]{1,0:T(8,128)(2,1)S(1)} %copy-done, ...), custom_call_target="tpu_custom_call" | custom-call | flops 100000000 | bytes 200000 | tf_op jit(solution)/shard_map/pallas_call | solution.py:302
  12.2 0.6 %collective-permute-start.3 = (bf16[1024,128]{1,0:T(8,128)(2,1)S(1)}, bf16[1024,128]{1,0:T(8,128)(2,1)S(1)}, u32[]{:S(2)}, u32[]{:S(2)}) collective-permute-start(bf16[1024,128]{1,0:T(8,128)(2,1)S(1)} %get-tuple-element.35.g_ref), channel_id=1, source_target_pairs={{0,1},{1,0},{2,3},{3,2},{4,5},{5,4},{6,7},{7,6},{8,9},{9,8},{10,11... | collective-permute-start | bytes 786440 | tf_op jit(solution)/shard_map/ppermute | solution.py:43
  12.8 0.2 collective-permute-done.partner_q_ref
  13.0 0.7 %shard_map.89 = (f32[256,2048]{1,0:T(8,128)S(1)}, f32[2,2048]{1,0:T(2,128)S(1)}, f32[5,1024]{1,0:T(8,128)S(1)}) custom-call(bf16[1024,128]{1,0:T(8,128)(2,1)S(1)} %shard_map.85.q2_ref.q_ref, bf16[1024,128]{1,0:T(8,128)(2,1)S(1)} %collective-permute-done.partner_q_ref, bf16[256,256]{1,0:T(8,128)(2,1)S(1)} %shard_map.88.keys_ref, ...), custom_call_target="tpu_custom_call" | custom-call | flops 1000000000 | bytes 2000000 | tf_op jit(solution)/shard_map/pallas_call | solution.py:302
  13.7 0.2 collective-permute-start.6
  14.0 0.4 %shard_map.90.u_ref = f32[256,2048]{1,0:T(8,128)S(1)} custom-call(bf16[1024,128]{1,0:T(8,128)(2,1)S(1)} %get-tuple-element.35.g_ref, bf16[1024,128]{1,0:T(8,128)(2,1)S(1)} %collective-permute-done.3.partner_g_ref, bf16[128,256]{1,0:T(8,128)(2,1)S(1)} %collective-permute-done.4.a_ref, bf16[128,256]{1,0:T(8,128)(2,1)S(1)} %collective-permute-done.5.b_ref), custom_call_target="tpu_custom_call" | custom-call | flops 1000000000 | bytes 2000000 | tf_op jit(solution)/shard_map/pallas_call | solution.py:302
  14.4 0.6 %collective-permute-done.6.far_ref = f32[5,1024]{1,0:T(8,128)S(1)} collective-permute-done((f32[5,1024]{1,0:T(8,128)S(1)}, f32[5,1024]{1,0:T(8,128)S(1)}, u32[]{:S(2)}, u32[]{:S(2)}) %collective-permute-start.6) | collective-permute-done | bytes 20512 | tf_op jit(solution)/shard_map/ppermute | solution.py:43
  15.0 0.5 %shard_map.91 = (bf16[128,256]{1,0:T(8,128)(2,1)S(1)}, bf16[128,2048]{1,0:T(8,128)(2,1)S(1)}, f32[2,2048]{1,0:T(2,128)S(1)}, f32[2,2048]{1,0:T(2,128)S(1)}) custom-call(bf16[1024,128]{1,0:T(8,128)(2,1)S(1)} %shard_map.85.q2_ref.q_ref, bf16[1024,128]{1,0:T(8,128)(2,1)S(1)} %collective-permute-done.partner_q_ref, ...), custom_call_target="tpu_custom_call" | custom-call | flops 1000000000 | bytes 2000000 | tf_op jit(solution)/shard_map/pallas_call | solution.py:302
  15.6 2.9 %collective-permute-start.7 = (bf16[128,256]{1,0:T(8,128)(2,1)S(1)}, bf16[128,256]{1,0:T(8,128)(2,1)S(1)}, u32[]{:S(2)}, u32[]{:S(2)}) collective-permute-start(bf16[128,256]{1,0:T(8,128)(2,1)S(1)} %get-tuple-element.45), channel_id=1, source_target_pairs={{6,0},{4,1},{16,3},{7,2},{18,4},{17,5},{21,6},{19,7},{22,16},{20,1... | collective-permute-start | bytes 196616 | tf_op jit(solution)/shard_map/ppermute | solution.py:55
  18.5 0.5 %shard_map.92 = (bf16[128,256]{1,0:T(8,128)(2,1)S(1)}, bf16[128,2048]{1,0:T(8,128)(2,1)S(1)}) custom-call(bf16[1024,128]{1,0:T(8,128)(2,1)S(1)} %shard_map.85.q2_ref.q_ref, bf16[1024,128]{1,0:T(8,128)(2,1)S(1)} %collective-permute-done.partner_q_ref, bf16[1024,128]{1,0:T(8,128)(2,1)S(1)} %get-tuple-element.35.g_ref, ...), custom_call_target="tpu_custom_call" | custom-call | flops 1000000000 | bytes 2000000 | tf_op jit(solution)/shard_map/pallas_call | solution.py:302
  19.0 1.8 %collective-permute-start.8 = (bf16[128,256]{1,0:T(8,128)(2,1)S(1)}, bf16[128,256]{1,0:T(8,128)(2,1)S(1)}, u32[]{:S(2)}, u32[]{:S(2)}) collective-permute-start(bf16[128,256]{1,0:T(8,128)(2,1)S(1)} %get-tuple-element.52), channel_id=1, source_target_pairs={{2,0},{16,1},{4,2},{19,3},{6,4},{21,5},{17,7},{23,6},{18,16},{32,1... | collective-permute-start | bytes 196616 | tf_op jit(solution)/shard_map/ppermute | solution.py:55
  20.8 0.9 %shard_map.93 = (f32[1024,128]{1,0:T(8,128)S(1)}, f32[128,256]{1,0:T(8,128)S(1)}, bf16[352,128]{1,0:T(8,128)(2,1)S(1)}, bf16[352,128]{1,0:T(8,128)(2,1)S(1)}, bf16[320,128]{1,0:T(8,128)(2,1)S(1)}) custom-call(bf16[1024,128]{1,0:T(8,128)(2,1)S(1)} %shard_map.85.q2_ref.q_ref, bf16[1024,128]{1,0:T(8,128)(2,1)S(1)} %get-tuple-element.35.g_ref, ...), custom_call_target="tpu_custom_call" | custom-call | flops 100000000 | bytes 200000 | tf_op jit(solution)/shard_map/pallas_call | solution.py:302
  21.8 0.8 %collective-permute-start.12 = (bf16[320,128]{1,0:T(8,128)(2,1)S(1)}, bf16[320,128]{1,0:T(8,128)(2,1)S(1)}, u32[]{:S(2)}, u32[]{:S(2)}) collective-permute-start(bf16[320,128]{1,0:T(8,128)(2,1)S(1)} %get-tuple-element.57), channel_id=1, source_target_pairs={{0,1},{1,0},{2,3},{3,2},{4,5},{5,4},{6,7},{7,6},{8,9},{9,8},{10,11... | collective-permute-start | bytes 245768 | tf_op jit(solution)/shard_map/ppermute | solution.py:43
  22.7 0.4 %collective-permute-start.11 = (bf16[352,128]{1,0:T(8,128)(2,1)S(1)}, bf16[352,128]{1,0:T(8,128)(2,1)S(1)}, u32[]{:S(2)}, u32[]{:S(2)}) collective-permute-start(bf16[352,128]{1,0:T(8,128)(2,1)S(1)} %get-tuple-element.56), channel_id=1, source_target_pairs={{0,1},{1,0},{2,3},{3,2},{4,5},{5,4},{6,7},{7,6},{8,9},{9,8},{10,11... | collective-permute-start | bytes 270344 | tf_op jit(solution)/shard_map/ppermute | solution.py:43
  23.1 3.3 %collective-permute-done.8 = bf16[128,256]{1,0:T(8,128)(2,1)S(1)} collective-permute-done((bf16[128,256]{1,0:T(8,128)(2,1)S(1)}, bf16[128,256]{1,0:T(8,128)(2,1)S(1)}, u32[]{:S(2)}, u32[]{:S(2)}) %collective-permute-start.8) | collective-permute-done | bytes 65568 | tf_op jit(solution)/shard_map/ppermute | solution.py:55
  26.6 0.8 %shard_map.95 = bf16[64,2048]{1,0:T(8,128)(2,1)} custom-call(f32[1024,128]{1,0:T(8,128)S(1)} %get-tuple-element.54.dq_ref, bf16[352,128]{1,0:T(8,128)(2,1)S(1)} %collective-permute-done.10.refs_0_, bf16[352,128]{1,0:T(8,128)(2,1)S(1)} %collective-permute-done.11.refs_1_, bf16[320,128]{1,0:T(8,128)(2,1)S(1)} %collective-permute-done.12.refs_2_), custom_call_target="tpu_custom_call" | custom-call | flops 1000000000 | bytes 2000000 | tf_op jit(solution)/shard_map/pallas_call | solution.py:302
  27.4 0.4 %collective-permute-done.9 = bf16[64,256]{1,0:T(8,128)(2,1)S(1)} collective-permute-done((bf16[64,256]{1,0:T(8,128)(2,1)S(1)}, bf16[64,256]{1,0:T(8,128)(2,1)S(1)}, u32[]{:S(2)}, u32[]{:S(2)}) %collective-permute-start.9) | collective-permute-done | bytes 32800 | tf_op jit(solution)/shard_map/ppermute | solution.py:43
  27.8 0.6 %fusion = (bf16[64,128]{1,0:T(8,128)(2,1)}, bf16[64,128]{1,0:T(8,128)(2,1)}) fusion(bf16[64,256]{1,0:T(8,128)(2,1)S(1)} %add_convert_fusion), kind=kLoop, calls=%fused_computation.4 | loop fusion | bytes 65536 | tf_op jit(solution)/shard_map/slice | solution.py:367
  (26 shorter events, 0.5 us)
Async XLA Ops:
  0.6 10.7 %copy-start.2 = (bf16[64,2048]{1,0:T(8,128)(2,1)S(1)}, bf16[64,2048]{1,0:T(8,128)(2,1)}, u32[]{:S(2)}) copy-start(bf16[64,2048]{1,0:T(8,128)(2,1)} %q_ref.1) | copy-start | bytes 786436
  0.6 1.8 %collective-permute-start.1 = (bf16[64,128]{1,0:T(8,128)(2,1)}, bf16[64,128]{1,0:T(8,128)(2,1)S(1)}, u32[]{:S(2)}, u32[]{:S(2)}) collective-permute-start(bf16[64,128]{1,0:T(8,128)(2,1)} %param.7), channel_id=1, source_target_pairs={{0,1},{1,0},{2,3},{3,2},{4,5},{5,4},{6,7},{7,6},{8,9},{9,8},{10,11... | collective-permute-start | bytes 49160 | tf_op jit(solution)/shard_map/ppermute | solution.py:43
  1.4 1.4 %collective-permute-start.2 = (bf16[64,128]{1,0:T(8,128)(2,1)}, bf16[64,128]{1,0:T(8,128)(2,1)S(1)}, u32[]{:S(2)}, u32[]{:S(2)}) collective-permute-start(bf16[64,128]{1,0:T(8,128)(2,1)} %param.8), channel_id=1, source_target_pairs={{0,1},{1,0},{2,3},{3,2},{4,5},{5,4},{6,7},{7,6},{8,9},{9,8},{10,11... | collective-permute-start | bytes 49160 | tf_op jit(solution)/shard_map/ppermute | solution.py:43
  2.2 9.3 %copy-start = (bf16[64,2048]{1,0:T(8,128)(2,1)S(1)}, bf16[64,2048]{1,0:T(8,128)(2,1)}, u32[]{:S(2)}) copy-start(bf16[64,2048]{1,0:T(8,128)(2,1)} %o_ref.1) | copy-start | bytes 786436
  2.2 9.3 %copy-start.1 = (bf16[64,2048]{1,0:T(8,128)(2,1)S(1)}, bf16[64,2048]{1,0:T(8,128)(2,1)}, u32[]{:S(2)}) copy-start(bf16[64,2048]{1,0:T(8,128)(2,1)} %g_ref.1) | copy-start | bytes 786436
  2.2 9.3 %copy-start.3 = (s32[64]{0:T(128)S(1)}, s32[64]{0:T(128)}, u32[]{:S(2)}) copy-start(s32[64]{0:T(128)} %param.11) | copy-start | bytes 772
  2.8 9.9 %collective-permute-start.5 = (bf16[128,256]{1,0:T(8,128)(2,1)S(1)}, bf16[128,256]{1,0:T(8,128)(2,1)S(1)}, u32[]{:S(2)}, u32[]{:S(2)}) collective-permute-start(bf16[128,256]{1,0:T(8,128)(2,1)S(1)} %shard_map.86.own_ref), channel_id=1, source_target_pairs={{0,6},{1,4},{3,16},{2,7},{4,18},{5,17},{6,21},{7,19},{16,22},{17,2... | collective-permute-start | bytes 196616 | tf_op jit(solution)/shard_map/ppermute | solution.py:55
  5.9 6.9 %collective-permute-start.4 = (bf16[128,256]{1,0:T(8,128)(2,1)S(1)}, bf16[128,256]{1,0:T(8,128)(2,1)S(1)}, u32[]{:S(2)}, u32[]{:S(2)}) collective-permute-start(bf16[128,256]{1,0:T(8,128)(2,1)S(1)} %shard_map.86.own_ref), channel_id=1, source_target_pairs={{0,2},{1,16},{2,4},{3,19},{4,6},{5,21},{7,17},{6,23},{16,18},{17,3... | collective-permute-start | bytes 196616 | tf_op jit(solution)/shard_map/ppermute | solution.py:55
  11.4 1.6 %collective-permute-start = (bf16[1024,128]{1,0:T(8,128)(2,1)S(1)}, bf16[1024,128]{1,0:T(8,128)(2,1)S(1)}, u32[]{:S(2)}, u32[]{:S(2)}) collective-permute-start(bf16[1024,128]{1,0:T(8,128)(2,1)S(1)} %shard_map.85.q2_ref.q_ref), channel_id=1, source_target_pairs={{0,1},{1,0},{2,3},{3,2},{4,5},{5,4},{6,7},{7,6},{8,9},{9,8},{10,11... | collective-permute-start | bytes 786440 | tf_op jit(solution)/shard_map/ppermute | solution.py:43
  12.2 1.8 %collective-permute-start.3 = (bf16[1024,128]{1,0:T(8,128)(2,1)S(1)}, bf16[1024,128]{1,0:T(8,128)(2,1)S(1)}, u32[]{:S(2)}, u32[]{:S(2)}) collective-permute-start(bf16[1024,128]{1,0:T(8,128)(2,1)S(1)} %get-tuple-element.35.g_ref), channel_id=1, source_target_pairs={{0,1},{1,0},{2,3},{3,2},{4,5},{5,4},{6,7},{7,6},{8,9},{9,8},{10,11... | collective-permute-start | bytes 786440 | tf_op jit(solution)/shard_map/ppermute | solution.py:43
  13.7 1.3 %collective-permute-start.6 = (f32[5,1024]{1,0:T(8,128)S(1)}, f32[5,1024]{1,0:T(8,128)S(1)}, u32[]{:S(2)}, u32[]{:S(2)}) collective-permute-start(f32[5,1024]{1,0:T(8,128)S(1)} %get-tuple-element.41.stats_ref), channel_id=1, source_target_pairs={{0,1},{1,0},{2,3},{3,2},{4,5},{5,4},{6,7},{7,6},{8,9},{9,8},{10,11... | collective-permute-start | bytes 61448 | tf_op jit(solution)/shard_map/ppermute | solution.py:43
  15.6 7.5 %collective-permute-start.7 = (bf16[128,256]{1,0:T(8,128)(2,1)S(1)}, bf16[128,256]{1,0:T(8,128)(2,1)S(1)}, u32[]{:S(2)}, u32[]{:S(2)}) collective-permute-start(bf16[128,256]{1,0:T(8,128)(2,1)S(1)} %get-tuple-element.45), channel_id=1, source_target_pairs={{6,0},{4,1},{16,3},{7,2},{18,4},{17,5},{21,6},{19,7},{22,16},{20,1... | collective-permute-start | bytes 196616 | tf_op jit(solution)/shard_map/ppermute | solution.py:55
  19.0 7.4 %collective-permute-start.8 = (bf16[128,256]{1,0:T(8,128)(2,1)S(1)}, bf16[128,256]{1,0:T(8,128)(2,1)S(1)}, u32[]{:S(2)}, u32[]{:S(2)}) collective-permute-start(bf16[128,256]{1,0:T(8,128)(2,1)S(1)} %get-tuple-element.52), channel_id=1, source_target_pairs={{2,0},{16,1},{4,2},{19,3},{6,4},{21,5},{17,7},{23,6},{18,16},{32,1... | collective-permute-start | bytes 196616 | tf_op jit(solution)/shard_map/ppermute | solution.py:55
  21.8 4.8 %collective-permute-start.12 = (bf16[320,128]{1,0:T(8,128)(2,1)S(1)}, bf16[320,128]{1,0:T(8,128)(2,1)S(1)}, u32[]{:S(2)}, u32[]{:S(2)}) collective-permute-start(bf16[320,128]{1,0:T(8,128)(2,1)S(1)} %get-tuple-element.57), channel_id=1, source_target_pairs={{0,1},{1,0},{2,3},{3,2},{4,5},{5,4},{6,7},{7,6},{8,9},{9,8},{10,11... | collective-permute-start | bytes 245768 | tf_op jit(solution)/shard_map/ppermute | solution.py:43
  22.6 4.0 %collective-permute-start.10 = (bf16[352,128]{1,0:T(8,128)(2,1)S(1)}, bf16[352,128]{1,0:T(8,128)(2,1)S(1)}, u32[]{:S(2)}, u32[]{:S(2)}) collective-permute-start(bf16[352,128]{1,0:T(8,128)(2,1)S(1)} %get-tuple-element.55), channel_id=1, source_target_pairs={{0,1},{1,0},{2,3},{3,2},{4,5},{5,4},{6,7},{7,6},{8,9},{9,8},{10,11... | collective-permute-start | bytes 270344 | tf_op jit(solution)/shard_map/ppermute | solution.py:43
  22.7 3.9 %collective-permute-start.11 = (bf16[352,128]{1,0:T(8,128)(2,1)S(1)}, bf16[352,128]{1,0:T(8,128)(2,1)S(1)}, u32[]{:S(2)}, u32[]{:S(2)}) collective-permute-start(bf16[352,128]{1,0:T(8,128)(2,1)S(1)} %get-tuple-element.56), channel_id=1, source_target_pairs={{0,1},{1,0},{2,3},{3,2},{4,5},{5,4},{6,7},{7,6},{8,9},{9,8},{10,11... | collective-permute-start | bytes 270344 | tf_op jit(solution)/shard_map/ppermute | solution.py:43
  26.5 1.3 %collective-permute-start.9 = (bf16[64,256]{1,0:T(8,128)(2,1)S(1)}, bf16[64,256]{1,0:T(8,128)(2,1)S(1)}, u32[]{:S(2)}, u32[]{:S(2)}) collective-permute-start(bf16[64,256]{1,0:T(8,128)(2,1)S(1)} %slice.22), channel_id=1, source_target_pairs={{0,1},{1,0},{2,3},{3,2},{4,5},{5,4},{6,7},{7,6},{8,9},{9,8},{10,11... | collective-permute-start | bytes 98312 | tf_op jit(solution)/shard_map/ppermute | solution.py:43

commit v8 on v7

--- a/solution.py
+++ b/solution.py
@@ -18,7 +18,7 @@
 COLS = HQ * ROWS
 CHIP_ROWS = 2 * ROWS
 PAST = 2 * CHIP_ROWS
-TILE = 256
+TILE = 1024
 TILES = COLS // TILE
 NEG = -1e30
 SCALING = 1.0 / math.sqrt(DH)

time: 28.5 us -> 28.5 us (level)
  no operation moved by 1% of the time
where the time goes in v8:
time: 28.5 us; the launch traced here: 28.4 us
  starting transfers between devices  16.5 us (58%)
  waiting for transfers between devices  5.31 us (19%)
  Pallas kernels  4.43 us (16%)
  between operations  0.78 us (3%)
  other arithmetic  0.77 us (3%)
  local copies, waits for them, and re-layouts  0.64 us (2%)
    ppermute x4, starting transfers between devices, move_chips(): return lax.ppermute(x, AXES, pairs)  13.3 us
    pallas_call x11, Pallas kernels, call(): pl.pallas_call(kernel, out_shape=outs, in_specs=[vmem] * len(args), out_s...  4.43 us
    ppermute x4, waiting for transfers between devices, move_chips(): return lax.ppermute(x, AXES, pairs)  3.49 us
    ppermute x9, starting transfers between devices, swap_cores(): return lax.ppermute(x, 'uly', [(i, i ^ 1) for i in range(16)])  3.16 us
    ppermute x9, waiting for transfers between devices, swap_cores(): return lax.ppermute(x, 'uly', [(i, i ^ 1) for i in range(16)])  1.82 us
    concatenate x1, other arithmetic, on_device(): mine = jnp.concatenate([key_rows, value_rows], axis=1)  0.74 us
    slice x1, local copies, waits for them, and re-layouts, on_device(): return (query_grad, result[:, :DH], result[:, DH:])  0.62 us
  transfers between devices with their start and end apart: 13, of which 6 were waited for; matrix products, arithmetic and copies ran while one was open for 3% of the time, Pallas kernels for 14%

profile of v8, /device:TPU:39, one launch (start us, length us, event | category | flops | bytes accessed | tf_op | source)
XLA Modules:
  0.0 28.4 jit_solution(2806630249054094605)
XLA Ops:
  0.6 0.8 %collective-permute-start.1 = (bf16[64,128]{1,0:T(8,128)(2,1)}, bf16[64,128]{1,0:T(8,128)(2,1)S(1)}, u32[]{:S(2)}, u32[]{:S(2)}) collective-permute-start(bf16[64,128]{1,0:T(8,128)(2,1)} %param.7), channel_id=1, source_target_pairs={{0,1},{1,0},{2,3},{3,2},{4,5},{5,4},{6,7},{7,6},{8,9},{9,8},{10,11... | collective-permute-start | bytes 49160 | tf_op jit(solution)/shard_map/ppermute | solution.py:43
  1.5 0.7 %pad_maximum_fusion.mine_ref = bf16[64,256]{1,0:T(8,128)(2,1)S(1)} fusion(bf16[64,128]{1,0:T(8,128)(2,1)} %param.8, bf16[64,128]{1,0:T(8,128)(2,1)} %param.7), kind=kLoop, calls=%fused_computation.3 | loop fusion | flops 65536 | bytes 65536 | tf_op jit(solution)/shard_map/concatenate | solution.py:318
  2.3 0.2 collective-permute-done.1.other_k_ref
  2.5 0.3 %collective-permute-done.2.other_v_ref = bf16[64,128]{1,0:T(8,128)(2,1)S(1)} collective-permute-done((bf16[64,128]{1,0:T(8,128)(2,1)}, bf16[64,128]{1,0:T(8,128)(2,1)S(1)}, u32[]{:S(2)}, u32[]{:S(2)}) %collective-permute-start.2) | collective-permute-done | bytes 16416 | tf_op jit(solution)/shard_map/ppermute | solution.py:43
  2.8 3.1 %collective-permute-start.5 = (bf16[128,256]{1,0:T(8,128)(2,1)S(1)}, bf16[128,256]{1,0:T(8,128)(2,1)S(1)}, u32[]{:S(2)}, u32[]{:S(2)}) collective-permute-start(bf16[128,256]{1,0:T(8,128)(2,1)S(1)} %shard_map.86.own_ref), channel_id=1, source_target_pairs={{0,6},{1,4},{3,16},{2,7},{4,18},{5,17},{6,21},{7,19},{16,22},{17,2... | collective-permute-start | bytes 196616 | tf_op jit(solution)/shard_map/ppermute | solution.py:55
  5.9 5.5 %collective-permute-start.4 = (bf16[128,256]{1,0:T(8,128)(2,1)S(1)}, bf16[128,256]{1,0:T(8,128)(2,1)S(1)}, u32[]{:S(2)}, u32[]{:S(2)}) collective-permute-start(bf16[128,256]{1,0:T(8,128)(2,1)S(1)} %shard_map.86.own_ref), channel_id=1, source_target_pairs={{0,2},{1,16},{2,4},{3,19},{4,6},{5,21},{7,17},{6,23},{16,18},{17,3... | collective-permute-start | bytes 196616 | tf_op jit(solution)/shard_map/ppermute | solution.py:55
  11.5 0.7 %shard_map.87 = (bf16[1024,128]{1,0:T(8,128)(2,1)S(1)}, f32[1,1024]{1,0:T(1,128)S(1)}, bf16[384,128]{1,0:T(8,128)(2,1)S(1)}, f32[128,1024]{1,0:T(8,128)S(1)}, f3...) custom-call(bf16[1024,128]{1,0:T(8,128)(2,1)S(1)} %shard_map.85.q2_ref.q_ref, bf16[64,2048]{1,0:T(8,128)(2,1)S(1)} %copy-done, ...), custom_call_target="tpu_custom_call" | custom-call | flops 100000000 | bytes 200000 | tf_op jit(solution)/shard_map/pallas_call | solution.py:302
  12.2 0.6 %collective-permute-start.3 = (bf16[1024,128]{1,0:T(8,128)(2,1)S(1)}, bf16[1024,128]{1,0:T(8,128)(2,1)S(1)}, u32[]{:S(2)}, u32[]{:S(2)}) collective-permute-start(bf16[1024,128]{1,0:T(8,128)(2,1)S(1)} %get-tuple-element.35.g_ref), channel_id=1, source_target_pairs={{0,1},{1,0},{2,3},{3,2},{4,5},{5,4},{6,7},{7,6},{8,9},{9,8},{10,11... | collective-permute-start | bytes 786440 | tf_op jit(solution)/shard_map/ppermute | solution.py:43
  12.8 0.2 collective-permute-done.partner_q_ref
  13.0 0.7 %shard_map.89 = (f32[256,2048]{1,0:T(8,128)S(1)}, f32[2,2048]{1,0:T(2,128)S(1)}, f32[5,1024]{1,0:T(8,128)S(1)}) custom-call(bf16[1024,128]{1,0:T(8,128)(2,1)S(1)} %shard_map.85.q2_ref.q_ref, bf16[1024,128]{1,0:T(8,128)(2,1)S(1)} %collective-permute-done.partner_q_ref, bf16[256,256]{1,0:T(8,128)(2,1)S(1)} %shard_map.88.keys_ref, ...), custom_call_target="tpu_custom_call" | custom-call | flops 1000000000 | bytes 2000000 | tf_op jit(solution)/shard_map/pallas_call | solution.py:302
  13.7 0.2 collective-permute-start.6
  14.0 0.4 %shard_map.90.u_ref = f32[256,2048]{1,0:T(8,128)S(1)} custom-call(bf16[1024,128]{1,0:T(8,128)(2,1)S(1)} %get-tuple-element.35.g_ref, bf16[1024,128]{1,0:T(8,128)(2,1)S(1)} %collective-permute-done.3.partner_g_ref, bf16[128,256]{1,0:T(8,128)(2,1)S(1)} %collective-permute-done.4.a_ref, bf16[128,256]{1,0:T(8,128)(2,1)S(1)} %collective-permute-done.5.b_ref), custom_call_target="tpu_custom_call" | custom-call | flops 1000000000 | bytes 2000000 | tf_op jit(solution)/shard_map/pallas_call | solution.py:302
  14.4 0.6 %collective-permute-done.6.far_ref = f32[5,1024]{1,0:T(8,128)S(1)} collective-permute-done((f32[5,1024]{1,0:T(8,128)S(1)}, f32[5,1024]{1,0:T(8,128)S(1)}, u32[]{:S(2)}, u32[]{:S(2)}) %collective-permute-start.6) | collective-permute-done | bytes 20512 | tf_op jit(solution)/shard_map/ppermute | solution.py:43
  15.0 0.5 %shard_map.91 = (bf16[128,256]{1,0:T(8,128)(2,1)S(1)}, bf16[128,2048]{1,0:T(8,128)(2,1)S(1)}, f32[2,2048]{1,0:T(2,128)S(1)}, f32[2,2048]{1,0:T(2,128)S(1)}) custom-call(bf16[1024,128]{1,0:T(8,128)(2,1)S(1)} %shard_map.85.q2_ref.q_ref, bf16[1024,128]{1,0:T(8,128)(2,1)S(1)} %collective-permute-done.partner_q_ref, ...), custom_call_target="tpu_custom_call" | custom-call | flops 1000000000 | bytes 2000000 | tf_op jit(solution)/shard_map/pallas_call | solution.py:302
  15.6 2.9 %collective-permute-start.7 = (bf16[128,256]{1,0:T(8,128)(2,1)S(1)}, bf16[128,256]{1,0:T(8,128)(2,1)S(1)}, u32[]{:S(2)}, u32[]{:S(2)}) collective-permute-start(bf16[128,256]{1,0:T(8,128)(2,1)S(1)} %get-tuple-element.45), channel_id=1, source_target_pairs={{6,0},{4,1},{16,3},{7,2},{18,4},{17,5},{21,6},{19,7},{22,16},{20,1... | collective-permute-start | bytes 196616 | tf_op jit(solution)/shard_map/ppermute | solution.py:55
  18.5 0.5 %shard_map.92 = (bf16[128,256]{1,0:T(8,128)(2,1)S(1)}, bf16[128,2048]{1,0:T(8,128)(2,1)S(1)}) custom-call(bf16[1024,128]{1,0:T(8,128)(2,1)S(1)} %shard_map.85.q2_ref.q_ref, bf16[1024,128]{1,0:T(8,128)(2,1)S(1)} %collective-permute-done.partner_q_ref, bf16[1024,128]{1,0:T(8,128)(2,1)S(1)} %get-tuple-element.35.g_ref, ...), custom_call_target="tpu_custom_call" | custom-call | flops 1000000000 | bytes 2000000 | tf_op jit(solution)/shard_map/pallas_call | solution.py:302
  19.0 1.8 %collective-permute-start.8 = (bf16[128,256]{1,0:T(8,128)(2,1)S(1)}, bf16[128,256]{1,0:T(8,128)(2,1)S(1)}, u32[]{:S(2)}, u32[]{:S(2)}) collective-permute-start(bf16[128,256]{1,0:T(8,128)(2,1)S(1)} %get-tuple-element.52), channel_id=1, source_target_pairs={{2,0},{16,1},{4,2},{19,3},{6,4},{21,5},{17,7},{23,6},{18,16},{32,1... | collective-permute-start | bytes 196616 | tf_op jit(solution)/shard_map/ppermute | solution.py:55
  20.8 0.7 %shard_map.93 = (f32[1024,128]{1,0:T(8,128)S(1)}, f32[128,256]{1,0:T(8,128)S(1)}, bf16[352,128]{1,0:T(8,128)(2,1)S(1)}, bf16[352,128]{1,0:T(8,128)(2,1)S(1)}, bf16[320,128]{1,0:T(8,128)(2,1)S(1)}) custom-call(bf16[1024,128]{1,0:T(8,128)(2,1)S(1)} %shard_map.85.q2_ref.q_ref, bf16[1024,128]{1,0:T(8,128)(2,1)S(1)} %get-tuple-element.35.g_ref, ...), custom_call_target="tpu_custom_call" | custom-call | flops 100000000 | bytes 200000 | tf_op jit(solution)/shard_map/pallas_call | solution.py:302
  21.6 0.8 %collective-permute-start.12 = (bf16[320,128]{1,0:T(8,128)(2,1)S(1)}, bf16[320,128]{1,0:T(8,128)(2,1)S(1)}, u32[]{:S(2)}, u32[]{:S(2)}) collective-permute-start(bf16[320,128]{1,0:T(8,128)(2,1)S(1)} %get-tuple-element.57), channel_id=1, source_target_pairs={{0,1},{1,0},{2,3},{3,2},{4,5},{5,4},{6,7},{7,6},{8,9},{9,8},{10,11... | collective-permute-start | bytes 245768 | tf_op jit(solution)/shard_map/ppermute | solution.py:43
  22.5 0.4 %collective-permute-start.11 = (bf16[352,128]{1,0:T(8,128)(2,1)S(1)}, bf16[352,128]{1,0:T(8,128)(2,1)S(1)}, u32[]{:S(2)}, u32[]{:S(2)}) collective-permute-start(bf16[352,128]{1,0:T(8,128)(2,1)S(1)} %get-tuple-element.56), channel_id=1, source_target_pairs={{0,1},{1,0},{2,3},{3,2},{4,5},{5,4},{6,7},{7,6},{8,9},{9,8},{10,11... | collective-permute-start | bytes 270344 | tf_op jit(solution)/shard_map/ppermute | solution.py:43
  22.9 3.5 %collective-permute-done.8 = bf16[128,256]{1,0:T(8,128)(2,1)S(1)} collective-permute-done((bf16[128,256]{1,0:T(8,128)(2,1)S(1)}, bf16[128,256]{1,0:T(8,128)(2,1)S(1)}, u32[]{:S(2)}, u32[]{:S(2)}) %collective-permute-start.8) | collective-permute-done | bytes 65568 | tf_op jit(solution)/shard_map/ppermute | solution.py:55
  26.6 0.8 %shard_map.95 = bf16[64,2048]{1,0:T(8,128)(2,1)} custom-call(f32[1024,128]{1,0:T(8,128)S(1)} %get-tuple-element.54.dq_ref, bf16[352,128]{1,0:T(8,128)(2,1)S(1)} %collective-permute-done.10.refs_0_, bf16[352,128]{1,0:T(8,128)(2,1)S(1)} %collective-permute-done.11.refs_1_, bf16[320,128]{1,0:T(8,128)(2,1)S(1)} %collective-permute-done.12.refs_2_), custom_call_target="tpu_custom_call" | custom-call | flops 1000000000 | bytes 2000000 | tf_op jit(solution)/shard_map/pallas_call | solution.py:302
  27.4 0.4 %collective-permute-done.9 = bf16[64,256]{1,0:T(8,128)(2,1)S(1)} collective-permute-done((bf16[64,256]{1,0:T(8,128)(2,1)S(1)}, bf16[64,256]{1,0:T(8,128)(2,1)S(1)}, u32[]{:S(2)}, u32[]{:S(2)}) %collective-permute-start.9) | collective-permute-done | bytes 32800 | tf_op jit(solution)/shard_map/ppermute | solution.py:43
  27.8 0.6 %fusion = (bf16[64,128]{1,0:T(8,128)(2,1)}, bf16[64,128]{1,0:T(8,128)(2,1)}) fusion(bf16[64,256]{1,0:T(8,128)(2,1)S(1)} %add_convert_fusion), kind=kLoop, calls=%fused_computation.4 | loop fusion | bytes 65536 | tf_op jit(solution)/shard_map/slice | solution.py:367
  (26 shorter events, 0.5 us)
Async XLA Ops:
  0.6 10.7 %copy-start.2 = (bf16[64,2048]{1,0:T(8,128)(2,1)S(1)}, bf16[64,2048]{1,0:T(8,128)(2,1)}, u32[]{:S(2)}) copy-start(bf16[64,2048]{1,0:T(8,128)(2,1)} %q_ref.1) | copy-start | bytes 786436
  0.6 1.8 %collective-permute-start.1 = (bf16[64,128]{1,0:T(8,128)(2,1)}, bf16[64,128]{1,0:T(8,128)(2,1)S(1)}, u32[]{:S(2)}, u32[]{:S(2)}) collective-permute-start(bf16[64,128]{1,0:T(8,128)(2,1)} %param.7), channel_id=1, source_target_pairs={{0,1},{1,0},{2,3},{3,2},{4,5},{5,4},{6,7},{7,6},{8,9},{9,8},{10,11... | collective-permute-start | bytes 49160 | tf_op jit(solution)/shard_map/ppermute | solution.py:43
  1.4 1.4 %collective-permute-start.2 = (bf16[64,128]{1,0:T(8,128)(2,1)}, bf16[64,128]{1,0:T(8,128)(2,1)S(1)}, u32[]{:S(2)}, u32[]{:S(2)}) collective-permute-start(bf16[64,128]{1,0:T(8,128)(2,1)} %param.8), channel_id=1, source_target_pairs={{0,1},{1,0},{2,3},{3,2},{4,5},{5,4},{6,7},{7,6},{8,9},{9,8},{10,11... | collective-permute-start | bytes 49160 | tf_op jit(solution)/shard_map/ppermute | solution.py:43
  2.2 9.3 %copy-start = (bf16[64,2048]{1,0:T(8,128)(2,1)S(1)}, bf16[64,2048]{1,0:T(8,128)(2,1)}, u32[]{:S(2)}) copy-start(bf16[64,2048]{1,0:T(8,128)(2,1)} %o_ref.1) | copy-start | bytes 786436
  2.2 9.3 %copy-start.1 = (bf16[64,2048]{1,0:T(8,128)(2,1)S(1)}, bf16[64,2048]{1,0:T(8,128)(2,1)}, u32[]{:S(2)}) copy-start(bf16[64,2048]{1,0:T(8,128)(2,1)} %g_ref.1) | copy-start | bytes 786436
  2.2 9.3 %copy-start.3 = (s32[64]{0:T(128)S(1)}, s32[64]{0:T(128)}, u32[]{:S(2)}) copy-start(s32[64]{0:T(128)} %param.11) | copy-start | bytes 772
  2.8 9.9 %collective-permute-start.5 = (bf16[128,256]{1,0:T(8,128)(2,1)S(1)}, bf16[128,256]{1,0:T(8,128)(2,1)S(1)}, u32[]{:S(2)}, u32[]{:S(2)}) collective-permute-start(bf16[128,256]{1,0:T(8,128)(2,1)S(1)} %shard_map.86.own_ref), channel_id=1, source_target_pairs={{0,6},{1,4},{3,16},{2,7},{4,18},{5,17},{6,21},{7,19},{16,22},{17,2... | collective-permute-start | bytes 196616 | tf_op jit(solution)/shard_map/ppermute | solution.py:55
  5.9 6.9 %collective-permute-start.4 = (bf16[128,256]{1,0:T(8,128)(2,1)S(1)}, bf16[128,256]{1,0:T(8,128)(2,1)S(1)}, u32[]{:S(2)}, u32[]{:S(2)}) collective-permute-start(bf16[128,256]{1,0:T(8,128)(2,1)S(1)} %shard_map.86.own_ref), channel_id=1, source_target_pairs={{0,2},{1,16},{2,4},{3,19},{4,6},{5,21},{7,17},{6,23},{16,18},{17,3... | collective-permute-start | bytes 196616 | tf_op jit(solution)/shard_map/ppermute | solution.py:55
  11.4 1.6 %collective-permute-start = (bf16[1024,128]{1,0:T(8,128)(2,1)S(1)}, bf16[1024,128]{1,0:T(8,128)(2,1)S(1)}, u32[]{:S(2)}, u32[]{:S(2)}) collective-permute-start(bf16[1024,128]{1,0:T(8,128)(2,1)S(1)} %shard_map.85.q2_ref.q_ref), channel_id=1, source_target_pairs={{0,1},{1,0},{2,3},{3,2},{4,5},{5,4},{6,7},{7,6},{8,9},{9,8},{10,11... | collective-permute-start | bytes 786440 | tf_op jit(solution)/shard_map/ppermute | solution.py:43
  12.2 1.8 %collective-permute-start.3 = (bf16[1024,128]{1,0:T(8,128)(2,1)S(1)}, bf16[1024,128]{1,0:T(8,128)(2,1)S(1)}, u32[]{:S(2)}, u32[]{:S(2)}) collective-permute-start(bf16[1024,128]{1,0:T(8,128)(2,1)S(1)} %get-tuple-element.35.g_ref), channel_id=1, source_target_pairs={{0,1},{1,0},{2,3},{3,2},{4,5},{5,4},{6,7},{7,6},{8,9},{9,8},{10,11... | collective-permute-start | bytes 786440 | tf_op jit(solution)/shard_map/ppermute | solution.py:43
  13.7 1.3 %collective-permute-start.6 = (f32[5,1024]{1,0:T(8,128)S(1)}, f32[5,1024]{1,0:T(8,128)S(1)}, u32[]{:S(2)}, u32[]{:S(2)}) collective-permute-start(f32[5,1024]{1,0:T(8,128)S(1)} %get-tuple-element.41.stats_ref), channel_id=1, source_target_pairs={{0,1},{1,0},{2,3},{3,2},{4,5},{5,4},{6,7},{7,6},{8,9},{9,8},{10,11... | collective-permute-start | bytes 61448 | tf_op jit(solution)/shard_map/ppermute | solution.py:43
  15.6 7.3 %collective-permute-start.7 = (bf16[128,256]{1,0:T(8,128)(2,1)S(1)}, bf16[128,256]{1,0:T(8,128)(2,1)S(1)}, u32[]{:S(2)}, u32[]{:S(2)}) collective-permute-start(bf16[128,256]{1,0:T(8,128)(2,1)S(1)} %get-tuple-element.45), channel_id=1, source_target_pairs={{6,0},{4,1},{16,3},{7,2},{18,4},{17,5},{21,6},{19,7},{22,16},{20,1... | collective-permute-start | bytes 196616 | tf_op jit(solution)/shard_map/ppermute | solution.py:55
  19.0 7.4 %collective-permute-start.8 = (bf16[128,256]{1,0:T(8,128)(2,1)S(1)}, bf16[128,256]{1,0:T(8,128)(2,1)S(1)}, u32[]{:S(2)}, u32[]{:S(2)}) collective-permute-start(bf16[128,256]{1,0:T(8,128)(2,1)S(1)} %get-tuple-element.52), channel_id=1, source_target_pairs={{2,0},{16,1},{4,2},{19,3},{6,4},{21,5},{17,7},{23,6},{18,16},{32,1... | collective-permute-start | bytes 196616 | tf_op jit(solution)/shard_map/ppermute | solution.py:55
  21.6 5.0 %collective-permute-start.12 = (bf16[320,128]{1,0:T(8,128)(2,1)S(1)}, bf16[320,128]{1,0:T(8,128)(2,1)S(1)}, u32[]{:S(2)}, u32[]{:S(2)}) collective-permute-start(bf16[320,128]{1,0:T(8,128)(2,1)S(1)} %get-tuple-element.57), channel_id=1, source_target_pairs={{0,1},{1,0},{2,3},{3,2},{4,5},{5,4},{6,7},{7,6},{8,9},{9,8},{10,11... | collective-permute-start | bytes 245768 | tf_op jit(solution)/shard_map/ppermute | solution.py:43
  22.4 4.2 %collective-permute-start.10 = (bf16[352,128]{1,0:T(8,128)(2,1)S(1)}, bf16[352,128]{1,0:T(8,128)(2,1)S(1)}, u32[]{:S(2)}, u32[]{:S(2)}) collective-permute-start(bf16[352,128]{1,0:T(8,128)(2,1)S(1)} %get-tuple-element.55), channel_id=1, source_target_pairs={{0,1},{1,0},{2,3},{3,2},{4,5},{5,4},{6,7},{7,6},{8,9},{9,8},{10,11... | collective-permute-start | bytes 270344 | tf_op jit(solution)/shard_map/ppermute | solution.py:43
  22.5 4.1 %collective-permute-start.11 = (bf16[352,128]{1,0:T(8,128)(2,1)S(1)}, bf16[352,128]{1,0:T(8,128)(2,1)S(1)}, u32[]{:S(2)}, u32[]{:S(2)}) collective-permute-start(bf16[352,128]{1,0:T(8,128)(2,1)S(1)} %get-tuple-element.56), channel_id=1, source_target_pairs={{0,1},{1,0},{2,3},{3,2},{4,5},{5,4},{6,7},{7,6},{8,9},{9,8},{10,11... | collective-permute-start | bytes 270344 | tf_op jit(solution)/shard_map/ppermute | solution.py:43
  26.5 1.3 %collective-permute-start.9 = (bf16[64,256]{1,0:T(8,128)(2,1)S(1)}, bf16[64,256]{1,0:T(8,128)(2,1)S(1)}, u32[]{:S(2)}, u32[]{:S(2)}) collective-permute-start(bf16[64,256]{1,0:T(8,128)(2,1)S(1)} %slice.22), channel_id=1, source_target_pairs={{0,1},{1,0},{2,3},{3,2},{4,5},{5,4},{6,7},{7,6},{8,9},{9,8},{10,11... | collective-permute-start | bytes 98312 | tf_op jit(solution)/shard_map/ppermute | solution.py:43

commit v9 on v8

--- a/solution.py
+++ b/solution.py
@@ -28,7 +28,7 @@
     ((1, 4), (0, 0, 0, 1), (1, 0, 0, 0)),
     ((3, 2), (0, 1, 0, 0), (0, 0, 1, 0)),
 )
-PIECES = (0, 352, 704, COLS)
+PIECES = (0, 512, COLS)
 KEY_COLS, VALUE_COLS = slice(0, DH), slice(DH, 2 * DH)
 
 

time: 28.5 us -> 28.5 us (level)
  starting transfers between devices: 16.5 us -> 16 us
  waiting for transfers between devices: 5.31 us -> 5.73 us
    ppermute x4, waiting for transfers between devices: 3.49 us -> 3.9 us  [move_chips(): return lax.ppermute(x, AXES, pairs)]
    ppermute x9 -> x8, starting transfers between devices: 3.16 us -> 2.75 us  [swap_cores(): return lax.ppermute(x, 'uly', [(i, i ^ 1) for i in range(16)])]
    ppermute x9 -> x8, waiting for transfers between devices: 1.82 us -> 1.83 us  [swap_cores(): return lax.ppermute(x, 'uly', [(i, i ^ 1) for i in range(16)])]
  transfers between devices with their start and end apart: 13 -> 12, of which waited for: 6 -> 6; matrix products, arithmetic and copies ran while one was open for 3% -> 3% of each run, Pallas kernels for 14% -> 14%
where the time goes in v9:
time: 28.5 us; the launch traced here: 28.4 us
  starting transfers between devices  16 us (56%)
  waiting for transfers between devices  5.73 us (20%)
  Pallas kernels  4.44 us (16%)
  other arithmetic  0.77 us (3%)
  between operations  0.77 us (3%)
  local copies, waits for them, and re-layouts  0.64 us (2%)
    ppermute x4, starting transfers between devices, move_chips(): return lax.ppermute(x, AXES, pairs)  13.3 us
    pallas_call x11, Pallas kernels, call(): pl.pallas_call(kernel, out_shape=outs, in_specs=[vmem] * len(args), out_s...  4.44 us
    ppermute x4, waiting for transfers between devices, move_chips(): return lax.ppermute(x, AXES, pairs)  3.9 us
    ppermute x8, starting transfers between devices, swap_cores(): return lax.ppermute(x, 'uly', [(i, i ^ 1) for i in range(16)])  2.75 us
    ppermute x8, waiting for transfers between devices, swap_cores(): return lax.ppermute(x, 'uly', [(i, i ^ 1) for i in range(16)])  1.83 us
    concatenate x1, other arithmetic, on_device(): mine = jnp.concatenate([key_rows, value_rows], axis=1)  0.74 us
    slice x1, local copies, waits for them, and re-layouts, on_device(): return (query_grad, result[:, :DH], result[:, DH:])  0.62 us
  transfers between devices with their start and end apart: 12, of which 6 were waited for; matrix products, arithmetic and copies ran while one was open for 3% of the time, Pallas kernels for 14%

profile of v9, /device:TPU:39, one launch (start us, length us, event | category | flops | bytes accessed | tf_op | source)
XLA Modules:
  0.0 28.4 jit_solution(13606078893022179202)
XLA Ops:
  0.6 0.8 %collective-permute-start.1 = (bf16[64,128]{1,0:T(8,128)(2,1)}, bf16[64,128]{1,0:T(8,128)(2,1)S(1)}, u32[]{:S(2)}, u32[]{:S(2)}) collective-permute-start(bf16[64,128]{1,0:T(8,128)(2,1)} %param.7), channel_id=1, source_target_pairs={{0,1},{1,0},{2,3},{3,2},{4,5},{5,4},{6,7},{7,6},{8,9},{9,8},{10,11... | collective-permute-start | bytes 49160 | tf_op jit(solution)/shard_map/ppermute | solution.py:43
  1.5 0.7 %pad_maximum_fusion.mine_ref = bf16[64,256]{1,0:T(8,128)(2,1)S(1)} fusion(bf16[64,128]{1,0:T(8,128)(2,1)} %param.8, bf16[64,128]{1,0:T(8,128)(2,1)} %param.7), kind=kLoop, calls=%fused_computation.3 | loop fusion | flops 65536 | bytes 65536 | tf_op jit(solution)/shard_map/concatenate | solution.py:318
  2.3 0.2 collective-permute-done.1.other_k_ref
  2.5 0.3 %collective-permute-done.2.other_v_ref = bf16[64,128]{1,0:T(8,128)(2,1)S(1)} collective-permute-done((bf16[64,128]{1,0:T(8,128)(2,1)}, bf16[64,128]{1,0:T(8,128)(2,1)S(1)}, u32[]{:S(2)}, u32[]{:S(2)}) %collective-permute-start.2) | collective-permute-done | bytes 16416 | tf_op jit(solution)/shard_map/ppermute | solution.py:43
  2.8 3.1 %collective-permute-start.5 = (bf16[128,256]{1,0:T(8,128)(2,1)S(1)}, bf16[128,256]{1,0:T(8,128)(2,1)S(1)}, u32[]{:S(2)}, u32[]{:S(2)}) collective-permute-start(bf16[128,256]{1,0:T(8,128)(2,1)S(1)} %shard_map.86.own_ref), channel_id=1, source_target_pairs={{0,6},{1,4},{3,16},{2,7},{4,18},{5,17},{6,21},{7,19},{16,22},{17,2... | collective-permute-start | bytes 196616 | tf_op jit(solution)/shard_map/ppermute | solution.py:55
  5.9 5.5 %collective-permute-start.4 = (bf16[128,256]{1,0:T(8,128)(2,1)S(1)}, bf16[128,256]{1,0:T(8,128)(2,1)S(1)}, u32[]{:S(2)}, u32[]{:S(2)}) collective-permute-start(bf16[128,256]{1,0:T(8,128)(2,1)S(1)} %shard_map.86.own_ref), channel_id=1, source_target_pairs={{0,2},{1,16},{2,4},{3,19},{4,6},{5,21},{7,17},{6,23},{16,18},{17,3... | collective-permute-start | bytes 196616 | tf_op jit(solution)/shard_map/ppermute | solution.py:55
  11.5 0.7 %shard_map.87 = (bf16[1024,128]{1,0:T(8,128)(2,1)S(1)}, f32[1,1024]{1,0:T(1,128)S(1)}, bf16[384,128]{1,0:T(8,128)(2,1)S(1)}, f32[128,1024]{1,0:T(8,128)S(1)}, f3...) custom-call(bf16[1024,128]{1,0:T(8,128)(2,1)S(1)} %shard_map.85.q2_ref.q_ref, bf16[64,2048]{1,0:T(8,128)(2,1)S(1)} %copy-done, ...), custom_call_target="tpu_custom_call" | custom-call | flops 100000000 | bytes 200000 | tf_op jit(solution)/shard_map/pallas_call | solution.py:302
  12.2 0.6 %collective-permute-start.3 = (bf16[1024,128]{1,0:T(8,128)(2,1)S(1)}, bf16[1024,128]{1,0:T(8,128)(2,1)S(1)}, u32[]{:S(2)}, u32[]{:S(2)}) collective-permute-start(bf16[1024,128]{1,0:T(8,128)(2,1)S(1)} %get-tuple-element.34.g_ref), channel_id=1, source_target_pairs={{0,1},{1,0},{2,3},{3,2},{4,5},{5,4},{6,7},{7,6},{8,9},{9,8},{10,11... | collective-permute-start | bytes 786440 | tf_op jit(solution)/shard_map/ppermute | solution.py:43
  12.8 0.2 collective-permute-done.partner_q_ref
  13.0 0.7 %shard_map.89 = (f32[256,2048]{1,0:T(8,128)S(1)}, f32[2,2048]{1,0:T(2,128)S(1)}, f32[5,1024]{1,0:T(8,128)S(1)}) custom-call(bf16[1024,128]{1,0:T(8,128)(2,1)S(1)} %shard_map.85.q2_ref.q_ref, bf16[1024,128]{1,0:T(8,128)(2,1)S(1)} %collective-permute-done.partner_q_ref, bf16[256,256]{1,0:T(8,128)(2,1)S(1)} %shard_map.88.keys_ref, ...), custom_call_target="tpu_custom_call" | custom-call | flops 1000000000 | bytes 2000000 | tf_op jit(solution)/shard_map/pallas_call | solution.py:302
  13.7 0.2 collective-permute-start.6
  14.0 0.4 %shard_map.90.u_ref = f32[256,2048]{1,0:T(8,128)S(1)} custom-call(bf16[1024,128]{1,0:T(8,128)(2,1)S(1)} %get-tuple-element.34.g_ref, bf16[1024,128]{1,0:T(8,128)(2,1)S(1)} %collective-permute-done.3.partner_g_ref, bf16[128,256]{1,0:T(8,128)(2,1)S(1)} %collective-permute-done.4.a_ref, bf16[128,256]{1,0:T(8,128)(2,1)S(1)} %collective-permute-done.5.b_ref), custom_call_target="tpu_custom_call" | custom-call | flops 1000000000 | bytes 2000000 | tf_op jit(solution)/shard_map/pallas_call | solution.py:302
  14.4 0.6 %collective-permute-done.6.far_ref = f32[5,1024]{1,0:T(8,128)S(1)} collective-permute-done((f32[5,1024]{1,0:T(8,128)S(1)}, f32[5,1024]{1,0:T(8,128)S(1)}, u32[]{:S(2)}, u32[]{:S(2)}) %collective-permute-start.6) | collective-permute-done | bytes 20512 | tf_op jit(solution)/shard_map/ppermute | solution.py:43
  15.0 0.5 %shard_map.91 = (bf16[128,256]{1,0:T(8,128)(2,1)S(1)}, bf16[128,2048]{1,0:T(8,128)(2,1)S(1)}, f32[2,2048]{1,0:T(2,128)S(1)}, f32[2,2048]{1,0:T(2,128)S(1)}) custom-call(bf16[1024,128]{1,0:T(8,128)(2,1)S(1)} %shard_map.85.q2_ref.q_ref, bf16[1024,128]{1,0:T(8,128)(2,1)S(1)} %collective-permute-done.partner_q_ref, ...), custom_call_target="tpu_custom_call" | custom-call | flops 1000000000 | bytes 2000000 | tf_op jit(solution)/shard_map/pallas_call | solution.py:302
  15.6 2.9 %collective-permute-start.7 = (bf16[128,256]{1,0:T(8,128)(2,1)S(1)}, bf16[128,256]{1,0:T(8,128)(2,1)S(1)}, u32[]{:S(2)}, u32[]{:S(2)}) collective-permute-start(bf16[128,256]{1,0:T(8,128)(2,1)S(1)} %get-tuple-element.44), channel_id=1, source_target_pairs={{6,0},{4,1},{16,3},{7,2},{18,4},{17,5},{21,6},{19,7},{22,16},{20,1... | collective-permute-start | bytes 196616 | tf_op jit(solution)/shard_map/ppermute | solution.py:55
  18.5 0.5 %shard_map.92 = (bf16[128,256]{1,0:T(8,128)(2,1)S(1)}, bf16[128,2048]{1,0:T(8,128)(2,1)S(1)}) custom-call(bf16[1024,128]{1,0:T(8,128)(2,1)S(1)} %shard_map.85.q2_ref.q_ref, bf16[1024,128]{1,0:T(8,128)(2,1)S(1)} %collective-permute-done.partner_q_ref, bf16[1024,128]{1,0:T(8,128)(2,1)S(1)} %get-tuple-element.34.g_ref, ...), custom_call_target="tpu_custom_call" | custom-call | flops 1000000000 | bytes 2000000 | tf_op jit(solution)/shard_map/pallas_call | solution.py:302
  19.0 1.8 %collective-permute-start.8 = (bf16[128,256]{1,0:T(8,128)(2,1)S(1)}, bf16[128,256]{1,0:T(8,128)(2,1)S(1)}, u32[]{:S(2)}, u32[]{:S(2)}) collective-permute-start(bf16[128,256]{1,0:T(8,128)(2,1)S(1)} %get-tuple-element.51), channel_id=1, source_target_pairs={{2,0},{16,1},{4,2},{19,3},{6,4},{21,5},{17,7},{23,6},{18,16},{32,1... | collective-permute-start | bytes 196616 | tf_op jit(solution)/shard_map/ppermute | solution.py:55
  20.8 0.7 %shard_map.93 = (f32[1024,128]{1,0:T(8,128)S(1)}, f32[128,256]{1,0:T(8,128)S(1)}, bf16[512,128]{1,0:T(8,128)(2,1)S(1)}, bf16[512,128]{1,0:T(8,128)(2,1)S(1)}) custom-call(bf16[1024,128]{1,0:T(8,128)(2,1)S(1)} %shard_map.85.q2_ref.q_ref, bf16[1024,128]{1,0:T(8,128)(2,1)S(1)} %get-tuple-element.34.g_ref, f32[1,1024]{1,0:T(1,128)S(1)} %get-tuple-element.38.dot_ref, ...), custom_call_target="tpu_custom_call" | custom-call | flops 100000000 | bytes 200000 | tf_op jit(solution)/shard_map/pallas_call | solution.py:302
  21.6 0.8 %collective-permute-start.10 = (bf16[512,128]{1,0:T(8,128)(2,1)S(1)}, bf16[512,128]{1,0:T(8,128)(2,1)S(1)}, u32[]{:S(2)}, u32[]{:S(2)}) collective-permute-start(bf16[512,128]{1,0:T(8,128)(2,1)S(1)} %get-tuple-element.54), channel_id=1, source_target_pairs={{0,1},{1,0},{2,3},{3,2},{4,5},{5,4},{6,7},{7,6},{8,9},{9,8},{10,11... | collective-permute-start | bytes 393224 | tf_op jit(solution)/shard_map/ppermute | solution.py:43
  22.4 0.1 collective-permute-start.11
  22.5 3.9 %collective-permute-done.8 = bf16[128,256]{1,0:T(8,128)(2,1)S(1)} collective-permute-done((bf16[128,256]{1,0:T(8,128)(2,1)S(1)}, bf16[128,256]{1,0:T(8,128)(2,1)S(1)}, u32[]{:S(2)}, u32[]{:S(2)}) %collective-permute-start.8) | collective-permute-done | bytes 65568 | tf_op jit(solution)/shard_map/ppermute | solution.py:55
  26.6 0.8 %shard_map.95 = bf16[64,2048]{1,0:T(8,128)(2,1)} custom-call(f32[1024,128]{1,0:T(8,128)S(1)} %get-tuple-element.53.dq_ref, bf16[512,128]{1,0:T(8,128)(2,1)S(1)} %collective-permute-done.10.refs_0_, bf16[512,128]{1,0:T(8,128)(2,1)S(1)} %collective-permute-done.11.refs_1_), custom_call_target="tpu_custom_call" | custom-call | flops 1000000000 | bytes 2000000 | tf_op jit(solution)/shard_map/pallas_call | solution.py:302
  27.4 0.4 %collective-permute-done.9 = bf16[64,256]{1,0:T(8,128)(2,1)S(1)} collective-permute-done((bf16[64,256]{1,0:T(8,128)(2,1)S(1)}, bf16[64,256]{1,0:T(8,128)(2,1)S(1)}, u32[]{:S(2)}, u32[]{:S(2)}) %collective-permute-start.9) | collective-permute-done | bytes 32800 | tf_op jit(solution)/shard_map/ppermute | solution.py:43
  27.8 0.6 %fusion = (bf16[64,128]{1,0:T(8,128)(2,1)}, bf16[64,128]{1,0:T(8,128)(2,1)}) fusion(bf16[64,256]{1,0:T(8,128)(2,1)S(1)} %add_convert_fusion), kind=kLoop, calls=%fused_computation.4 | loop fusion | bytes 65536 | tf_op jit(solution)/shard_map/slice | solution.py:367
  (24 shorter events, 0.4 us)
Async XLA Ops:
  0.6 10.7 %copy-start.2 = (bf16[64,2048]{1,0:T(8,128)(2,1)S(1)}, bf16[64,2048]{1,0:T(8,128)(2,1)}, u32[]{:S(2)}) copy-start(bf16[64,2048]{1,0:T(8,128)(2,1)} %q_ref.1) | copy-start | bytes 786436
  0.6 1.8 %collective-permute-start.1 = (bf16[64,128]{1,0:T(8,128)(2,1)}, bf16[64,128]{1,0:T(8,128)(2,1)S(1)}, u32[]{:S(2)}, u32[]{:S(2)}) collective-permute-start(bf16[64,128]{1,0:T(8,128)(2,1)} %param.7), channel_id=1, source_target_pairs={{0,1},{1,0},{2,3},{3,2},{4,5},{5,4},{6,7},{7,6},{8,9},{9,8},{10,11... | collective-permute-start | bytes 49160 | tf_op jit(solution)/shard_map/ppermute | solution.py:43
  1.4 1.4 %collective-permute-start.2 = (bf16[64,128]{1,0:T(8,128)(2,1)}, bf16[64,128]{1,0:T(8,128)(2,1)S(1)}, u32[]{:S(2)}, u32[]{:S(2)}) collective-permute-start(bf16[64,128]{1,0:T(8,128)(2,1)} %param.8), channel_id=1, source_target_pairs={{0,1},{1,0},{2,3},{3,2},{4,5},{5,4},{6,7},{7,6},{8,9},{9,8},{10,11... | collective-permute-start | bytes 49160 | tf_op jit(solution)/shard_map/ppermute | solution.py:43
  2.2 9.3 %copy-start = (bf16[64,2048]{1,0:T(8,128)(2,1)S(1)}, bf16[64,2048]{1,0:T(8,128)(2,1)}, u32[]{:S(2)}) copy-start(bf16[64,2048]{1,0:T(8,128)(2,1)} %o_ref.1) | copy-start | bytes 786436
  2.2 9.3 %copy-start.1 = (bf16[64,2048]{1,0:T(8,128)(2,1)S(1)}, bf16[64,2048]{1,0:T(8,128)(2,1)}, u32[]{:S(2)}) copy-start(bf16[64,2048]{1,0:T(8,128)(2,1)} %g_ref.1) | copy-start | bytes 786436
  2.2 9.3 %copy-start.3 = (s32[64]{0:T(128)S(1)}, s32[64]{0:T(128)}, u32[]{:S(2)}) copy-start(s32[64]{0:T(128)} %param.11) | copy-start | bytes 772
  2.8 9.9 %collective-permute-start.5 = (bf16[128,256]{1,0:T(8,128)(2,1)S(1)}, bf16[128,256]{1,0:T(8,128)(2,1)S(1)}, u32[]{:S(2)}, u32[]{:S(2)}) collective-permute-start(bf16[128,256]{1,0:T(8,128)(2,1)S(1)} %shard_map.86.own_ref), channel_id=1, source_target_pairs={{0,6},{1,4},{3,16},{2,7},{4,18},{5,17},{6,21},{7,19},{16,22},{17,2... | collective-permute-start | bytes 196616 | tf_op jit(solution)/shard_map/ppermute | solution.py:55
  5.9 6.9 %collective-permute-start.4 = (bf16[128,256]{1,0:T(8,128)(2,1)S(1)}, bf16[128,256]{1,0:T(8,128)(2,1)S(1)}, u32[]{:S(2)}, u32[]{:S(2)}) collective-permute-start(bf16[128,256]{1,0:T(8,128)(2,1)S(1)} %shard_map.86.own_ref), channel_id=1, source_target_pairs={{0,2},{1,16},{2,4},{3,19},{4,6},{5,21},{7,17},{6,23},{16,18},{17,3... | collective-permute-start | bytes 196616 | tf_op jit(solution)/shard_map/ppermute | solution.py:55
  11.4 1.6 %collective-permute-start = (bf16[1024,128]{1,0:T(8,128)(2,1)S(1)}, bf16[1024,128]{1,0:T(8,128)(2,1)S(1)}, u32[]{:S(2)}, u32[]{:S(2)}) collective-permute-start(bf16[1024,128]{1,0:T(8,128)(2,1)S(1)} %shard_map.85.q2_ref.q_ref), channel_id=1, source_target_pairs={{0,1},{1,0},{2,3},{3,2},{4,5},{5,4},{6,7},{7,6},{8,9},{9,8},{10,11... | collective-permute-start | bytes 786440 | tf_op jit(solution)/shard_map/ppermute | solution.py:43
  12.2 1.8 %collective-permute-start.3 = (bf16[1024,128]{1,0:T(8,128)(2,1)S(1)}, bf16[1024,128]{1,0:T(8,128)(2,1)S(1)}, u32[]{:S(2)}, u32[]{:S(2)}) collective-permute-start(bf16[1024,128]{1,0:T(8,128)(2,1)S(1)} %get-tuple-element.34.g_ref), channel_id=1, source_target_pairs={{0,1},{1,0},{2,3},{3,2},{4,5},{5,4},{6,7},{7,6},{8,9},{9,8},{10,11... | collective-permute-start | bytes 786440 | tf_op jit(solution)/shard_map/ppermute | solution.py:43
  13.7 1.3 %collective-permute-start.6 = (f32[5,1024]{1,0:T(8,128)S(1)}, f32[5,1024]{1,0:T(8,128)S(1)}, u32[]{:S(2)}, u32[]{:S(2)}) collective-permute-start(f32[5,1024]{1,0:T(8,128)S(1)} %get-tuple-element.40.stats_ref), channel_id=1, source_target_pairs={{0,1},{1,0},{2,3},{3,2},{4,5},{5,4},{6,7},{7,6},{8,9},{9,8},{10,11... | collective-permute-start | bytes 61448 | tf_op jit(solution)/shard_map/ppermute | solution.py:43
  15.6 6.9 %collective-permute-start.7 = (bf16[128,256]{1,0:T(8,128)(2,1)S(1)}, bf16[128,256]{1,0:T(8,128)(2,1)S(1)}, u32[]{:S(2)}, u32[]{:S(2)}) collective-permute-start(bf16[128,256]{1,0:T(8,128)(2,1)S(1)} %get-tuple-element.44), channel_id=1, source_target_pairs={{6,0},{4,1},{16,3},{7,2},{18,4},{17,5},{21,6},{19,7},{22,16},{20,1... | collective-permute-start | bytes 196616 | tf_op jit(solution)/shard_map/ppermute | solution.py:55
  19.0 7.4 %collective-permute-start.8 = (bf16[128,256]{1,0:T(8,128)(2,1)S(1)}, bf16[128,256]{1,0:T(8,128)(2,1)S(1)}, u32[]{:S(2)}, u32[]{:S(2)}) collective-permute-start(bf16[128,256]{1,0:T(8,128)(2,1)S(1)} %get-tuple-element.51), channel_id=1, source_target_pairs={{2,0},{16,1},{4,2},{19,3},{6,4},{21,5},{17,7},{23,6},{18,16},{32,1... | collective-permute-start | bytes 196616 | tf_op jit(solution)/shard_map/ppermute | solution.py:55
  21.6 5.0 %collective-permute-start.10 = (bf16[512,128]{1,0:T(8,128)(2,1)S(1)}, bf16[512,128]{1,0:T(8,128)(2,1)S(1)}, u32[]{:S(2)}, u32[]{:S(2)}) collective-permute-start(bf16[512,128]{1,0:T(8,128)(2,1)S(1)} %get-tuple-element.54), channel_id=1, source_target_pairs={{0,1},{1,0},{2,3},{3,2},{4,5},{5,4},{6,7},{7,6},{8,9},{9,8},{10,11... | collective-permute-start | bytes 393224 | tf_op jit(solution)/shard_map/ppermute | solution.py:43
  22.4 4.2 %collective-permute-start.11 = (bf16[512,128]{1,0:T(8,128)(2,1)S(1)}, bf16[512,128]{1,0:T(8,128)(2,1)S(1)}, u32[]{:S(2)}, u32[]{:S(2)}) collective-permute-start(bf16[512,128]{1,0:T(8,128)(2,1)S(1)} %get-tuple-element.55), channel_id=1, source_target_pairs={{0,1},{1,0},{2,3},{3,2},{4,5},{5,4},{6,7},{7,6},{8,9},{9,8},{10,11... | collective-permute-start | bytes 393224 | tf_op jit(solution)/shard_map/ppermute | solution.py:43
  26.5 1.3 %collective-permute-start.9 = (bf16[64,256]{1,0:T(8,128)(2,1)S(1)}, bf16[64,256]{1,0:T(8,128)(2,1)S(1)}, u32[]{:S(2)}, u32[]{:S(2)}) collective-permute-start(bf16[64,256]{1,0:T(8,128)(2,1)S(1)} %slice.22), channel_id=1, source_target_pairs={{0,1},{1,0},{2,3},{3,2},{4,5},{5,4},{6,7},{7,6},{8,9},{9,8},{10,11... | collective-permute-start | bytes 98312 | tf_op jit(solution)/shard_map/ppermute | solution.py:43

commit v10 on v8

--- a/solution.py
+++ b/solution.py
@@ -26,7 +26,7 @@
 AXES = ("blk", "uly")
 MOVES = (
     ((1, 4), (0, 0, 0, 1), (1, 0, 0, 0)),
-    ((3, 2), (0, 1, 0, 0), (0, 0, 1, 0)),
+    ((3, 2), (0, 0, 0, 0), (1, 1, 1, 1)),
 )
 PIECES = (0, 352, 704, COLS)
 KEY_COLS, VALUE_COLS = slice(0, DH), slice(DH, 2 * DH)

time: 28.5 us -> 28.6 us (level)
  waiting for transfers between devices: 5.31 us -> 4.76 us
  starting transfers between devices: 16.5 us -> 17 us
    ppermute x4, starting transfers between devices: 13.3 us -> 14.5 us  [move_chips(): return lax.ppermute(x, AXES, pairs)]
    ppermute x9, starting transfers between devices: 3.16 us -> 2.51 us  [swap_cores(): return lax.ppermute(x, 'uly', [(i, i ^ 1) for i in range(16)])]
    ppermute x4, waiting for transfers between devices: 3.49 us -> 2.94 us  [move_chips(): return lax.ppermute(x, AXES, pairs)]
where the time goes in v10:
time: 28.6 us; the launch traced here: 28.4 us
  starting transfers between devices  17 us (59%)
  waiting for transfers between devices  4.76 us (17%)
  Pallas kernels  4.42 us (15%)
  between operations  0.79 us (3%)
  other arithmetic  0.77 us (3%)
  local copies, waits for them, and re-layouts  0.64 us (2%)
    ppermute x4, starting transfers between devices, move_chips(): return lax.ppermute(x, AXES, pairs)  14.5 us
    pallas_call x11, Pallas kernels, call(): pl.pallas_call(kernel, out_shape=outs, in_specs=[vmem] * len(args), out_s...  4.42 us
    ppermute x4, waiting for transfers between devices, move_chips(): return lax.ppermute(x, AXES, pairs)  2.94 us
    ppermute x9, starting transfers between devices, swap_cores(): return lax.ppermute(x, 'uly', [(i, i ^ 1) for i in range(16)])  2.51 us
    ppermute x9, waiting for transfers between devices, swap_cores(): return lax.ppermute(x, 'uly', [(i, i ^ 1) for i in range(16)])  1.82 us
    concatenate x1, other arithmetic, on_device(): mine = jnp.concatenate([key_rows, value_rows], axis=1)  0.74 us
    slice x1, local copies, waits for them, and re-layouts, on_device(): return (query_grad, result[:, :DH], result[:, DH:])  0.62 us
  transfers between devices with their start and end apart: 13, of which 6 were waited for; matrix products, arithmetic and copies ran while one was open for 3% of the time, Pallas kernels for 14%

profile of v10, /device:TPU:39, one launch (start us, length us, event | category | flops | bytes accessed | tf_op | source)
XLA Modules:
  0.0 28.4 jit_solution(16995104863544150159)
XLA Ops:
  0.6 0.8 %collective-permute-start.1 = (bf16[64,128]{1,0:T(8,128)(2,1)}, bf16[64,128]{1,0:T(8,128)(2,1)S(1)}, u32[]{:S(2)}, u32[]{:S(2)}) collective-permute-start(bf16[64,128]{1,0:T(8,128)(2,1)} %param.7), channel_id=1, source_target_pairs={{0,1},{1,0},{2,3},{3,2},{4,5},{5,4},{6,7},{7,6},{8,9},{9,8},{10,11... | collective-permute-start | bytes 49160 | tf_op jit(solution)/shard_map/ppermute | solution.py:43
  1.5 0.7 %pad_maximum_fusion.mine_ref = bf16[64,256]{1,0:T(8,128)(2,1)S(1)} fusion(bf16[64,128]{1,0:T(8,128)(2,1)} %param.8, bf16[64,128]{1,0:T(8,128)(2,1)} %param.7), kind=kLoop, calls=%fused_computation.3 | loop fusion | flops 65536 | bytes 65536 | tf_op jit(solution)/shard_map/concatenate | solution.py:318
  2.3 0.2 collective-permute-done.1.other_k_ref
  2.5 0.3 %collective-permute-done.2.other_v_ref = bf16[64,128]{1,0:T(8,128)(2,1)S(1)} collective-permute-done((bf16[64,128]{1,0:T(8,128)(2,1)}, bf16[64,128]{1,0:T(8,128)(2,1)S(1)}, u32[]{:S(2)}, u32[]{:S(2)}) %collective-permute-start.2) | collective-permute-done | bytes 16416 | tf_op jit(solution)/shard_map/ppermute | solution.py:43
  2.8 3.0 %collective-permute-start.5 = (bf16[128,256]{1,0:T(8,128)(2,1)S(1)}, bf16[128,256]{1,0:T(8,128)(2,1)S(1)}, u32[]{:S(2)}, u32[]{:S(2)}) collective-permute-start(bf16[128,256]{1,0:T(8,128)(2,1)S(1)} %shard_map.86.own_ref), channel_id=1, source_target_pairs={{0,7},{1,4},{2,17},{3,6},{4,19},{5,16},{6,21},{7,18},{16,23},{17,2... | collective-permute-start | bytes 196616 | tf_op jit(solution)/shard_map/ppermute | solution.py:55
  5.9 5.4 %collective-permute-start.4 = (bf16[128,256]{1,0:T(8,128)(2,1)S(1)}, bf16[128,256]{1,0:T(8,128)(2,1)S(1)}, u32[]{:S(2)}, u32[]{:S(2)}) collective-permute-start(bf16[128,256]{1,0:T(8,128)(2,1)S(1)} %shard_map.86.own_ref), channel_id=1, source_target_pairs={{0,2},{1,16},{2,4},{3,19},{4,6},{5,21},{7,17},{6,23},{16,18},{17,3... | collective-permute-start | bytes 196616 | tf_op jit(solution)/shard_map/ppermute | solution.py:55
  11.5 0.7 %shard_map.87 = (bf16[1024,128]{1,0:T(8,128)(2,1)S(1)}, f32[1,1024]{1,0:T(1,128)S(1)}, bf16[384,128]{1,0:T(8,128)(2,1)S(1)}, f32[128,1024]{1,0:T(8,128)S(1)}, f3...) custom-call(bf16[1024,128]{1,0:T(8,128)(2,1)S(1)} %shard_map.85.q2_ref.q_ref, bf16[64,2048]{1,0:T(8,128)(2,1)S(1)} %copy-done, ...), custom_call_target="tpu_custom_call" | custom-call | flops 100000000 | bytes 200000 | tf_op jit(solution)/shard_map/pallas_call | solution.py:302
  12.1 0.6 %collective-permute-start.3 = (bf16[1024,128]{1,0:T(8,128)(2,1)S(1)}, bf16[1024,128]{1,0:T(8,128)(2,1)S(1)}, u32[]{:S(2)}, u32[]{:S(2)}) collective-permute-start(bf16[1024,128]{1,0:T(8,128)(2,1)S(1)} %get-tuple-element.35.g_ref), channel_id=1, source_target_pairs={{0,1},{1,0},{2,3},{3,2},{4,5},{5,4},{6,7},{7,6},{8,9},{9,8},{10,11... | collective-permute-start | bytes 786440 | tf_op jit(solution)/shard_map/ppermute | solution.py:43
  12.7 0.2 collective-permute-done.partner_q_ref
  13.0 0.7 %shard_map.89 = (f32[256,2048]{1,0:T(8,128)S(1)}, f32[2,2048]{1,0:T(2,128)S(1)}, f32[5,1024]{1,0:T(8,128)S(1)}) custom-call(bf16[1024,128]{1,0:T(8,128)(2,1)S(1)} %shard_map.85.q2_ref.q_ref, bf16[1024,128]{1,0:T(8,128)(2,1)S(1)} %collective-permute-done.partner_q_ref, bf16[256,256]{1,0:T(8,128)(2,1)S(1)} %shard_map.88.keys_ref, ...), custom_call_target="tpu_custom_call" | custom-call | flops 1000000000 | bytes 2000000 | tf_op jit(solution)/shard_map/pallas_call | solution.py:302
  13.7 0.2 collective-permute-start.6
  13.9 0.4 %shard_map.90.u_ref = f32[256,2048]{1,0:T(8,128)S(1)} custom-call(bf16[1024,128]{1,0:T(8,128)(2,1)S(1)} %get-tuple-element.35.g_ref, bf16[1024,128]{1,0:T(8,128)(2,1)S(1)} %collective-permute-done.3.partner_g_ref, bf16[128,256]{1,0:T(8,128)(2,1)S(1)} %collective-permute-done.4.a_ref, bf16[128,256]{1,0:T(8,128)(2,1)S(1)} %collective-permute-done.5.b_ref), custom_call_target="tpu_custom_call" | custom-call | flops 1000000000 | bytes 2000000 | tf_op jit(solution)/shard_map/pallas_call | solution.py:302
  14.3 0.6 %collective-permute-done.6.far_ref = f32[5,1024]{1,0:T(8,128)S(1)} collective-permute-done((f32[5,1024]{1,0:T(8,128)S(1)}, f32[5,1024]{1,0:T(8,128)S(1)}, u32[]{:S(2)}, u32[]{:S(2)}) %collective-permute-start.6) | collective-permute-done | bytes 20512 | tf_op jit(solution)/shard_map/ppermute | solution.py:43
  15.0 0.5 %shard_map.91 = (bf16[128,256]{1,0:T(8,128)(2,1)S(1)}, bf16[128,2048]{1,0:T(8,128)(2,1)S(1)}, f32[2,2048]{1,0:T(2,128)S(1)}, f32[2,2048]{1,0:T(2,128)S(1)}) custom-call(bf16[1024,128]{1,0:T(8,128)(2,1)S(1)} %shard_map.85.q2_ref.q_ref, bf16[1024,128]{1,0:T(8,128)(2,1)S(1)} %collective-permute-done.partner_q_ref, ...), custom_call_target="tpu_custom_call" | custom-call | flops 1000000000 | bytes 2000000 | tf_op jit(solution)/shard_map/pallas_call | solution.py:302
  15.5 3.0 %collective-permute-start.7 = (bf16[128,256]{1,0:T(8,128)(2,1)S(1)}, bf16[128,256]{1,0:T(8,128)(2,1)S(1)}, u32[]{:S(2)}, u32[]{:S(2)}) collective-permute-start(bf16[128,256]{1,0:T(8,128)(2,1)S(1)} %get-tuple-element.45), channel_id=1, source_target_pairs={{7,0},{4,1},{17,2},{6,3},{19,4},{16,5},{21,6},{18,7},{23,16},{20,1... | collective-permute-start | bytes 196616 | tf_op jit(solution)/shard_map/ppermute | solution.py:55
  18.5 0.5 %shard_map.92 = (bf16[128,256]{1,0:T(8,128)(2,1)S(1)}, bf16[128,2048]{1,0:T(8,128)(2,1)S(1)}) custom-call(bf16[1024,128]{1,0:T(8,128)(2,1)S(1)} %shard_map.85.q2_ref.q_ref, bf16[1024,128]{1,0:T(8,128)(2,1)S(1)} %collective-permute-done.partner_q_ref, bf16[1024,128]{1,0:T(8,128)(2,1)S(1)} %get-tuple-element.35.g_ref, ...), custom_call_target="tpu_custom_call" | custom-call | flops 1000000000 | bytes 2000000 | tf_op jit(solution)/shard_map/pallas_call | solution.py:302
  19.0 3.1 %collective-permute-start.8 = (bf16[128,256]{1,0:T(8,128)(2,1)S(1)}, bf16[128,256]{1,0:T(8,128)(2,1)S(1)}, u32[]{:S(2)}, u32[]{:S(2)}) collective-permute-start(bf16[128,256]{1,0:T(8,128)(2,1)S(1)} %get-tuple-element.52), channel_id=1, source_target_pairs={{2,0},{16,1},{4,2},{19,3},{6,4},{21,5},{17,7},{23,6},{18,16},{32,1... | collective-permute-start | bytes 196616 | tf_op jit(solution)/shard_map/ppermute | solution.py:55
  22.1 0.7 %shard_map.93 = (f32[1024,128]{1,0:T(8,128)S(1)}, f32[128,256]{1,0:T(8,128)S(1)}, bf16[352,128]{1,0:T(8,128)(2,1)S(1)}, bf16[352,128]{1,0:T(8,128)(2,1)S(1)}, bf16[320,128]{1,0:T(8,128)(2,1)S(1)}) custom-call(bf16[1024,128]{1,0:T(8,128)(2,1)S(1)} %shard_map.85.q2_ref.q_ref, bf16[1024,128]{1,0:T(8,128)(2,1)S(1)} %get-tuple-element.35.g_ref, ...), custom_call_target="tpu_custom_call" | custom-call | flops 100000000 | bytes 200000 | tf_op jit(solution)/shard_map/pallas_call | solution.py:302
  22.9 0.5 %collective-permute-start.10 = (bf16[352,128]{1,0:T(8,128)(2,1)S(1)}, bf16[352,128]{1,0:T(8,128)(2,1)S(1)}, u32[]{:S(2)}, u32[]{:S(2)}) collective-permute-start(bf16[352,128]{1,0:T(8,128)(2,1)S(1)} %get-tuple-element.55), channel_id=1, source_target_pairs={{0,1},{1,0},{2,3},{3,2},{4,5},{5,4},{6,7},{7,6},{8,9},{9,8},{10,11... | collective-permute-start | bytes 270344 | tf_op jit(solution)/shard_map/ppermute | solution.py:43
  23.4 0.1 collective-permute-start.11
  23.5 2.9 %collective-permute-done.8 = bf16[128,256]{1,0:T(8,128)(2,1)S(1)} collective-permute-done((bf16[128,256]{1,0:T(8,128)(2,1)S(1)}, bf16[128,256]{1,0:T(8,128)(2,1)S(1)}, u32[]{:S(2)}, u32[]{:S(2)}) %collective-permute-start.8) | collective-permute-done | bytes 65568 | tf_op jit(solution)/shard_map/ppermute | solution.py:55
  26.6 0.8 %shard_map.95 = bf16[64,2048]{1,0:T(8,128)(2,1)} custom-call(f32[1024,128]{1,0:T(8,128)S(1)} %get-tuple-element.54.dq_ref, bf16[352,128]{1,0:T(8,128)(2,1)S(1)} %collective-permute-done.10.refs_0_, bf16[352,128]{1,0:T(8,128)(2,1)S(1)} %collective-permute-done.11.refs_1_, bf16[320,128]{1,0:T(8,128)(2,1)S(1)} %collective-permute-done.12.refs_2_), custom_call_target="tpu_custom_call" | custom-call | flops 1000000000 | bytes 2000000 | tf_op jit(solution)/shard_map/pallas_call | solution.py:302
  27.4 0.4 %collective-permute-done.9 = bf16[64,256]{1,0:T(8,128)(2,1)S(1)} collective-permute-done((bf16[64,256]{1,0:T(8,128)(2,1)S(1)}, bf16[64,256]{1,0:T(8,128)(2,1)S(1)}, u32[]{:S(2)}, u32[]{:S(2)}) %collective-permute-start.9) | collective-permute-done | bytes 32800 | tf_op jit(solution)/shard_map/ppermute | solution.py:43
  27.8 0.6 %fusion = (bf16[64,128]{1,0:T(8,128)(2,1)}, bf16[64,128]{1,0:T(8,128)(2,1)}) fusion(bf16[64,256]{1,0:T(8,128)(2,1)S(1)} %add_convert_fusion), kind=kLoop, calls=%fused_computation.4 | loop fusion | bytes 65536 | tf_op jit(solution)/shard_map/slice | solution.py:367
  (26 shorter events, 0.5 us)
Async XLA Ops:
  0.6 10.7 %copy-start.2 = (bf16[64,2048]{1,0:T(8,128)(2,1)S(1)}, bf16[64,2048]{1,0:T(8,128)(2,1)}, u32[]{:S(2)}) copy-start(bf16[64,2048]{1,0:T(8,128)(2,1)} %q_ref.1) | copy-start | bytes 786436
  0.6 1.8 %collective-permute-start.1 = (bf16[64,128]{1,0:T(8,128)(2,1)}, bf16[64,128]{1,0:T(8,128)(2,1)S(1)}, u32[]{:S(2)}, u32[]{:S(2)}) collective-permute-start(bf16[64,128]{1,0:T(8,128)(2,1)} %param.7), channel_id=1, source_target_pairs={{0,1},{1,0},{2,3},{3,2},{4,5},{5,4},{6,7},{7,6},{8,9},{9,8},{10,11... | collective-permute-start | bytes 49160 | tf_op jit(solution)/shard_map/ppermute | solution.py:43
  1.4 1.4 %collective-permute-start.2 = (bf16[64,128]{1,0:T(8,128)(2,1)}, bf16[64,128]{1,0:T(8,128)(2,1)S(1)}, u32[]{:S(2)}, u32[]{:S(2)}) collective-permute-start(bf16[64,128]{1,0:T(8,128)(2,1)} %param.8), channel_id=1, source_target_pairs={{0,1},{1,0},{2,3},{3,2},{4,5},{5,4},{6,7},{7,6},{8,9},{9,8},{10,11... | collective-permute-start | bytes 49160 | tf_op jit(solution)/shard_map/ppermute | solution.py:43
  2.2 9.2 %copy-start = (bf16[64,2048]{1,0:T(8,128)(2,1)S(1)}, bf16[64,2048]{1,0:T(8,128)(2,1)}, u32[]{:S(2)}) copy-start(bf16[64,2048]{1,0:T(8,128)(2,1)} %o_ref.1) | copy-start | bytes 786436
  2.2 9.2 %copy-start.1 = (bf16[64,2048]{1,0:T(8,128)(2,1)S(1)}, bf16[64,2048]{1,0:T(8,128)(2,1)}, u32[]{:S(2)}) copy-start(bf16[64,2048]{1,0:T(8,128)(2,1)} %g_ref.1) | copy-start | bytes 786436
  2.2 9.2 %copy-start.3 = (s32[64]{0:T(128)S(1)}, s32[64]{0:T(128)}, u32[]{:S(2)}) copy-start(s32[64]{0:T(128)} %param.11) | copy-start | bytes 772
  2.8 9.9 %collective-permute-start.5 = (bf16[128,256]{1,0:T(8,128)(2,1)S(1)}, bf16[128,256]{1,0:T(8,128)(2,1)S(1)}, u32[]{:S(2)}, u32[]{:S(2)}) collective-permute-start(bf16[128,256]{1,0:T(8,128)(2,1)S(1)} %shard_map.86.own_ref), channel_id=1, source_target_pairs={{0,7},{1,4},{2,17},{3,6},{4,19},{5,16},{6,21},{7,18},{16,23},{17,2... | collective-permute-start | bytes 196616 | tf_op jit(solution)/shard_map/ppermute | solution.py:55
  5.9 6.8 %collective-permute-start.4 = (bf16[128,256]{1,0:T(8,128)(2,1)S(1)}, bf16[128,256]{1,0:T(8,128)(2,1)S(1)}, u32[]{:S(2)}, u32[]{:S(2)}) collective-permute-start(bf16[128,256]{1,0:T(8,128)(2,1)S(1)} %shard_map.86.own_ref), channel_id=1, source_target_pairs={{0,2},{1,16},{2,4},{3,19},{4,6},{5,21},{7,17},{6,23},{16,18},{17,3... | collective-permute-start | bytes 196616 | tf_op jit(solution)/shard_map/ppermute | solution.py:55
  11.3 1.6 %collective-permute-start = (bf16[1024,128]{1,0:T(8,128)(2,1)S(1)}, bf16[1024,128]{1,0:T(8,128)(2,1)S(1)}, u32[]{:S(2)}, u32[]{:S(2)}) collective-permute-start(bf16[1024,128]{1,0:T(8,128)(2,1)S(1)} %shard_map.85.q2_ref.q_ref), channel_id=1, source_target_pairs={{0,1},{1,0},{2,3},{3,2},{4,5},{5,4},{6,7},{7,6},{8,9},{9,8},{10,11... | collective-permute-start | bytes 786440 | tf_op jit(solution)/shard_map/ppermute | solution.py:43
  12.1 1.8 %collective-permute-start.3 = (bf16[1024,128]{1,0:T(8,128)(2,1)S(1)}, bf16[1024,128]{1,0:T(8,128)(2,1)S(1)}, u32[]{:S(2)}, u32[]{:S(2)}) collective-permute-start(bf16[1024,128]{1,0:T(8,128)(2,1)S(1)} %get-tuple-element.35.g_ref), channel_id=1, source_target_pairs={{0,1},{1,0},{2,3},{3,2},{4,5},{5,4},{6,7},{7,6},{8,9},{9,8},{10,11... | collective-permute-start | bytes 786440 | tf_op jit(solution)/shard_map/ppermute | solution.py:43
  13.7 1.3 %collective-permute-start.6 = (f32[5,1024]{1,0:T(8,128)S(1)}, f32[5,1024]{1,0:T(8,128)S(1)}, u32[]{:S(2)}, u32[]{:S(2)}) collective-permute-start(f32[5,1024]{1,0:T(8,128)S(1)} %get-tuple-element.41.stats_ref), channel_id=1, source_target_pairs={{0,1},{1,0},{2,3},{3,2},{4,5},{5,4},{6,7},{7,6},{8,9},{9,8},{10,11... | collective-permute-start | bytes 61448 | tf_op jit(solution)/shard_map/ppermute | solution.py:43
  15.5 8.0 %collective-permute-start.7 = (bf16[128,256]{1,0:T(8,128)(2,1)S(1)}, bf16[128,256]{1,0:T(8,128)(2,1)S(1)}, u32[]{:S(2)}, u32[]{:S(2)}) collective-permute-start(bf16[128,256]{1,0:T(8,128)(2,1)S(1)} %get-tuple-element.45), channel_id=1, source_target_pairs={{7,0},{4,1},{17,2},{6,3},{19,4},{16,5},{21,6},{18,7},{23,16},{20,1... | collective-permute-start | bytes 196616 | tf_op jit(solution)/shard_map/ppermute | solution.py:55
  19.0 7.5 %collective-permute-start.8 = (bf16[128,256]{1,0:T(8,128)(2,1)S(1)}, bf16[128,256]{1,0:T(8,128)(2,1)S(1)}, u32[]{:S(2)}, u32[]{:S(2)}) collective-permute-start(bf16[128,256]{1,0:T(8,128)(2,1)S(1)} %get-tuple-element.52), channel_id=1, source_target_pairs={{2,0},{16,1},{4,2},{19,3},{6,4},{21,5},{17,7},{23,6},{18,16},{32,1... | collective-permute-start | bytes 196616 | tf_op jit(solution)/shard_map/ppermute | solution.py:55
  22.8 3.8 %collective-permute-start.12 = (bf16[320,128]{1,0:T(8,128)(2,1)S(1)}, bf16[320,128]{1,0:T(8,128)(2,1)S(1)}, u32[]{:S(2)}, u32[]{:S(2)}) collective-permute-start(bf16[320,128]{1,0:T(8,128)(2,1)S(1)} %get-tuple-element.57), channel_id=1, source_target_pairs={{0,1},{1,0},{2,3},{3,2},{4,5},{5,4},{6,7},{7,6},{8,9},{9,8},{10,11... | collective-permute-start | bytes 245768 | tf_op jit(solution)/shard_map/ppermute | solution.py:43
  22.9 3.7 %collective-permute-start.10 = (bf16[352,128]{1,0:T(8,128)(2,1)S(1)}, bf16[352,128]{1,0:T(8,128)(2,1)S(1)}, u32[]{:S(2)}, u32[]{:S(2)}) collective-permute-start(bf16[352,128]{1,0:T(8,128)(2,1)S(1)} %get-tuple-element.55), channel_id=1, source_target_pairs={{0,1},{1,0},{2,3},{3,2},{4,5},{5,4},{6,7},{7,6},{8,9},{9,8},{10,11... | collective-permute-start | bytes 270344 | tf_op jit(solution)/shard_map/ppermute | solution.py:43
  23.4 3.2 %collective-permute-start.11 = (bf16[352,128]{1,0:T(8,128)(2,1)S(1)}, bf16[352,128]{1,0:T(8,128)(2,1)S(1)}, u32[]{:S(2)}, u32[]{:S(2)}) collective-permute-start(bf16[352,128]{1,0:T(8,128)(2,1)S(1)} %get-tuple-element.56), channel_id=1, source_target_pairs={{0,1},{1,0},{2,3},{3,2},{4,5},{5,4},{6,7},{7,6},{8,9},{9,8},{10,11... | collective-permute-start | bytes 270344 | tf_op jit(solution)/shard_map/ppermute | solution.py:43
  26.5 1.3 %collective-permute-start.9 = (bf16[64,256]{1,0:T(8,128)(2,1)S(1)}, bf16[64,256]{1,0:T(8,128)(2,1)S(1)}, u32[]{:S(2)}, u32[]{:S(2)}) collective-permute-start(bf16[64,256]{1,0:T(8,128)(2,1)S(1)} %slice.22), channel_id=1, source_target_pairs={{0,1},{1,0},{2,3},{3,2},{4,5},{5,4},{6,7},{7,6},{8,9},{9,8},{10,11... | collective-permute-start | bytes 98312 | tf_op jit(solution)/shard_map/ppermute | solution.py:43
